TPU v7x, 32 devices: a whole 2x2x4 slice. The times are simulated.
32 devices in a mesh: seq: 2 (over x), ctx: 8 (over z, y), tp: 2 (over core).
Axes of the slice: x: 2, y: 2, z: 4, core: 2. Of those that a mesh axis runs over, the one named last changes fastest.
Arguments:
- tokens: bfloat16 [2048, 2880], P(('seq', 'ctx')), may hold values from -6 to 6
- gain_attn: float32 [2880], replicated, may hold values from 0.5 to 1.5
- w_query: bfloat16 [2880, 4096], P(('seq', 'ctx'), 'tp'), may hold values from -0.109375 to 0.109375
- b_query: float32 [4096], P('tp'), may hold values from -4 to 4
- key_value_weight: bfloat16 [2880, 2, 512], P(('seq', 'ctx'), None, 'tp'), may hold values from -0.109375 to 0.109375
- key_value_bias: float32 [2, 512], P(None, 'tp'), may hold values from -4 to 4
- sinks: float32 [64], P('tp'), may hold values from -1 to 3
- w_out: bfloat16 [4096, 2880], P('tp', ('seq', 'ctx')), may hold values from -1.5 to 1.5
- b_out: float32 [2880], replicated, may hold values from -4 to 4
- gain_moe: float32 [2880], replicated, may hold values from 0.5 to 1.5
- w_router: bfloat16 [2880, 8], replicated, may hold values from -0.0546875 to 0.0546875
- b_router: float32 [8], replicated, may hold values from -3 to 3
- routes: int32 [2048, 4], P(('seq', 'ctx')), may hold values from 0 to 7, all different within a row; in each aligned block of 128 rows (0 to 127, 128 to 255, ...) at most 128 rows name the same one
- w_gate_up: bfloat16 [8, 2880, 2, 2880], P('ctx', None, None, ('seq', 'tp')), may hold values from -0.109375 to 0.109375
- b_gate_up: float32 [8, 2, 2880], P('ctx', None, ('seq', 'tp')), may hold values from -1.5 to 1.5
- w_down: bfloat16 [8, 2880, 2880], P('ctx', ('seq', 'tp')), may hold values from -0.109375 to 0.109375
- b_down: float32 [8, 2880], P('ctx'), may hold values from -1.5 to 1.5
- cotangent: bfloat16 [2048, 2880], P(('seq', 'ctx')), may hold values from -6 to 6
Outputs:
- mixed: bfloat16 [2048, 2880], P(('seq', 'ctx'))
- grad_tokens: bfloat16 [2048, 2880], P(('seq', 'ctx'))
- grad_gain_attn: float32 [2880], replicated
- grad_w_query: float32 [2880, 4096], P(('seq', 'ctx'), 'tp')
- grad_b_query: float32 [4096], P('tp')
- grad_w_key_value: float32 [2880, 2, 512], P(('seq', 'ctx'), None, 'tp')
- grad_b_key_value: float32 [2, 512], P(None, 'tp')
- grad_sinks: float32 [64], P('tp')
- grad_w_out: float32 [4096, 2880], P('tp', ('seq', 'ctx'))
- grad_b_out: float32 [2880], replicated
- grad_gain_moe: float32 [2880], replicated
- grad_w_router: float32 [2880, 8], replicated
- grad_b_router: float32 [8], replicated
- grad_w_gate_up: float32 [8, 2880, 2, 2880], P('ctx', None, None, ('seq', 'tp'))
- grad_b_gate_up: float32 [8, 2, 2880], P('ctx', None, ('seq', 'tp'))
- grad_w_down: float32 [8, 2880, 2880], P('ctx', ('seq', 'tp'))
- grad_b_down: float32 [8, 2880], P('ctx')
Inputs may be any that keep to these rules, and one draw needn't show every extreme that they name: `routes`: each row names 4 different experts. In every aligned block of 128 rows (the rows of one index of seq and ctx) no expert is named by more than 128 rows, and in some block some expert is named by exactly 128 rows.
All inputs are finite; a program needn't handle non-finite values.
Results may differ from a plain program's by a relative error of at most 0.03.
Values may be sent and summed in bfloat16 or wider, within the bound.
A program may use at most 320 MiB of HBM per device.

v0:
```python
import math

import jax
import jax.numpy as jnp
from jax import lax
from jax.sharding import PartitionSpec as P

HEAD_DIMENSION = 64


rms_eps = 1e-05
rope_base = 150000.0
clamp_limit = 7.0
glu_alpha = 1.702
masked_score = -1e30


def passed_along(x, axis, by):
    size = lax.axis_size(axis)
    pairs = [(i, i + by) for i in range(size) if 0 <= i + by < size]
    return lax.ppermute(x, axis, pairs)


def shifted(block, axis, distance):
    devices = range(lax.axis_size(axis))
    route = [((i - distance) % len(devices), i) for i in devices]
    return lax.ppermute(block, axis, route)


def rms_norm(row_block, gain_vec):
    return (
        row_block
        * lax.rsqrt(jnp.mean(row_block * row_block, axis=-1, keepdims=True) + rms_eps)
        * gain_vec
    )


def rotary(positions, head_size):
    half_size = head_size // 2
    frequency = rope_base ** (-2.0 * jnp.arange(half_size, dtype=jnp.float32) / head_size)
    angles = positions.astype(jnp.float32)[:, None] * frequency[None, :]
    return (jnp.cos(angles), jnp.sin(angles))


def apply_rotation(heads_in, cosine_lookup, sine_lookup):
    half_size = heads_in.shape[-1] // 2
    lower_half = heads_in[..., :half_size]
    upper_half = heads_in[..., half_size:]
    cosine_part = cosine_lookup[:, None, :]
    sine_part = sine_lookup[:, None, :]
    return jnp.concatenate(
        [
            lower_half * cosine_part - upper_half * sine_part,
            upper_half * cosine_part + lower_half * sine_part,
        ],
        axis=-1,
    )


def rotate_back(gradient, cosine_lookup, sine_lookup):
    half_size = gradient.shape[-1] // 2
    lower_half = gradient[..., :half_size]
    upper_half = gradient[..., half_size:]
    cosine_part = cosine_lookup[:, None, :]
    sine_part = sine_lookup[:, None, :]
    return jnp.concatenate(
        [
            lower_half * cosine_part + upper_half * sine_part,
            upper_half * cosine_part - lower_half * sine_part,
        ],
        axis=-1,
    )


def expert_act(gate_part, up_part):
    gate_soft = clamp_limit * jnp.tanh(gate_part / clamp_limit)
    up_soft = clamp_limit * jnp.tanh(up_part / clamp_limit)
    return (up_soft + 1.0) * gate_soft * jax.nn.sigmoid(glu_alpha * gate_soft)


def project_grad(left, right):
    return lax.dot_general(
        left, right, (((0,), (0,)), ((), ())), preferred_element_type=jnp.float32
    )


def over_heads(partial_sum):
    return lax.psum(partial_sum.astype(jnp.bfloat16), "tp").astype(jnp.float32)


def to_experts(outgoing):
    arrived = lax.all_to_all(outgoing, "ctx", split_axis=0, concat_axis=0, tiled=True)
    return lax.all_gather(arrived[None], "seq", axis=0, tiled=True)


def from_hidden(partial_sum):
    own_rows = lax.psum_scatter(
        partial_sum.astype(jnp.bfloat16), "seq", scatter_dimension=0, tiled=True
    )
    return lax.psum(own_rows, "tp").astype(jnp.float32)[0]


def to_sources(expert_rows):
    return lax.all_to_all(expert_rows, "ctx", split_axis=0, concat_axis=0, tiled=True)


def on_device(
    tokens,
    gain_attn,
    w_query,
    b_query,
    key_value_weight,
    key_value_bias,
    sinks,
    w_out,
    b_out,
    gain_moe,
    w_router,
    b_router,
    routes,
    w_gate_up,
    b_gate_up,
    w_down,
    b_down,
    cotangent,
):
    tok_rows = tokens.shape[0]
    model_width = tokens.shape[1]
    ctx_size = lax.axis_size("ctx")
    ctx_rank = lax.axis_index("ctx")
    local_heads = sinks.shape[0]
    key_value_width = key_value_weight.shape[2]
    kv_heads = key_value_width // HEAD_DIMENSION
    query_group_width = local_heads // kv_heads
    score_scale = 1.0 / math.sqrt(HEAD_DIMENSION)
    experts = w_router.shape[1]
    top_count = routes.shape[1]
    capacity = 2 * tok_rows * top_count // experts
    residual = tokens.astype(jnp.float32)
    normed_attn, attn_norm_back = jax.vjp(rms_norm, residual, gain_attn)
    normed_low = normed_attn.astype(jnp.bfloat16)
    full_query, full_kv, full_out = (
        lax.all_gather(w_query, ("seq", "ctx"), axis=0, tiled=True),
        lax.all_gather(key_value_weight, ("seq", "ctx"), axis=0, tiled=True),
        lax.all_gather(w_out, ("seq", "ctx"), axis=1, tiled=True),
    )
    query_proj = jnp.dot(normed_low, full_query, preferred_element_type=jnp.float32) + b_query
    key_value_projected = jnp.dot(
        normed_low,
        full_kv.reshape(model_width, 2 * key_value_width),
        preferred_element_type=jnp.float32,
    ) + key_value_bias.reshape(-1)
    positions = ctx_rank * tok_rows + jnp.arange(tok_rows, dtype=jnp.int32)
    cosine_lookup, sine_lookup = rotary(positions, HEAD_DIMENSION)
    query_rows = apply_rotation(
        query_proj.reshape(tok_rows, local_heads, HEAD_DIMENSION), cosine_lookup, sine_lookup
    ).astype(jnp.bfloat16)
    query_rows = query_rows.reshape(tok_rows, kv_heads, query_group_width, HEAD_DIMENSION)
    key_matrix_rows = apply_rotation(
        key_value_projected[:, :key_value_width].reshape(tok_rows, kv_heads, HEAD_DIMENSION),
        cosine_lookup,
        sine_lookup,
    ).astype(jnp.bfloat16)
    value_matrix_rows = (
        key_value_projected[:, key_value_width:]
        .reshape(tok_rows, kv_heads, HEAD_DIMENSION)
        .astype(jnp.bfloat16)
    )
    last_query = positions[tok_rows - 1]
    start_state = (
        jnp.broadcast_to(
            sinks.reshape(kv_heads, query_group_width, 1), (kv_heads, query_group_width, tok_rows)
        ),
        jnp.ones((kv_heads, query_group_width, tok_rows), jnp.float32),
        jnp.zeros((kv_heads, query_group_width, tok_rows, HEAD_DIMENSION), jnp.float32),
    )
    carried = start_state
    key_piece = lax.all_gather(key_matrix_rows, "ctx", axis=0, tiled=True)
    value_piece = lax.all_gather(value_matrix_rows, "ctx", axis=0, tiled=True)
    piece_rows = key_piece.shape[0]
    rows_per_block = math.gcd(piece_rows, 512)
    block_count = piece_rows // rows_per_block
    key_blocks = key_piece.reshape(block_count, rows_per_block, kv_heads, HEAD_DIMENSION)
    value_blocks = value_piece.reshape(block_count, rows_per_block, kv_heads, HEAD_DIMENSION)
    first_keys = jnp.arange(block_count, dtype=jnp.int32) * rows_per_block

    def scan_step(inner, packed):
        key_blk, value_blk, first_key = packed

        def scan_visit(inner_state):
            running_max, norm_total, weighted = inner_state
            scores = (
                jnp.einsum(
                    "qgjd,kgd->gjqk", query_rows, key_blk, preferred_element_type=jnp.float32
                )
                * score_scale
            )
            key_pos = first_key + jnp.arange(rows_per_block, dtype=jnp.int32)
            allowed = key_pos[None, :] <= positions[:, None]
            scores = jnp.where(allowed, scores, masked_score)
            new_max = jnp.maximum(running_max, jnp.max(scores, axis=-1))
            decay = jnp.exp(running_max - new_max)
            weights = jnp.exp(scores - new_max[..., None])
            norm_total = norm_total * decay + jnp.sum(weights, axis=-1)
            weighted = weighted * decay[..., None] + jnp.einsum(
                "gjqk,kgd->gjqd",
                weights.astype(jnp.bfloat16),
                value_blk,
                preferred_element_type=jnp.float32,
            )
            return (new_max, norm_total, weighted)

        def scan_unchanged(inner_state):
            return inner_state

        return (lax.cond(first_key <= last_query, scan_visit, scan_unchanged, inner), None)

    carried, _ = lax.scan(scan_step, carried, (key_blocks, value_blocks, first_keys))
    running_max, norm_total, weighted = carried
    log_total = running_max + jnp.log(norm_total)
    attention_result = jnp.transpose(weighted / norm_total[..., None], (2, 0, 1, 3))
    attended_low = attention_result.reshape(tok_rows, local_heads * HEAD_DIMENSION).astype(
        jnp.bfloat16
    )
    attn_out = (
        over_heads(jnp.dot(attended_low, full_out, preferred_element_type=jnp.float32)) + b_out
    )
    hidden = residual + attn_out
    gate_up_full = w_gate_up[0]
    gate_bias_full = b_gate_up[0]
    down_full = w_down[0]
    hidden_units = down_full.shape[0]
    gate_up_weight = gate_up_full.reshape(model_width, 2 * hidden_units)
    gate_up_bias = gate_bias_full.reshape(-1)
    normed_moe, moe_norm_back = jax.vjp(rms_norm, hidden, gain_moe)
    moe_input = normed_moe.astype(jnp.bfloat16)
    logits = jnp.dot(moe_input, w_router, preferred_element_type=jnp.float32) + b_router
    chosen = jnp.take_along_axis(logits, routes, axis=1)
    gates = jax.nn.softmax(chosen, axis=-1)
    flat_routes = routes.reshape(-1)
    route_hits = (flat_routes[:, None] == jnp.arange(experts, dtype=jnp.int32)[None, :]).astype(
        jnp.int32
    )
    slot_rank = jnp.sum((jnp.cumsum(route_hits, axis=0) - route_hits) * route_hits, axis=1)
    target = flat_routes * capacity + slot_rank
    outgoing = (
        jnp.zeros((experts * capacity, model_width), jnp.bfloat16)
        .at[target]
        .set(jnp.repeat(moe_input, top_count, axis=0))
    )
    arrived = to_experts(outgoing.reshape(experts, capacity, model_width))
    arrived_rows = arrived.reshape(-1, model_width)
    projected = (
        jnp.dot(arrived_rows, gate_up_weight, preferred_element_type=jnp.float32) + gate_up_bias
    )
    activated, act_back = jax.vjp(
        expert_act, projected[:, :hidden_units], projected[:, hidden_units:]
    )
    act_low = activated.astype(jnp.bfloat16)
    partial_out = jnp.dot(act_low, down_full, preferred_element_type=jnp.float32).reshape(
        arrived.shape
    )
    expert_out = (from_hidden(partial_out) + b_down[0]).astype(jnp.bfloat16)
    returned = to_sources(expert_out)
    picked = (
        jnp.take(returned.reshape(-1, model_width), target, axis=0)
        .reshape(tok_rows, top_count, model_width)
        .astype(jnp.float32)
    )
    mixed = (hidden + jnp.sum(gates[..., None] * picked, axis=1)).astype(jnp.bfloat16)
    upstream = cotangent.astype(jnp.float32)
    gate_grad = jnp.sum(picked * upstream[:, None, :], axis=-1)
    slot_grad = (
        (gates[..., None] * upstream[:, None, :]).astype(jnp.bfloat16).reshape(-1, model_width)
    )
    grad_rows = jnp.zeros((experts * capacity, model_width), jnp.bfloat16).at[target].set(slot_grad)
    expert_grad = to_experts(grad_rows.reshape(experts, capacity, model_width)).reshape(
        -1, model_width
    )
    down_grad_local = project_grad(act_low, expert_grad)
    down_bias_local = jnp.sum(expert_grad, axis=0, dtype=jnp.float32)
    act_grad = jnp.dot(expert_grad, down_full.T, preferred_element_type=jnp.float32)
    gate_part, up_part = act_back(act_grad)
    proj_grad = jnp.concatenate([gate_part, up_part], axis=1).astype(jnp.bfloat16)
    gate_grad_local = project_grad(arrived_rows, proj_grad).reshape(model_width, 2, hidden_units)
    gate_bias_local = jnp.sum(proj_grad, axis=0, dtype=jnp.float32).reshape(2, hidden_units)
    grad_w_gate_up = gate_grad_local[None]
    grad_b_gate_up = gate_bias_local[None]
    grad_w_down = down_grad_local[None]
    grad_b_down = down_bias_local[None]
    input_grad = jnp.dot(proj_grad, gate_up_weight.T, preferred_element_type=jnp.float32).reshape(
        arrived.shape
    )
    back_rows = to_sources(from_hidden(input_grad).astype(jnp.bfloat16))
    moe_grad = jnp.sum(
        jnp.take(back_rows.reshape(-1, model_width), target, axis=0).reshape(
            tok_rows, top_count, model_width
        ),
        axis=1,
        dtype=jnp.float32,
    )
    chosen_grad = gates * (gate_grad - jnp.sum(gates * gate_grad, axis=1, keepdims=True))
    route_onehot = (routes[..., None] == jnp.arange(experts, dtype=jnp.int32)).astype(jnp.float32)
    logit_grad = jnp.sum(route_onehot * chosen_grad[..., None], axis=1).astype(jnp.bfloat16)
    grad_w_router = project_grad(moe_input, logit_grad)
    grad_b_router = jnp.sum(logit_grad, axis=0, dtype=jnp.float32)
    moe_grad = moe_grad + jnp.dot(logit_grad, w_router.T, preferred_element_type=jnp.float32)
    hidden_norm_grad, grad_gain_moe = moe_norm_back(moe_grad)
    hidden_grad = upstream + hidden_norm_grad
    branch_grad = hidden_grad.astype(jnp.bfloat16)
    grad_b_out = jnp.sum(branch_grad, axis=0, dtype=jnp.float32)
    full_query, full_kv, full_out = (
        lax.all_gather(w_query, ("seq", "ctx"), axis=0, tiled=True),
        lax.all_gather(key_value_weight, ("seq", "ctx"), axis=0, tiled=True),
        lax.all_gather(w_out, ("seq", "ctx"), axis=1, tiled=True),
    )
    grad_w_out = project_grad(attended_low, branch_grad)
    out_grad = jnp.dot(branch_grad, full_out.T, preferred_element_type=jnp.float32).astype(
        jnp.bfloat16
    )
    out_grad = out_grad.reshape(tok_rows, kv_heads, query_group_width, HEAD_DIMENSION)
    row_delta = jnp.einsum("qgjd,qgjd->gjq", out_grad.astype(jnp.float32), attention_result)
    sink_share = jnp.exp(sinks.reshape(kv_heads, query_group_width, 1) - log_total)
    grad_sinks = -jnp.sum(sink_share * row_delta, axis=-1).reshape(-1)

    def cycle_step(cycle_turn, carried):
        key_blk, value_blk, key_grad, value_grad, query_grad = carried
        source_rank = (ctx_rank - cycle_turn) % ctx_size

        def cycle_visit(grads_in):
            key_acc, value_acc, query_acc = grads_in
            scores = (
                jnp.einsum(
                    "qgjd,kgd->gjqk", query_rows, key_blk, preferred_element_type=jnp.float32
                )
                * score_scale
            )
            key_pos = source_rank * tok_rows + jnp.arange(tok_rows, dtype=jnp.int32)
            allowed = key_pos[None, :] <= positions[:, None]
            probs = jnp.where(allowed, jnp.exp(scores - log_total[..., None]), 0.0)
            prob_grad = jnp.einsum(
                "qgjd,kgd->gjqk", out_grad, value_blk, preferred_element_type=jnp.float32
            )
            score_grad = (probs * (prob_grad - row_delta[..., None])).astype(jnp.bfloat16)
            query_acc = (
                query_acc
                + jnp.einsum(
                    "gjqk,kgd->qgjd", score_grad, key_blk, preferred_element_type=jnp.float32
                )
                * score_scale
            )
            key_acc = (
                key_acc
                + jnp.einsum(
                    "gjqk,qgjd->kgd", score_grad, query_rows, preferred_element_type=jnp.float32
                )
                * score_scale
            )
            value_acc = value_acc + jnp.einsum(
                "gjqk,qgjd->kgd",
                probs.astype(jnp.bfloat16),
                out_grad,
                preferred_element_type=jnp.float32,
            )
            return (key_acc, value_acc, query_acc)

        def cycle_unchanged(grads_in):
            return grads_in

        key_grad, value_grad, query_grad = lax.cond(
            source_rank <= ctx_rank,
            cycle_visit,
            cycle_unchanged,
            (key_grad, value_grad, query_grad),
        )
        key_blk, value_blk = passed_along((key_blk, value_blk), "ctx", 1)
        key_grad, value_grad = (
            shifted(key_grad.astype(jnp.bfloat16), "ctx", 1).astype(key_grad.dtype),
            shifted(value_grad.astype(jnp.bfloat16), "ctx", 1).astype(value_grad.dtype),
        )
        return (key_blk, value_blk, key_grad, value_grad, query_grad)

    cycle_state = (
        key_matrix_rows,
        value_matrix_rows,
        jnp.zeros((tok_rows, kv_heads, HEAD_DIMENSION), jnp.float32),
        jnp.zeros((tok_rows, kv_heads, HEAD_DIMENSION), jnp.float32),
        jnp.zeros((tok_rows, kv_heads, query_group_width, HEAD_DIMENSION), jnp.float32),
    )
    cycle_state = lax.fori_loop(0, ctx_size, cycle_step, cycle_state)
    key_grad = cycle_state[2]
    value_grad = cycle_state[3]
    query_grad = cycle_state[4]
    query_pre = rotate_back(
        query_grad.reshape(tok_rows, local_heads, HEAD_DIMENSION), cosine_lookup, sine_lookup
    )
    query_pre = query_pre.reshape(tok_rows, local_heads * HEAD_DIMENSION).astype(jnp.bfloat16)
    key_pre = rotate_back(key_grad, cosine_lookup, sine_lookup).reshape(tok_rows, key_value_width)
    kv_grad = jnp.concatenate(
        [key_pre, value_grad.reshape(tok_rows, key_value_width)], axis=1
    ).astype(jnp.bfloat16)
    grad_b_query = jnp.sum(query_pre, axis=0, dtype=jnp.float32)
    grad_b_key_value = jnp.sum(kv_grad, axis=0, dtype=jnp.float32).reshape(2, key_value_width)
    weight_query = project_grad(normed_low, query_pre)
    weight_kv = project_grad(normed_low, kv_grad).reshape(model_width, 2, key_value_width)
    input_part = jnp.dot(query_pre, full_query.T, preferred_element_type=jnp.float32)
    input_part = input_part + jnp.dot(
        kv_grad,
        full_kv.reshape(model_width, 2 * key_value_width).T,
        preferred_element_type=jnp.float32,
    )
    normed_grad = over_heads(input_part)
    tokens_norm_grad, grad_gain_attn = attn_norm_back(normed_grad)
    grad_tokens = (hidden_grad + tokens_norm_grad).astype(jnp.bfloat16)
    grad_w_query, grad_w_key_value, grad_w_out = (
        lax.psum_scatter(weight_query, ("seq", "ctx"), scatter_dimension=0, tiled=True),
        lax.psum_scatter(weight_kv, ("seq", "ctx"), scatter_dimension=0, tiled=True),
        lax.psum_scatter(grad_w_out, ("seq", "ctx"), scatter_dimension=1, tiled=True),
    )
    summed = lax.psum(
        (
            grad_gain_attn,
            grad_b_query,
            grad_b_key_value,
            grad_sinks,
            grad_b_out,
            grad_gain_moe,
            grad_w_router,
            grad_b_router,
        ),
        ("seq", "ctx"),
    )
    return (
        mixed,
        grad_tokens,
        summed[0],
        grad_w_query,
        summed[1],
        grad_w_key_value,
        summed[2],
        summed[3],
        grad_w_out,
        summed[4],
        summed[5],
        summed[6],
        summed[7],
        grad_w_gate_up,
        grad_b_gate_up,
        grad_w_down,
        grad_b_down,
    )


def solution(mesh):
    in_specs = (
        P(("seq", "ctx"), None),
        P(),
        P(("seq", "ctx"), "tp"),
        P("tp"),
        P(("seq", "ctx"), None, "tp"),
        P(None, "tp"),
        P("tp"),
        P("tp", ("seq", "ctx")),
        P(),
        P(),
        P(),
        P(),
        P(("seq", "ctx"), None),
        P("ctx", None, None, ("seq", "tp")),
        P("ctx", None, ("seq", "tp")),
        P("ctx", ("seq", "tp"), None),
        P("ctx", None),
        P(("seq", "ctx"), None),
    )
    out_specs = (
        P(("seq", "ctx"), None),
        P(("seq", "ctx"), None),
        P(),
        P(("seq", "ctx"), "tp"),
        P("tp"),
        P(("seq", "ctx"), None, "tp"),
        P(None, "tp"),
        P("tp"),
        P("tp", ("seq", "ctx")),
        P(),
        P(),
        P(),
        P(),
        P("ctx", None, None, ("seq", "tp")),
        P("ctx", None, ("seq", "tp")),
        P("ctx", ("seq", "tp"), None),
        P("ctx", None),
    )
    return jax.shard_map(
        on_device, mesh=mesh, in_specs=in_specs, out_specs=out_specs, check_vma=False
    )
```

profile of v0, /device:TPU:0, one launch (start us, length us, event | category | flops | bytes accessed | tf_op | source)
XLA Modules:
  0.0 2987.7 jit_solution(5619959633382923589)
XLA Ops:
  13.9 65.8 %all-gather.10.cloned.1.call-done = bf16[2880,2,256]{2,1,0:T(2,128)(2,1)} async-done(((bf16[180,2,256]{2,1,0:T(2,128)(2,1)}), bf16[2880,2,256]{2,1,0:T(2,128)(2,1)}) %all-gather.10.cloned.1.call-update) | async-done | bytes 2949136 | tf_op jit(solution)/shard_map/all_gather | solution.py:144
  85.8 33.3 %all_gather.27 = bf16[1024,4,64]{0,2,1:T(8,128)(2,1)S(1)} all-gather(bf16[128,4,64]{0,2,1:T(8,128)(2,1)} %bitcast.29), channel_id=1, replica_groups=mesh['seq'=2,'ctx'=8,'tp'=2] {'ctx'}, dimensions={0}, use_global_device_ids=true | all-gather | bytes 589824 | tf_op jit(solution)/shard_map/all_gather | solution.py:179
  119.2 30.8 %all_gather.25 = bf16[1024,4,64]{0,2,1:T(8,128)(2,1)S(1)} all-gather(bf16[128,4,64]{0,2,1:T(8,128)(2,1)S(1)} %pad_maximum_fusion.3), channel_id=1, replica_groups=mesh['seq'=2,'ctx'=8,'tp'=2] {'ctx'}, dimensions={0}, use_global_device_ids=true | all-gather | bytes 589824 | tf_op jit(solution)/shard_map/all_gather | solution.py:178
  150.0 91.4 %all-gather.16.cloned.1.call-done = bf16[16,180,2048]{2,1,0:T(8,128)(2,1)} async-done(((bf16[1,180,2048]{2,1,0:T(8,128)(2,1)}), bf16[16,180,2048]{2,1,0:T(8,128)(2,1)}) %all-gather.16.cloned.1.call-update) | async-done | bytes 11796496 | tf_op jit(solution)/shard_map/all_gather | solution.py:143
  241.5 11.8 reshape.432
  253.3 6.3 convolution_add_fusion.2
  262.5 10.0 while.39
  264.4 6.1 conditional.6
  273.6 115.9 %all-gather.18.cloned.1.call-done = bf16[16,180,2048]{2,1,0:T(8,128)(2,1)} async-done(((bf16[1,180,2048]{2,1,0:T(8,128)(2,1)}), bf16[16,180,2048]{2,1,0:T(8,128)(2,1)}) %all-gather.18.cloned.1.call-update) | async-done | bytes 11796496 | tf_op jit(solution)/shard_map/all_gather | solution.py:145
  389.5 11.7 reshape.434
  401.3 8.6 convolution_convert_fusion.2
  416.6 7.8 mul.463
  434.9 10.5 scatter_custom_fusion.1
  445.5 8.4 copy.234
  453.9 136.4 %all_to_all.20 = bf16[8,128,2880]{1,2,0:T(8,128)(2,1)} all-to-all(bf16[8,128,2880]{1,2,0:T(8,128)(2,1)} %copy.234), channel_id=1, replica_groups=mesh['seq'=2,'ctx'=8,'tp'=2] {'ctx'}, dimensions={0} | all-to-all | bytes 11796480 | tf_op jit(solution)/shard_map/all_to_all | solution.py:92
  596.2 10.5 scatter_custom_fusion
  606.7 8.6 copy.227
  615.2 134.2 %all_to_all.21 = bf16[8,128,2880]{1,2,0:T(8,128)(2,1)} all-to-all(bf16[8,128,2880]{1,2,0:T(8,128)(2,1)} %copy.227), channel_id=1, replica_groups=mesh['seq'=2,'ctx'=8,'tp'=2] {'ctx'}, dimensions={0} | all-to-all | bytes 11796480 | tf_op jit(solution)/shard_map/all_to_all | solution.py:92
  750.2 16.7 copy.235
  766.9 125.2 %all-gather.12.cloned.1.call-done = bf16[16,128,2880]{1,2,0:T(8,128)(2,1)} async-done(((bf16[8,128,2880]{1,2,0:T(8,128)(2,1)}), bf16[16,128,2880]{1,2,0:T(8,128)(2,1)}) %all-gather.12.cloned.1.call-update) | async-done | bytes 11796496 | tf_op jit(solution)/shard_map/all_gather | solution.py:93
  892.1 25.0 fusion.41
  917.1 23.5 fusion.50
  944.0 24.3 convolution_convert_fusion.1
  971.2 14.8 convolution_convert_fusion
  986.0 118.5 %reduce-scatter.9.cloned.1.call-done = bf16[1,8,128,2880]{2,3,1,0:T(8,128)(2,1)} async-done(((bf16[2,8,128,2880]{2,3,1,0:T(8,128)(2,1)}), bf16[1,8,128,2880]{2,3,1,0:T(8,128)(2,1)}) %reduce-scatter.9.cloned.1.call-update) | async-done | bytes 5898256 | tf_op jit(solution)/shard_map/reduce_scatter | solution.py:97
  1104.5 138.3 %reduce-scatter.7.cloned.1.call-done = bf16[1,8,128,2880]{2,3,1,0:T(8,128)(2,1)} async-done(((bf16[2,8,128,2880]{2,3,1,0:T(8,128)(2,1)}), bf16[1,8,128,2880]{2,3,1,0:T(8,128)(2,1)}) %reduce-scatter.7.cloned.1.call-update) | async-done | bytes 5898256 | tf_op jit(solution)/shard_map/reduce_scatter | solution.py:97
  1242.9 47.7 %all-reduce.19.cloned.1.call-done = (bf16[8,128,2880]{1,2,0:T(8,128)(2,1)}, bf16[8,128,2880]{1,2,0:T(8,128)(2,1)}) async-done(((bf16[8,128,2880]{1,2,0:T(8,128)(2,1)}, bf16[8,128,2880]{1,2,0:T(8,128)(2,1)}), (bf16[8,128,2880]{1,2,0:T(8,128)(2,1)}, bf16[8,128,2880]{1,2,0:T(8,128)(2,1)})) %all-reduce.19.cloned.1.call-update) | async-done | bytes 11796496 | tf_op jit(solution)/shard_map/psum | solution.py:100
  1290.5 5.9 all-to-all-start.3
  1296.5 6.4 add_convert_fusion
  1302.9 123.8 %all-to-all-done.3 = bf16[8,128,2880]{1,2,0:T(8,128)(2,1)} async-done(((bf16[8,128,2880]{1,2,0:T(8,128)(2,1)}), bf16[8,128,2880]{1,2,0:T(8,128)(2,1)}, u32[]{:S(2)}, u32[]{:S(2)}) %all-to-all-start.3) | async-done | bytes 5898272 | tf_op jit(solution)/shard_map/all_to_all | solution.py:104
  1426.7 4.8 all-to-all-start.1
  1433.5 25.1 copy.228
  1458.6 18.6 reshape.450
  1480.1 15.2 convolution_bitcast_fusion.3
  1495.3 21.6 convolution_bitcast_fusion.2
  1516.9 8.3 copy.238
  1525.2 10.2 gather_fusion.2
  1535.4 25.4 all-to-all-done.1
  1560.8 8.3 copy.230
  1569.1 9.7 gather_fusion.1
  1582.8 7.1 select_convert_fusion
  1589.9 7.6 reshape.380
  1597.6 6.4 reduce_sum.219
  1605.6 5.7 multiply_reduce_fusion.2
  1611.3 7.8 reshape.379
  1619.2 7.0 multiply_reduce_fusion.1
  1627.8 4.7 convert_reduce_fusion.2
  1632.4 7.6 convolution_convert_fusion.3
  1640.1 9.6 fusion.87
  1652.5 123.5 %while.40 = (s32[]{:T(128)}, bf16[128,4,64]{0,2,1:T(8,128)(2,1)S(1)}, bf16[128,4,64]{0,2,1:T(8,128)(2,1)}, f32[128,4,64]{0,2,1:T(8,128)S(1)}, f32[128,4,64]{0,2,...) while((s32[]{:T(128)}, ...), condition=%wide.region_29.31_spmd.clone, body=%wide.region_26.30_spmd.clone.sunk | while | flops 340050176 | bytes 17043056 | solution.py:390
  1666.7 5.8 collective-permute-start.3
  1688.0 5.7 collective-permute-start.2
  1706.4 4.6 collective-permute-start
  1723.3 6.7 collective-permute-start.1
  1736.2 4.4 collective-permute-start
  1778.0 6.3 fusion.102
  1786.3 486.5 %fusion.5 = f32[2048,184]{0,1:T(8,128)S(1)} fusion(f32[2048,2880]{0,1:T(8,128)} %fusion.87), kind=kCustom, calls=%all-reduce-scatter.1 | all-reduce-scatter fusion | flops 6029313 | bytes 25100800
  2272.8 9.8 fusion.95
  2286.1 7.9 reshape.377
  2297.9 567.0 %fusion.4 = f32[184,2048]{1,0:T(8,128)} fusion(f32[2880,2048]{1,0:T(8,128)} %fusion.95), kind=kCustom, calls=%all-reduce-scatter | all-reduce-scatter fusion | flops 6029313 | bytes 25100800
  2869.3 6.0 convert_reduce_fusion
  2879.7 6.3 concatenate.51
  2886.0 7.5 concatenate.50
  2901.0 74.0 %all-reduce.5 = (f32[2880]{0:T(1024)}, f32[2048]{0:T(1024)}, f32[2,256]{1,0:T(2,128)}, f32[32]{0:T(128)}, f32[2880]{0:T(1024)}, /*index=5*/f32[2880]{0:T(1024)}, f32[8]{0:T(128)}) all-reduce(f32[2880]{0:T(1024)S(1)} %get-tuple-element.658, f32[2048]{0:T(1024)S(1)} %reduce_sum.228, ...), channel_id=1, replica_groups=mesh['seq'=2,'ctx'=8,'tp'=2] {'seq','ctx'}, use_global_device_ids=true, to_apply=%region_33.35 | all-reduce | flops 11240 | bytes 89920 | tf_op jit(solution)/shard_map/psum | solution.py:420
  (438 shorter events, 199.8 us)
Async XLA Ops:
  7.2 424.4 %copy-start = (bf16[2880,8]{0,1:T(8,128)(2,1)S(1)}, bf16[2880,8]{0,1:T(8,128)(2,1)}, u32[]{:S(2)}) copy-start(bf16[2880,8]{0,1:T(8,128)(2,1)} %param.38) | copy-start | bytes 138244
  7.2 72.5 %all-gather.10.cloned.1.call-start = ((), (), s32[]{:S(2)}) async-start(), calls=%async_computation.6 | async-start | bytes 3133440 | tf_op jit(solution)/shard_map/all_gather | solution.py:144
  8.0 233.5 %all-gather.16.cloned.1.call-start = ((), (), s32[]{:S(2)}) async-start(), calls=%async_computation.13 | async-start | bytes 12812288 | tf_op jit(solution)/shard_map/all_gather | solution.py:143
  8.7 380.8 %all-gather.18.cloned.1.call-start = ((), (), s32[]{:S(2)}) async-start(), calls=%async_computation.14 | async-start | bytes 12812288 | tf_op jit(solution)/shard_map/all_gather | solution.py:145
  9.4 417.9 %all-reduce.13.cloned.1.call-start = ((), (), s32[]{:S(2)}) async-start(), calls=%async_computation.7 | async-start | bytes 1474560 | tf_op jit(solution)/shard_map/psum | solution.py:88
  10.8 251.5 %copy-start.47 = (f32[4,8]{1,0:T(4,128)}, f32[4,8]{1,0:T(4,128)S(1)}, u32[]{:S(2)}) copy-start(f32[4,8]{1,0:T(4,128)S(1)} %broadcast_in_dim.59) | copy-start | bytes 388
  13.1 240.2 %copy-start.43 = (f32[128]{0:T(128)}, f32[128]{0:T(128)S(1)}, u32[]{:S(2)}) copy-start(f32[128]{0:T(128)S(1)} %fusion.82) | copy-start | bytes 1540
  13.9 247.0 %copy-start.31 = (f32[128,32]{0,1:T(8,128)}, f32[128,32]{0,1:T(8,128)S(1)}, u32[]{:S(2)}) copy-start(f32[128,32]{0,1:T(8,128)S(1)} %get-tuple-element.745) | copy-start | bytes 49156
  13.9 247.0 %copy-start.32 = (f32[128,32]{0,1:T(8,128)}, f32[128,32]{0,1:T(8,128)S(1)}, u32[]{:S(2)}) copy-start(f32[128,32]{0,1:T(8,128)S(1)} %get-tuple-element.746) | copy-start | bytes 49156
  272.5 128.7 %copy-start.3 = (bf16[128,4,8,64]{0,3,2,1:T(8,128)(2,1)}, bf16[128,4,8,64]{0,3,2,1:T(8,128)(2,1)S(1)}, u32[]{:S(2)}) copy-start(bf16[128,4,8,64]{0,3,2,1:T(8,128)(2,1)S(1)} %get-tuple-element.1033) | copy-start | bytes 1572868
  272.5 128.7 %copy-start.15 = (f32[4,8,128,64]{2,3,1,0:T(8,128)}, f32[4,8,128,64]{2,3,1,0:T(8,128)S(1)}, u32[]{:S(2)}) copy-start(f32[4,8,128,64]{2,3,1,0:T(8,128)S(1)} %get-tuple-element.491) | copy-start | bytes 3145732
  272.5 128.7 %copy-start.21 = (f32[4,8,128]{2,1,0:T(8,128)}, f32[4,8,128]{2,1,0:T(8,128)S(1)}, u32[]{:S(2)}) copy-start(f32[4,8,128]{2,1,0:T(8,128)S(1)} %get-tuple-element.493) | copy-start | bytes 49156
  272.5 128.7 %copy-start.25 = (f32[4,8,128]{2,1,0:T(8,128)}, f32[4,8,128]{2,1,0:T(8,128)S(1)}, u32[]{:S(2)}) copy-start(f32[4,8,128]{2,1,0:T(8,128)S(1)} %get-tuple-element.492) | copy-start | bytes 49156
  409.9 340.4 %all-gather.14.cloned.1.call-start = ((), (), s32[]{:S(2)}) async-start(), calls=%async_computation.12 | async-start | bytes 17694720 | tf_op jit(solution)/shard_map/all_gather | solution.py:93
  431.6 158.7 %copy-start.13 = (bf16[128,2880]{0,1:T(8,128)(2,1)}, bf16[128,2880]{0,1:T(8,128)(2,1)S(1)}, u32[]{:S(2)}) copy-start(bf16[128,2880]{0,1:T(8,128)(2,1)S(1)} %multiply_convert_fusion.4) | copy-start | bytes 2211844
  590.2 301.9 %all-gather.12.cloned.1.call-start = ((), (), s32[]{:S(2)}) async-start(), calls=%async_computation.11 | async-start | bytes 17694720 | tf_op jit(solution)/shard_map/all_gather | solution.py:93
  749.5 355.0 %reduce-scatter.9.cloned.1.call-start = ((), (), s32[]{:S(2)}) async-start(), calls=%async_computation.9 | async-start | bytes 17694720 | tf_op jit(solution)/shard_map/reduce_scatter | solution.py:97
  940.6 536.6 %copy-start.9 = (bf16[2048,720]{0,1:T(8,128)(2,1)}, bf16[2048,720]{0,1:T(8,128)(2,1)S(1)}, u32[]{:S(2)}) copy-start(bf16[2048,720]{0,1:T(8,128)(2,1)S(1)} %get-tuple-element.733) | copy-start | bytes 8847364
  968.3 274.5 %reduce-scatter.7.cloned.1.call-start = ((), (), s32[]{:S(2)}) async-start(), calls=%async_computation.8 | async-start | bytes 17694720 | tf_op jit(solution)/shard_map/reduce_scatter | solution.py:97
  986.0 304.5 %all-reduce.19.cloned.1.call-start = ((), (), s32[]{:S(2)}) async-start(), calls=%async_computation.16 | async-start | bytes 23592960 | tf_op jit(solution)/shard_map/psum | solution.py:100
  1290.5 136.2 %all-to-all-start.3 = ((bf16[8,128,2880]{1,2,0:T(8,128)(2,1)}), bf16[8,128,2880]{1,2,0:T(8,128)(2,1)}, u32[]{:S(2)}, u32[]{:S(2)}) async-start(bf16[8,128,2880]{1,2,0:T(8,128)(2,1)} %get-tuple-element.714), calls=%async_computation.5 | async-start | bytes 11796480 | tf_op jit(solution)/shard_map/all_to_all | solution.py:104
  1302.9 128.7 %copy-start.63 = (u32[32]{0:T(128)S(1)}, u32[32]{0:T(128)}, u32[]{:S(2)}) copy-start(u32[32]{0:T(128)} %constant.190) | copy-start | bytes 388
  1302.9 130.6 %copy-start.50 = (s32[512]{0:T(512)S(1)}, s32[512]{0:T(512)}, u32[]{:S(2)}) copy-start(s32[512]{0:T(512)} %copy-done.49) | copy-start | bytes 6148
  1302.9 130.6 %copy-start.52 = (s32[512]{0:T(512)S(1)}, s32[512]{0:T(512)}, u32[]{:S(2)}) copy-start(s32[512]{0:T(512)} %copy-done.51) | copy-start | bytes 6148
  1426.7 134.1 %all-to-all-start.1 = ((bf16[8,128,2880]{1,2,0:T(8,128)(2,1)}), bf16[8,128,2880]{1,2,0:T(8,128)(2,1)}, u32[]{:S(2)}, u32[]{:S(2)}) async-start(bf16[8,128,2880]{1,2,0:T(8,128)(2,1)} %add_convert_fusion), calls=%async_computation.2 | async-start | bytes 11796480 | tf_op jit(solution)/shard_map/all_to_all | solution.py:104
  1431.5 1467.4 %all-reduce.15.cloned.1.call-start = ((), (), s32[]{:S(2)}) async-start(), calls=%async_computation.10 | async-start | bytes 1474560 | tf_op jit(solution)/shard_map/psum | solution.py:88
  1657.0 7.6 collective-permute-start.3
  1658.5 7.0 collective-permute-start.2
  1658.6 7.0 collective-permute-start
  1660.5 5.3 collective-permute-start.1
  1666.7 16.6 collective-permute-start.3
  1672.5 10.8 collective-permute-start.2
  1674.9 8.4 collective-permute-start
  1679.2 5.3 collective-permute-start.1
  1685.5 15.0 collective-permute-start.3
  1688.0 12.5 collective-permute-start.2
  1693.7 6.9 collective-permute-start
  1697.1 4.7 collective-permute-start.1
  1702.7 11.8 collective-permute-start.3
  1705.3 9.3 collective-permute-start.2
  1706.4 8.1 collective-permute-start
  1711.1 4.7 collective-permute-start.1
  1716.7 13.3 collective-permute-start.3
  1719.3 10.8 collective-permute-start.2
  1720.6 9.5 collective-permute-start
  1723.3 8.0 collective-permute-start.1
  1732.2 11.8 collective-permute-start.3
  1734.8 9.2 collective-permute-start.2
  1736.2 7.9 collective-permute-start
  1740.7 4.6 collective-permute-start.1
  1746.2 12.5 collective-permute-start.3
  1749.2 9.6 collective-permute-start.2
  1752.6 6.2 collective-permute-start
  1755.3 4.7 collective-permute-start.1
  1760.9 13.8 collective-permute-start.3
  1763.5 11.3 collective-permute-start.2
  1766.4 8.4 collective-permute-start
  1770.8 5.2 collective-permute-start.1
  1786.2 486.6 %copy-start.24 = (bf16[128,32,64]{0,2,1:T(8,128)(2,1)S(1)}, bf16[128,32,64]{0,2,1:T(8,128)(2,1)}, u32[]{:S(2)}) copy-start(bf16[128,32,64]{0,2,1:T(8,128)(2,1)} %copy-done.23) | copy-start | bytes 1572868
  1786.2 486.6 %copy-start.28 = (f32[2880]{0:T(1024)S(1)}, f32[2880]{0:T(1024)}, u32[]{:S(2)}) copy-start(f32[2880]{0:T(1024)} %param.29) | copy-start | bytes 34564
  1786.3 486.6 %copy-start.44 = (f32[128]{0:T(128)S(1)}, f32[128]{0:T(128)}, u32[]{:S(2)}) copy-start(f32[128]{0:T(128)} %copy-done.43) | copy-start | bytes 1540
  1786.3 1191.3 %all-reduce.17.cloned.1.call-start = ((), (), s32[]{:S(2)}) async-start(), calls=%async_computation.15 | async-start | bytes 11984896
  2294.8 584.9 %collective-permute-start.5 = (f32[2048,60]{0,1:T(8,128)}, f32[2048,60]{0,1:T(8,128)}, u32[]{:S(2)}, u32[]{:S(2)}) collective-permute-start(f32[2048,60]{0,1:T(8,128)} %slice.79), channel_id=1, source_target_pairs={{0,2},{2,4},{4,6},{6,8},{8,10},{10,12},{12,14},{14,16},{16,18},{18... | collective-permute-start | bytes 1474568
  2866.7 19.3 collective-permute-start.4
  (55 other events, 985.5 us)
Sparse Core Ops, SparseCore 0:
  10.7 68.8 all-gather.9
  82.4 159.0 all-gather.15
  244.2 145.3 all-gather.17
  410.0 17.3 all-reduce.12
  590.4 142.5 all-gather.13
  749.6 142.4 all-gather.11
  968.5 135.9 reduce-scatter.8
  1106.8 135.9 reduce-scatter.6
  1245.4 45.0 all-reduce.18
  1786.4 18.2 all-reduce.14
  2298.0 426.2 all-reduce.16
where the time goes:
time: 3000 us; the launch traced here: 2990 us
  blocking collectives  1460 us (49%)
  waiting for transfers between devices  867 us (29%)
  local copies, waits for them, and re-layouts  248 us (8%)
  matrix products  192 us (6%)
  starting transfers between devices  119 us (4%)
  other arithmetic  79.2 us (3%)
    unnamed x2, blocking collectives  1050 us
    all_to_all x2, blocking collectives, to_experts(): lax.all_to_all(outgoing, 'ctx', split_axis=0, concat_axis=0, tiled=True)  271 us
    reduce_scatter x2, waiting for transfers between devices, from_hidden(): lax.psum_scatter(partial_sum.astype(jnp.bfloat16), 'seq', scatter_dimensi...  257 us
    all_to_all x2, waiting for transfers between devices, to_sources(): lax.all_to_all(expert_rows, 'ctx', split_axis=0, concat_axis=0, tiled=True)  149 us
    all_gather x2, waiting for transfers between devices, to_experts(): return lax.all_gather(arrived[None], 'seq', axis=0, tiled=True)  125 us
    all_gather x1, waiting for transfers between devices, on_device(): lax.all_gather(w_out, ('seq', 'ctx'), axis=1, tiled=True)  116 us
    all_gather x1, waiting for transfers between devices, on_device(): lax.all_gather(w_query, ('seq', 'ctx'), axis=0, tiled=True)  91.4 us
    psum x1, blocking collectives, on_device(): lax.psum((grad_gain_attn, grad_b_query, grad_b_key_value, grad_sinks, gra...  74 us
  transfers between devices with their start and end apart: 47, of which 19 were waited for; matrix products, arithmetic and copies ran while one was open for 45% of the time, Pallas kernels for 0%

commit v1 on v0

v1 whole, which is shorter than its diff:
```python
import functools
import math

import jax
import jax.numpy as jnp
from jax import lax
from jax.experimental import pallas as pl
from jax.experimental.pallas import tpu as pltpu
from jax.sharding import PartitionSpec as P

HEAD_DIMENSION = 64

rms_eps = 1e-05
rope_base = 150000.0
clamp_limit = 7.0
glu_alpha = 1.702
masked_score = -1e30
vmem_bytes = 56 * 1024 * 1024
vmem_most = 63 * 1024 * 1024
bf16 = jnp.bfloat16
f32 = jnp.float32


def across(left, right):
    return lax.dot_general(left, right, (((1,), (1,)), ((), ())), preferred_element_type=f32)


def down(left, right):
    return lax.dot_general(left, right, (((0,), (0,)), ((), ())), preferred_element_type=f32)


def ring_place(index, size):
    half = index // 2
    return jnp.where(index % 2 == 0, half, size - 1 - half)


def ring_index(place, size):
    place = lax.rem(place + size, size)
    return jnp.where(place < size // 2, 2 * place, 2 * (size - 1 - place) + 1)


def greet(devices):
    barrier = pltpu.get_barrier_semaphore()
    for device in devices:
        pl.semaphore_signal(barrier, inc=1, device_id=device, device_id_type=pl.DeviceIdType.MESH)
    pl.semaphore_wait(barrier, len(devices))


def remote(src, dst, send_sem, recv_sem, device):
    copy = pltpu.make_async_remote_copy(
        src_ref=src,
        dst_ref=dst,
        send_sem=send_sem,
        recv_sem=recv_sem,
        device_id=device,
        device_id_type=pl.DeviceIdType.MESH,
    )
    copy.start()
    return copy


def rows_at(start, count):
    return pl.ds(pl.multiple_of(start, count), count)


class Around:
    def __init__(self, size):
        self.size = size
        self.seq = lax.axis_index("seq")
        self.ctx = lax.axis_index("ctx")
        self.core = lax.axis_index("tp")
        self.place = ring_place(self.ctx, size)
        self.right = (self.seq, ring_index(self.place + 1, size), self.core)
        self.left = (self.seq, ring_index(self.place - 1, size), self.core)
        self.across = (1 - self.seq, self.ctx, self.core)
        self.sibling = (self.seq, self.ctx, 1 - self.core)

    def index(self, offset):
        return ring_index(self.place + offset, self.size)

    def at(self, offset):
        return (self.seq, self.index(offset), self.core)


class RingGather:
    def __init__(self, around, both, x_ref, o_ref, ring_s, ring_r, cross_s, cross_r, core_s, core_r, loc):
        self.a, self.both, self.x, self.o = around, both, x_ref, o_ref
        self.rs, self.rr, self.cs, self.cr = ring_s, ring_r, cross_s, cross_r
        self.ts, self.tr, self.loc = core_s, core_r, loc
        self.rows = x_ref.shape[0]
        self.chunk = self.rows // 4
        size = around.size
        far, near = size // 2, size - 1 - size // 2
        if both:
            self.items = [(1, False, far, near), (0, False, near, far), (0, True, far, near)]
        else:
            self.items = [(0, False, far, near), (1, False, near, far)]

    def partners(self):
        a = self.a
        return [a.right, a.left, a.sibling] + ([a.across] if self.both else [])

    def spot(self, other, index, chunk):
        a = self.a
        if self.both:
            block = (1 - a.seq if other else a.seq) * a.size + index + a.core * 2 * a.size
            return rows_at(block * (2 * self.chunk) + chunk * self.chunk, self.chunk)
        return rows_at(index * self.rows + a.core * (2 * self.chunk) + chunk * self.chunk, self.chunk)

    def own(self, chunk):
        return self.x.at[rows_at(self.a.core * (2 * self.chunk) + chunk * self.chunk, self.chunk)]

    def hop(self, item, way, step, src, where):
        device = self.a.right if way == 0 else self.a.left
        copy = remote(
            src, self.o.at[where], self.rs.at[item, way, step], self.rr.at[item, way, step], device
        )
        self.ring[item, way, step] = copy
        self.sent.append(copy)

    def cross(self, slot, src, where):
        copy = remote(src, self.o.at[where], self.cs.at[slot], self.cr.at[slot], self.a.across)
        self.crossed[slot] = copy
        self.sent.append(copy)

    def share(self, where):
        slot = len(self.shared)
        src = self.o.at[where]
        copy = remote(src, src, self.ts.at[slot], self.tr.at[slot], self.a.sibling)
        self.shared.append(copy)
        self.sent.append(copy)

    def start(self):
        a = self.a
        self.ring, self.crossed, self.shared, self.sent = {}, {}, [], []
        if self.both:
            half = 2 * self.chunk
            block = a.seq * a.size + a.ctx
            pairs = [
                (self.x.at[pl.ds(core * half, half)], rows_at((core * 2 * a.size + block) * half, half))
                for core in range(2)
            ]
        else:
            pairs = [(self.x, rows_at(a.ctx * self.rows, self.rows))]
        self.local = [
            pltpu.make_async_copy(src, self.o.at[where], self.loc.at[at])
            for at, (src, where) in enumerate(pairs)
        ]
        for copy in self.local:
            copy.start()
        if self.both:
            self.cross(0, self.own(0), self.spot(False, a.ctx, 0))
        for item, (chunk, other, _, _) in enumerate(self.items):
            if not other:
                for way in range(2):
                    self.hop(item, way, 0, self.own(chunk), self.spot(False, a.ctx, chunk))
        self.landed = []
        if self.both:
            self.cross(1, self.own(1), self.spot(False, a.ctx, 1))
            self.landed.append((1, a.ctx))
            self.crossed[0].wait_recv()
            where = self.spot(True, a.ctx, 0)
            for way in range(2):
                self.hop(2, way, 0, self.o.at[where], where)
            self.share(where)

    def step(self, k):
        a = self.a
        for item, (chunk, other, right, left) in enumerate(self.items):
            for way, hops in ((0, right), (1, left)):
                if k >= hops:
                    continue
                self.ring[item, way, k].wait_recv()
                index = a.index(-(k + 1) if way == 0 else k + 1)
                where = self.spot(other, index, chunk)
                if k + 1 < hops:
                    self.hop(item, way, k + 1, self.o.at[where], where)
                if self.both and item == 0:
                    slot = 1 + len(self.landed)
                    self.cross(slot, self.o.at[where], where)
                    self.landed.append((slot, index))
                self.share(where)

    def finish(self):
        for slot, index in self.landed:
            self.crossed[slot].wait_recv()
            self.share(self.spot(True, index, 1))
        for copy in self.shared:
            copy.wait_recv()
        for copy in self.sent:
            copy.wait_send()
        for copy in self.local:
            copy.wait()

    @staticmethod
    def semaphores(size, both):
        items = 3 if both else 2
        shares = 2 * (size - 1) + (2 * size if both else 0)
        dma = pltpu.SemaphoreType.DMA
        return [
            dma((items, 2, size // 2)),
            dma((items, 2, size // 2)),
            dma((1 + size,)),
            dma((1 + size,)),
            dma((shares,)),
            dma((shares,)),
            dma((2,)),
        ]


def gather_kernel(size, both, *refs):
    if both:
        x_ref, half_ref, o_ref, whole_ref, held, half_s, half_r, half_l, *sems = refs
    else:
        x_ref, o_ref, *sems = refs
    ring = RingGather(Around(size), both, x_ref, o_ref, *sems)
    greet(ring.partners())
    ring.start()
    if both:
        where = whole_ref.at[rows_at(ring.a.core * half_ref.shape[0], half_ref.shape[0])]
        other = remote(half_ref, where, half_s, half_r, ring.a.sibling)
        here = pltpu.make_async_copy(half_ref, held, half_l.at[0])
        here.start()
        here.wait()
        here = pltpu.make_async_copy(held, where, half_l.at[1])
        here.start()
    for k in range(size // 2):
        ring.step(k)
    ring.finish()
    if both:
        here.wait()
        other.wait()


def ring_gather(x, size, ident, half=None):
    hbm = pl.BlockSpec(memory_space=pl.ANY)
    both = half is not None
    blocks = (2 if both else 1) * size
    shapes = [jax.ShapeDtypeStruct((blocks * x.shape[0], x.shape[1]), x.dtype)]
    if both:
        shapes.append(jax.ShapeDtypeStruct((2 * half.shape[0], half.shape[1]), half.dtype))
    dma = pltpu.SemaphoreType.DMA
    extra = [pltpu.VMEM(half.shape, half.dtype), dma(()), dma(()), dma((2,))] if both else []
    out = pl.pallas_call(
        functools.partial(gather_kernel, size, both),
        out_shape=shapes,
        in_specs=[hbm, hbm] if both else [hbm],
        out_specs=[hbm] * len(shapes),
        scratch_shapes=extra + RingGather.semaphores(size, both),
        compiler_params=pltpu.CompilerParams(
            collective_id=ident, has_side_effects=True, vmem_limit_bytes=vmem_bytes
        ),
        name="gather_all" if both else "gather_ctx",
    )(*((x, half) if both else (x,)))
    return out if both else out[0]


def enter_kernel(size, x_ref, w_ref, o_ref, wo_ref, w_s, w_r, wx_s, wx_r, wl, *sems):
    a = Around(size)
    ring = RingGather(a, False, x_ref, o_ref, *sems)
    order = []
    for d in range(1, size // 2 + 1):
        order += [d] if 2 * d == size else [d, size - d]
    greet(ring.partners() + [a.across] + [a.at(d) for d in order if 1 < d < size - 1])
    mine = a.seq * size + a.ctx
    local = pltpu.make_async_copy(w_ref.at[a.ctx], wo_ref.at[mine], wl)
    local.start()
    ring.start()
    crossed = [remote(w_ref.at[a.ctx], wo_ref.at[mine], wx_s.at[0], wx_r.at[0], a.across)]
    sent = {}
    for d in order:
        sent[d] = remote(w_ref.at[a.index(d)], wo_ref.at[mine], w_s.at[d], w_r.at[d], a.at(d))
    taken = 0

    def take():
        d = order[len(crossed) - 1]
        sent[d].wait_recv()
        block = wo_ref.at[a.seq * size + a.index(-d)]
        crossed.append(remote(block, block, wx_s.at[d], wx_r.at[d], a.across))

    for k in range(size // 2):
        ring.step(k)
        for _ in range(2):
            if len(crossed) < size:
                take()
    ring.finish()
    for copy in crossed:
        copy.wait()
    for copy in sent.values():
        copy.wait_send()
    local.wait()


def enter(x, w, size, ident):
    dma = pltpu.SemaphoreType.DMA
    hbm = pl.BlockSpec(memory_space=pl.ANY)
    return pl.pallas_call(
        functools.partial(enter_kernel, size),
        out_shape=(
            jax.ShapeDtypeStruct((size * x.shape[0], x.shape[1]), x.dtype),
            jax.ShapeDtypeStruct((2 * size,) + w.shape[1:], w.dtype),
        ),
        in_specs=[hbm, hbm],
        out_specs=(hbm, hbm),
        scratch_shapes=[dma((size,)), dma((size,)), dma((size,)), dma((size,)), dma(())]
        + RingGather.semaphores(size, False),
        compiler_params=pltpu.CompilerParams(collective_id=ident, has_side_effects=True),
        name="enter_rows_and_weights",
    )(x, w)


class RingSum:
    def __init__(
        self, around, both, p_ref, o_ref, acc, met, ringbuf, crossbuf, lastbuf,
        ring_s, ring_r, cross_s, cross_r, core_s, core_r, out_s, out_r, loc,
    ):
        self.a, self.both, self.p, self.o = around, both, p_ref, o_ref
        self.acc, self.met, self.ringbuf = acc, met, ringbuf
        self.crossbuf, self.lastbuf = crossbuf, lastbuf
        self.rs, self.rr, self.cs, self.cr = ring_s, ring_r, cross_s, cross_r
        self.ts, self.tr, self.os, self.or_, self.loc = core_s, core_r, out_s, out_r, loc
        self.rows = o_ref.shape[0]
        self.half, self.chunk = self.rows // 2, self.rows // 4
        size = around.size
        far, near = size // 2, size - 1 - size // 2
        if both:
            self.items = [(0, 1, far, near), (0, 0, near, far), (1, 0, far, near)]
        else:
            self.items = [(0, 0, far, near), (1, 0, near, far)]
        order = []
        for d in range(size // 2, 0, -1):
            order += [d] if 2 * d == size else [d, size - d]
        self.order = order + [0]

    def partners(self):
        a = self.a
        return [a.right, a.left, a.sibling] + ([a.across] if self.both else [])

    def spot(self, other, offset, core):
        a = self.a
        block = a.index(offset)
        if self.both:
            block = core * 2 * a.size + (1 - a.seq if other else a.seq) * a.size + block
        else:
            block = 2 * block + core
        return rows_at(block * self.half, self.half)

    def start(self):
        a = self.a
        self.pending, self.sent, self.ring, self.crossed = {}, [], {}, {}
        for other in ((1, 0) if self.both else (0,)):
            for j in self.order:
                away = remote(
                    self.p.at[self.spot(other, j, 1 - a.core)],
                    self.met.at[other, j],
                    self.ts.at[other, j],
                    self.tr.at[other, j],
                    a.sibling,
                )
                here = pltpu.make_async_copy(
                    self.p.at[self.spot(other, j, a.core)], self.acc.at[other, j], self.loc.at[other, j]
                )
                here.start()
                self.pending[other, j] = (away, here)
                self.sent.append(away)
        if self.both:
            for j in self.order:
                self.ready(1, j)
                self.crossed[j] = remote(
                    self.part(self.acc, 1, j, 1), self.crossbuf.at[j], self.cs.at[j], self.cr.at[j], a.across
                )
                self.sent.append(self.crossed[j])

    def part(self, ref, other, j, chunk):
        return ref.at[other, j, pl.ds(chunk * self.chunk, self.chunk)]

    def ready(self, other, j):
        if (other, j) in self.pending:
            away, here = self.pending.pop((other, j))
            away.wait_recv()
            here.wait()
            self.add(self.acc.at[other, j], self.met.at[other, j])

    def add(self, into, more):
        into[...] = (into[...].astype(f32) + more[...].astype(f32)).astype(into.dtype)

    def prepare(self, other, j, chunk):
        self.ready(other, j)
        if self.both and chunk == 1 and j in self.crossed:
            self.crossed.pop(j).wait_recv()
            self.add(self.part(self.acc, 0, j, 1), self.crossbuf.at[j])

    def step(self, k):
        a = self.a
        for item, (chunk, other, right, left) in enumerate(self.items):
            for way, hops in ((0, right), (1, left)):
                d = hops - k
                if d < 1:
                    continue
                j = d if way == 0 else a.size - d
                self.prepare(other, j, chunk)
                block = self.part(self.acc, other, j, chunk)
                if k > 0:
                    self.ring[item, way, d].wait_recv()
                    self.add(block, self.ringbuf.at[item, way, d])
                copy = remote(
                    block,
                    self.ringbuf.at[item, way, d - 1],
                    self.rs.at[item, way, d - 1],
                    self.rr.at[item, way, d - 1],
                    a.right if way == 0 else a.left,
                )
                self.ring[item, way, d - 1] = copy
                self.sent.append(copy)

    def finish(self):
        a = self.a
        last = []
        for item, (chunk, other, _, _) in enumerate(self.items):
            self.prepare(other, 0, chunk)
            block = self.part(self.acc, other, 0, chunk)
            for way in range(2):
                self.ring[item, way, 0].wait_recv()
                self.add(block, self.ringbuf.at[item, way, 0])
            if other:
                slot = a.size
                final = remote(block, self.lastbuf, self.cs.at[slot], self.cr.at[slot], a.across)
                self.sent.append(final)
            else:
                last.append((chunk, block))
        for chunk, block in sorted(last, key=lambda entry: -entry[0]):
            if self.both and chunk == 0:
                final.wait_recv()
                self.add(block, self.lastbuf)
            where = rows_at(a.core * self.half + chunk * self.chunk, self.chunk)
            self.o[where] = block[...]
            copy = remote(
                self.o.at[where], self.o.at[where], self.os.at[chunk], self.or_.at[chunk], a.sibling
            )
            self.sent.append(copy)
            last_copy = copy
            self.outs = getattr(self, "outs", []) + [last_copy]
        for copy in self.outs:
            copy.wait_recv()
        for copy in self.sent:
            copy.wait_send()

    @staticmethod
    def scratch(size, both, rows, width, dtype):
        items = 3 if both else 2
        plane = 2 if both else 1
        half, chunk = rows // 2, rows // 4
        dma = pltpu.SemaphoreType.DMA
        few = size if both else 1
        return [
            pltpu.VMEM((plane, size, half, width), dtype),
            pltpu.VMEM((plane, size, half, width), dtype),
            pltpu.VMEM((items, 2, size // 2, chunk, width), dtype),
            pltpu.VMEM((few, chunk, width), dtype),
            pltpu.VMEM((chunk, width), dtype),
            dma((items, 2, size // 2)),
            dma((items, 2, size // 2)),
            dma((few + 1,)),
            dma((few + 1,)),
            dma((plane, size)),
            dma((plane, size)),
            dma((2,)),
            dma((2,)),
            dma((plane, size)),
        ]


def sum_kernel(size, both, p_ref, o_ref, *scratch):
    ring = RingSum(Around(size), both, p_ref, o_ref, *scratch)
    greet(ring.partners())
    ring.start()
    for k in range(size // 2):
        ring.step(k)
    ring.finish()


def ring_sum(p, size, both, ident):
    blocks = (2 if both else 1) * size
    rows, width = p.shape[0] // blocks, p.shape[1]
    return pl.pallas_call(
        functools.partial(sum_kernel, size, both),
        out_shape=jax.ShapeDtypeStruct((rows, width), p.dtype),
        in_specs=[pl.BlockSpec(memory_space=pl.ANY)],
        out_specs=pl.BlockSpec(memory_space=pltpu.VMEM),
        scratch_shapes=RingSum.scratch(size, both, rows, width, p.dtype),
        compiler_params=pltpu.CompilerParams(
            collective_id=ident, has_side_effects=True, vmem_limit_bytes=vmem_bytes
        ),
        name="sum_all" if both else "sum_ctx",
    )(p)


def leave_kernel(
    size, shared, p_ref, g_ref, v_ref, o_ref, go_ref, vo_ref,
    gacc, gmet, vmet, gx_s, gx_r, g_s, g_r, gl, v_s, v_r, *scratch,
):
    a = Around(size)
    ring = RingSum(a, False, p_ref, o_ref, *scratch)
    order = ring.order
    greet(ring.partners() + [a.across] + [a.at(d) for d in order if 1 < d < size - 1])

    swaps = [remote(v_ref, vmet.at[0], v_s.at[0], v_r.at[0], a.across)]

    def swap(slot, device):
        return remote(vo_ref, vmet.at[slot], v_s.at[slot], v_r.at[slot], device)

    crossed, here = {}, {}
    for d in order:
        index = a.index(d)
        crossed[d] = remote(
            g_ref.at[(1 - a.seq) * size + index], gmet.at[d], gx_s.at[d], gx_r.at[d], a.across
        )
        here[d] = pltpu.make_async_copy(g_ref.at[a.seq * size + index], gacc.at[d], gl.at[d])
        here[d].start()
    ring.start()
    sent = {}

    def pass_on(d):
        crossed[d].wait_recv()
        here[d].wait()
        ring.add(gacc.at[d], gmet.at[d])
        if d:
            sent[d] = remote(gacc.at[d], go_ref.at[a.ctx], g_s.at[d], g_r.at[d], a.at(d))
        else:
            go_ref[a.ctx] = gacc[d]

    todo = list(order)
    pair = a.ctx + 1 - 2 * (a.ctx % 2)
    for k in range(size // 2):
        ring.step(k)
        if k == 0:
            swaps[0].wait()
            vo_ref[...] = v_ref[...] + vmet[0]
            swaps = [swap(1, (a.seq, pair, a.core))]
        elif k == 2:
            swaps[0].wait()
            vo_ref[...] += vmet[1]
            swaps = [
                swap(1 + d, (a.seq, lax.rem(a.ctx + 2 * d, size), a.core)) for d in range(1, size // 2)
            ]
        for _ in range(2):
            pass_on(todo.pop(0))
    ring.finish()
    while todo:
        pass_on(todo.pop(0))
    for copy in swaps:
        copy.wait()
    for d in range(1, size // 2):
        vo_ref[...] += vmet[1 + d]
    head = pl.ds(0, shared)
    last = 1 + size // 2
    copy = remote(vo_ref.at[head], vmet.at[last, head], v_s.at[last], v_r.at[last], a.sibling)
    copy.wait()
    vo_ref[head] += vmet[last, head]
    for copy in crossed.values():
        copy.wait_send()
    for copy in sent.values():
        copy.wait()


def leave(p, g, small, shared, size, ident):
    rows, width = p.shape[0] // size, p.shape[1]
    dma = pltpu.SemaphoreType.DMA
    hbm = pl.BlockSpec(memory_space=pl.ANY)
    vmem = pl.BlockSpec(memory_space=pltpu.VMEM)
    block = (size,) + g.shape[1:]
    steps = 2 + size // 2
    return pl.pallas_call(
        functools.partial(leave_kernel, size, shared),
        out_shape=(
            jax.ShapeDtypeStruct((rows, width), p.dtype),
            jax.ShapeDtypeStruct(block, g.dtype),
            jax.ShapeDtypeStruct(small.shape, small.dtype),
        ),
        in_specs=[hbm, hbm, vmem],
        out_specs=(vmem, vmem, vmem),
        scratch_shapes=[
            pltpu.VMEM(block, g.dtype),
            pltpu.VMEM(block, g.dtype),
            pltpu.VMEM((steps,) + small.shape, small.dtype),
            dma((size,)),
            dma((size,)),
            dma((size,)),
            dma((size,)),
            dma((size,)),
            dma((steps,)),
            dma((steps,)),
        ]
        + RingSum.scratch(size, False, rows, width, p.dtype),
        compiler_params=pltpu.CompilerParams(
            collective_id=ident, has_side_effects=True, vmem_limit_bytes=vmem_bytes
        ),
        name="leave_rows_and_weights",
    )(p, g, small)


def plain_enter(x, w):
    rows = lax.all_gather(x, "ctx", axis=0, tiled=True)
    mine = lax.all_to_all(w, "ctx", split_axis=0, concat_axis=0, tiled=True)
    return rows, lax.all_gather(mine, "seq", axis=0, tiled=True)


def plain_sum(p, axes):
    part = lax.psum_scatter(p, axes, scatter_dimension=0, tiled=True)
    return lax.psum(part, "tp")


def plain_leave(p, g, small, shared):
    kept = lax.psum_scatter(g, "seq", scatter_dimension=0, tiled=True)
    owned = lax.all_to_all(kept, "ctx", split_axis=0, concat_axis=0, tiled=True)
    small = jnp.concatenate([lax.psum(small[:shared], "tp"), small[shared:]])
    return plain_sum(p, "ctx"), owned, lax.psum(small, ("seq", "ctx"))


def expert_kernel(
    units, model, lead_ref, x_ref, dy_ref, wt_ref, bias_ref, wd_ref, bd_ref, pick_ref, place_ref,
    out_ref, back_ref, act_ref, dgu_ref, gbias_ref, dbias_ref,
):
    step = pl.program_id(0)
    tail = model // 128 * 128
    rows = x_ref.shape[0]
    x = x_ref[:, :model]
    dy = dy_ref[...]
    ends = x_ref[:, tail:]
    gate_row = across(pick_ref[...], ends)[:1]
    gate_col = across(ends, pick_ref[...])[:, :1]

    gate = clamp_limit * jnp.tanh((across(wt_ref[:units], x) + bias_ref[:units]) / clamp_limit)
    up = clamp_limit * jnp.tanh((across(wt_ref[units:], x) + bias_ref[units:]) / clamp_limit)
    squash = jax.nn.sigmoid(glu_alpha * gate)
    swish = gate * squash
    act = (up + 1.0) * swish
    out = down(act.astype(bf16), wd_ref[...]) + lead_ref[0, 0] * bd_ref[...]
    out_ref[...] = (gate_col * out).astype(bf16)

    act_grad = across(wd_ref[...], dy)
    high = bd_ref[...].astype(bf16)
    low = (bd_ref[...] - high.astype(f32)).astype(bf16)
    bias_dot = across(jnp.concatenate([high, low] + [jnp.zeros_like(high)] * 14, axis=0), dy)
    gate_grad = jnp.sum(act * act_grad, axis=0, keepdims=True) + lead_ref[0, 0] * (
        bias_dot[0:1] + bias_dot[1:2]
    )
    gate_grad = jnp.where(gate_row > 0, gate_grad, 0.0)
    act_grad = act_grad * gate_row
    slope = 1.0 - (gate / clamp_limit) * (gate / clamp_limit)
    dgate = (
        act_grad * (up + 1.0) * (squash + glu_alpha * swish * (1.0 - squash)) * slope
    ).astype(bf16)
    dup = (act_grad * swish * (1.0 - (up / clamp_limit) * (up / clamp_limit))).astype(bf16)
    act_ref[...] = (act * gate_row).astype(bf16)
    dgu_ref[:units] = dgate
    dgu_ref[units:] = dup

    back = down(dgate, wt_ref[:units]) + down(dup, wt_ref[units:])
    back_ref[:, :model] = back.astype(bf16)
    top = gate_grad.astype(bf16)
    rest = (gate_grad - top.astype(f32)).astype(bf16)
    sent = jnp.concatenate([top, rest] + [jnp.zeros_like(top)] * 14, axis=0)
    ends_out = down(sent, place_ref[...]).astype(bf16)
    back_ref[:, model:] = ends_out[:, model - tail :]

    @pl.when(step == 0)
    def _():
        gbias_ref[...] = jnp.zeros_like(gbias_ref)
        dbias_ref[...] = jnp.zeros_like(dbias_ref)

    gbias_ref[:units] += jnp.sum(dgate.astype(f32), axis=1, keepdims=True)
    gbias_ref[units:] += jnp.sum(dup.astype(f32), axis=1, keepdims=True)
    gate_high = gate_row.astype(bf16)
    gate_low = (gate_row - gate_high.astype(f32)).astype(bf16)
    gates = jnp.concatenate([gate_high, gate_low] + [jnp.zeros_like(gate_high)] * 14, axis=0)
    sums = jnp.dot(gates, dy, preferred_element_type=f32)
    dbias_ref[...] += sums[0:1] + sums[1:2]


def expert_rows(lead, x, dy, wt, bias, wd, bd, pick, place):
    count, wide = x.shape
    model = dy.shape[1]
    units = wd.shape[0]
    rows = min(256, count)
    tail = model // 128 * 128
    back_wide = tail + place.shape[1]
    row = lambda i: (i, 0)
    col = lambda i: (0, i)
    fixed = lambda i: (0, 0)
    whole = lambda v: pl.BlockSpec(v.shape, fixed)
    return pl.pallas_call(
        functools.partial(expert_kernel, units, model),
        grid=(count // rows,),
        out_shape=(
            jax.ShapeDtypeStruct((count, model), bf16),
            jax.ShapeDtypeStruct((count, back_wide), bf16),
            jax.ShapeDtypeStruct((units, count), bf16),
            jax.ShapeDtypeStruct((2 * units, count), bf16),
            jax.ShapeDtypeStruct((2 * units, 1), f32),
            jax.ShapeDtypeStruct((1, model), f32),
        ),
        in_specs=[
            pl.BlockSpec(memory_space=pltpu.SMEM),
            pl.BlockSpec((rows, wide), row),
            pl.BlockSpec((rows, model), row),
            whole(wt),
            whole(bias),
            whole(wd),
            whole(bd),
            whole(pick),
            whole(place),
        ],
        out_specs=(
            pl.BlockSpec((rows, model), row),
            pl.BlockSpec((rows, back_wide), row),
            pl.BlockSpec((units, rows), col),
            pl.BlockSpec((2 * units, rows), col),
            pl.BlockSpec((2 * units, 1), fixed),
            pl.BlockSpec((1, model), fixed),
        ),
        compiler_params=pltpu.CompilerParams(vmem_limit_bytes=vmem_bytes),
        name="expert_rows",
    )(lead, x, dy, wt, bias, wd, bd, pick, place)


def unit_order(size):
    order = [size // 2]
    for d in range(size // 2 - 1, 0, -1):
        order += [d, size - d]
    return order + [0]


def unit_slots(size):
    return {j: slot for slot, j in enumerate(unit_order(size))}


def expert_in_kernel(
    size, units, model, wide,
    x_ref, wt_ref, wd_ref, bias_ref, extra_ref, pick_ref,
    x_all, act_all, dgu_all, dg_ref, gbias_ref,
    xbuf, wt, wd, act_buf, dgu_buf,
    load_s, ring_s, ring_r, cross_s, cross_r, core_s, core_r, keep_s,
):
    a = Around(size)
    rows = x_ref.shape[0]
    half, chunk = rows // 2, rows // 4
    far, near = size // 2, size - 1 - size // 2
    items = [(1, 0, far, near), (0, 0, near, far), (0, 1, far, near)]
    slot_of = unit_slots(size)
    tail = model // 128 * 128

    loads = [
        pltpu.make_async_copy(wt_ref, wt, load_s.at[0]),
        pltpu.make_async_copy(wd_ref, wd.at[pl.ds(0, units)], load_s.at[1]),
    ]
    for copy in loads:
        copy.start()
    wd[units:] = extra_ref[...]
    gbias_ref[...] = jnp.zeros_like(gbias_ref)
    greet([a.right, a.left, a.sibling, a.across])

    def spot(j, other, core, piece):
        return xbuf.at[slot_of[j], pl.ds(other * rows + core * half + piece * chunk, chunk)]

    sent, ring, crossed, shared = [], {}, {}, {}

    def hop(item, way, k, src):
        piece, other, _, _ = items[item]
        j = size - (k + 1) if way == 0 else k + 1
        copy = remote(
            src, spot(j, other, 0, piece), ring_s.at[item, way, k], ring_r.at[item, way, k],
            a.right if way == 0 else a.left,
        )
        ring[item, way, k] = copy
        sent.append(copy)

    def cross(j, piece, src):
        at = slot_of[j] if piece else size
        copy = remote(src, spot(j, 1, 0, piece), cross_s.at[at], cross_r.at[at], a.across)
        crossed[j, piece] = copy
        sent.append(copy)

    def share(j, other, piece):
        at = (slot_of[j], other, piece)
        copy = remote(
            spot(j, other, 0, piece), spot(j, other, 1, piece), core_s.at[at], core_r.at[at], a.sibling
        )
        shared[j, other, piece] = copy
        sent.append(copy)

    def own(core, piece, count):
        return x_ref.at[rows_at(core * half + piece * chunk, count)]

    mine = [
        pltpu.make_async_copy(
            own(a.core if here == 0 else 1 - a.core, 0, half),
            xbuf.at[slot_of[0], pl.ds(here * half, half)],
            load_s.at[2 + here],
        )
        for here in range(2)
    ]
    for copy in mine:
        copy.start()
    cross(0, 0, own(a.core, 0, chunk))
    for item in range(2):
        for way in range(2):
            hop(item, way, 0, own(a.core, items[item][0], chunk))
    cross(0, 1, own(a.core, 1, chunk))

    def unit(slot, carry):
        x = xbuf[slot, :, :model]
        dy = xbuf[slot, :, wide : wide + model]
        ends = xbuf[slot, :, tail:wide]
        columns = pl.ds(pl.multiple_of(slot * 2 * rows, 2 * rows), 2 * rows)
        gate_row = across(pick_ref[...], ends)[:1]
        gate = clamp_limit * jnp.tanh((across(wt[:units], x) + bias_ref[:units]) / clamp_limit)
        up = clamp_limit * jnp.tanh((across(wt[units:], x) + bias_ref[units:]) / clamp_limit)
        squash = jax.nn.sigmoid(glu_alpha * gate)
        swish = gate * squash
        act = (up + 1.0) * swish
        act_grad = across(wd[...], dy)
        bias_dot = act_grad[units : units + 1] + act_grad[units + 1 : units + 2]
        act_grad = act_grad[:units]
        gate_grad = jnp.sum(act * act_grad, axis=0, keepdims=True) + bias_dot
        gate_grad = jnp.where(gate_row > 0, gate_grad, 0.0)
        act_grad = act_grad * gate_row
        slope = 1.0 - (gate / clamp_limit) * (gate / clamp_limit)
        dgate = (
            act_grad * (up + 1.0) * (squash + glu_alpha * swish * (1.0 - squash)) * slope
        ).astype(bf16)
        dup = (act_grad * swish * (1.0 - (up / clamp_limit) * (up / clamp_limit))).astype(bf16)
        dgu_buf[:units, columns] = dgate
        dgu_buf[units:, columns] = dup
        gbias_ref[:units] += jnp.sum(dgate.astype(f32), axis=1, keepdims=True)
        gbias_ref[units:] += jnp.sum(dup.astype(f32), axis=1, keepdims=True)
        high = gate_row.astype(bf16)
        low = (gate_row - high.astype(f32)).astype(bf16)
        act_buf[:units, columns] = (act * gate_row).astype(bf16)
        act_buf[units:, columns] = jnp.concatenate([high, high, low] + [jnp.zeros_like(high)] * 13, axis=0)
        top = gate_grad.astype(bf16)
        rest = (gate_grad - top.astype(f32)).astype(bf16)
        dg_ref[:, columns] = jnp.concatenate([top, rest] + [jnp.zeros_like(top)] * 14, axis=0)
        return carry

    kept = []

    def compute(js):
        for j in js:
            if j == 0:
                for copy in mine:
                    copy.wait()
            else:
                crossed[j, 1].wait_recv()
                share(j, 1, 1)
            for key in [(j, 0, 0), (j, 0, 1), (j, 1, 0), (j, 1, 1)]:
                if key in shared:
                    shared[key].wait_recv()
        slots = [slot_of[j] for j in js]
        lax.fori_loop(slots[0], slots[-1] + 1, unit, 0)
        for slot in slots:
            columns = pl.ds(slot * 2 * rows, 2 * rows)
            for at, (src, dst) in enumerate(
                (
                    (xbuf.at[slot], x_all.at[slot]),
                    (act_buf.at[:, columns], act_all.at[:, columns]),
                    (dgu_buf.at[:, columns], dgu_all.at[:, columns]),
                )
            ):
                copy = pltpu.make_async_copy(src, dst, keep_s.at[at, slot])
                copy.start()
                kept.append(copy)

    crossed[0, 0].wait_recv()
    for way in range(2):
        hop(2, way, 0, spot(0, 1, 0, 0))
    share(0, 1, 0)
    crossed[0, 1].wait_recv()
    share(0, 1, 1)
    for copy in loads:
        copy.wait()
    ready = [0]
    for k in range(size // 2):
        compute(ready)
        for item, (piece, other, right, left) in enumerate(items):
            for way, hops in ((0, right), (1, left)):
                if k >= hops:
                    continue
                ring[item, way, k].wait_recv()
                j = size - (k + 1) if way == 0 else k + 1
                if k + 1 < hops:
                    hop(item, way, k + 1, spot(j, other, 0, piece))
                if item == 0:
                    cross(j, 1, spot(j, 0, 0, 1))
                share(j, other, piece)
        ready = [k + 1] if 2 * (k + 1) == size else [k + 1, size - (k + 1)]
    compute(ready)
    for copy in sent:
        copy.wait_send()
    for copy in kept:
        copy.wait()


def expert_in(x, wt, wd, bias, extra, pick, model, wide, size, ident):
    rows, width = x.shape
    units = wd.shape[0]
    deep = units + extra.shape[0]
    count = 2 * size * rows
    dma = pltpu.SemaphoreType.DMA
    hbm = pl.BlockSpec(memory_space=pl.ANY)
    vmem = pl.BlockSpec(memory_space=pltpu.VMEM)
    return pl.pallas_call(
        functools.partial(expert_in_kernel, size, units, model, wide),
        out_shape=(
            jax.ShapeDtypeStruct((size, 2 * rows, width), bf16),
            jax.ShapeDtypeStruct((deep, count), bf16),
            jax.ShapeDtypeStruct((2 * units, count), bf16),
            jax.ShapeDtypeStruct((16, count), bf16),
            jax.ShapeDtypeStruct((2 * units, 1), f32),
        ),
        in_specs=[hbm, hbm, hbm, vmem, vmem, vmem],
        out_specs=(hbm, hbm, hbm, vmem, vmem),
        scratch_shapes=[
            pltpu.VMEM((size, 2 * rows, width), bf16),
            pltpu.VMEM((2 * units, model), bf16),
            pltpu.VMEM((deep, model), bf16),
            pltpu.VMEM((deep, count), bf16),
            pltpu.VMEM((2 * units, count), bf16),
            dma((4,)),
            dma((3, 2, size // 2)),
            dma((3, 2, size // 2)),
            dma((size + 1,)),
            dma((size + 1,)),
            dma((size, 2, 2)),
            dma((size, 2, 2)),
            dma((3, size)),
        ],
        compiler_params=pltpu.CompilerParams(
            collective_id=ident, has_side_effects=True, vmem_limit_bytes=vmem_most
        ),
        name="expert_in",
    )(x, wt, wd, bias, extra, pick)


def expert_out_kernel(
    size, rows, units, model, start, tiles, more, *refs,
):
    if more:
        lhs_ref, w_ref, x_ref, dg_ref, place_ref, o_ref, grad_ref, *refs = refs
    else:
        lhs_ref, w_ref, x_ref, extra_ref, o_ref, grad_ref, grad_extra, *refs = refs
    (
        lhs, w, x, acc, own, out, ringbuf, crossbuf, lastbuf, tile,
        load_s, ring_s, ring_r, cross_s, cross_r, core_s, core_r, out_s, out_r, tile_s,
    ) = refs
    a = Around(size)
    half, chunk = rows // 2, rows // 4
    far, near = size // 2, size - 1 - size // 2
    items = [(0, 1, far, near), (0, 0, near, far), (1, 0, far, near)]
    slot_of = unit_slots(size)
    tail = model // 128 * 128
    step_rows = units // tiles

    loads = [
        pltpu.make_async_copy(w_ref, w.at[pl.ds(0, units)], load_s.at[0]),
        pltpu.make_async_copy(lhs_ref, lhs, load_s.at[1]),
        pltpu.make_async_copy(
            x_ref.at[:, :, pl.ds(start, x.shape[2])], x, load_s.at[2]
        ),
    ]
    for copy in loads:
        copy.start()
    if not more:
        w[units:] = extra_ref[...]
    greet([a.right, a.left, a.sibling, a.across])
    for copy in loads[:2]:
        copy.wait()

    def handed(slot, other):
        return pltpu.make_async_remote_copy(
            src_ref=out.at[slot % 2, other],
            dst_ref=acc.at[other, slot],
            send_sem=core_s.at[other, slot],
            recv_sem=core_r.at[other, slot],
            device_id=a.sibling,
            device_id_type=pl.DeviceIdType.MESH,
        )

    def over(slot):
        return pltpu.make_async_remote_copy(
            src_ref=acc.at[1, slot, pl.ds(chunk, chunk)],
            dst_ref=crossbuf.at[slot],
            send_sem=cross_s.at[slot],
            recv_sem=cross_r.at[slot],
            device_id=a.across,
            device_id_type=pl.DeviceIdType.MESH,
        )

    def add(into, other):
        into[...] = (into[...].astype(f32) + other[...].astype(f32)).astype(bf16)

    def settle(slot):
        for other in range(2):
            handed(slot, other).wait_recv()
            add(acc.at[other, slot], own.at[slot % 2, other])
        over(slot).start()

    def produce(slot, carry):
        @pl.when(slot >= 2)
        def _():
            for other in range(2):
                handed(slot - 2, other).wait_send()

        columns = pl.ds(pl.multiple_of(slot * 2 * rows, 2 * rows), 2 * rows)
        y = down(lhs[:, columns], w[...])
        for other in range(2):
            for place, into in ((0, own), (half, out)):
                part = y[other * rows + place : other * rows + place + half]
                into[slot % 2, other, :, :model] = part.astype(bf16)
        if more:
            ends = down(dg_ref[:, columns], place_ref[...])[:, model - tail :].astype(bf16)
            for other in range(2):
                for place, into in ((0, own), (half, out)):
                    part = ends[other * rows + place : other * rows + place + half]
                    into[slot % 2, other, :, model:] = part
        for other in range(2):
            handed(slot, other).start()

        @pl.when(slot >= 1)
        def _():
            settle(slot - 1)

        return carry

    def tile_copy(i):
        return pltpu.make_async_copy(
            tile.at[i % 2], grad_ref.at[pl.ds(pl.multiple_of(i * step_rows, 16), step_rows)], tile_s.at[i % 2]
        )

    def weight_grad(i, carry):
        @pl.when(i >= 2)
        def _():
            tile_copy(i - 2).wait()

        left = lhs[pl.ds(pl.multiple_of(i * step_rows, 16), step_rows)]
        total = None
        for at in range(size):
            piece = jnp.dot(
                left[:, at * 2 * rows : (at + 1) * 2 * rows], x[at, :, :model], preferred_element_type=f32
            )
            total = piece if total is None else total + piece
        tile[i % 2] = total
        tile_copy(i).start()
        return carry

    ring, sent = {}, []

    def part(other, j, piece):
        return acc.at[other, slot_of[j], pl.ds(piece * chunk, chunk)]

    joined = set()

    def join(j):
        if j not in joined:
            joined.add(j)
            over(slot_of[j]).wait_recv()
            add(part(0, j, 1), crossbuf.at[slot_of[j]])

    def step(k):
        for item, (piece, other, right, left) in enumerate(items):
            for way, hops in ((0, right), (1, left)):
                d = hops - k
                if d < 1:
                    continue
                j = d if way == 0 else size - d
                if piece == 1:
                    join(j)
                block = part(other, j, piece)
                if k > 0:
                    ring[item, way, d].wait_recv()
                    add(block, ringbuf.at[item, way, d])
                copy = remote(
                    block, ringbuf.at[item, way, d - 1], ring_s.at[item, way, d - 1],
                    ring_r.at[item, way, d - 1], a.right if way == 0 else a.left,
                )
                ring[item, way, d - 1] = copy
                sent.append(copy)

    made, graded = [0], [0]

    def make(upto):
        lax.fori_loop(made[0], upto, produce, 0)
        made[0] = upto

    def grade(count):
        upto = min(tiles, graded[0] + count)
        if upto > graded[0]:
            lax.fori_loop(graded[0], upto, weight_grad, 0)
            graded[0] = upto

    steps = size // 2
    per = -(-tiles // steps)
    make(4)
    step(0)
    make(min(6, size))
    loads[2].wait()
    for k in range(1, steps):
        upto = min(size, 4 + 2 * (k + 1))
        if k > 1 and made[0] < upto:
            make(upto)
        if k == steps - 1:
            settle(size - 1)
        if k == 1 and steps > 2:
            grade(per)
            step(k)
            make(min(size, 8))
            continue
        grade(per)
        step(k)
    grade(tiles)

    last = []
    for item, (piece, other, _, _) in enumerate(items):
        if piece == 1:
            join(0)
        block = part(other, 0, piece)
        for way in range(2):
            ring[item, way, 0].wait_recv()
            add(block, ringbuf.at[item, way, 0])
        if other:
            final = remote(block, lastbuf, cross_s.at[size], cross_r.at[size], a.across)
            sent.append(final)
        else:
            last.append((piece, block))
    outs = []
    for piece, block in sorted(last, key=lambda entry: -entry[0]):
        if piece == 0:
            final.wait_recv()
            add(block, lastbuf)
        where = o_ref.at[rows_at(a.core * half + piece * chunk, chunk)]
        where[...] = block[...]
        outs.append(remote(where, where, out_s.at[piece], out_r.at[piece], a.sibling))
    if not more:
        left = lhs[pl.ds(units, lhs.shape[0] - units)]
        total = None
        for at in range(size):
            piece = jnp.dot(
                left[:, at * 2 * rows : (at + 1) * 2 * rows], x[at, :, :model], preferred_element_type=f32
            )
            total = piece if total is None else total + piece
        grad_extra[...] = total
    for copy in outs:
        copy.wait()
    for copy in sent:
        copy.wait_send()
    for slot in range(size):
        over(slot).wait_send()
    for slot in range(size - 2, size):
        for other in range(2):
            handed(slot, other).wait_send()
    for i in range(max(0, tiles - 2), tiles):
        tile_copy(i).wait()


def expert_out(lhs, w, x, start, tiles, size, ident, dg=None, place=None, extra=None):
    units, model = w.shape
    rows = x.shape[1] // 2
    half, chunk = rows // 2, rows // 4
    more = dg is not None
    padded = -(-model // 128) * 128
    width = model // 128 * 128 + place.shape[1] if more else model
    dma = pltpu.SemaphoreType.DMA
    hbm = pl.BlockSpec(memory_space=pl.ANY)
    vmem = pl.BlockSpec(memory_space=pltpu.VMEM)
    shapes = [
        jax.ShapeDtypeStruct((rows, width), bf16),
        jax.ShapeDtypeStruct((units, model), f32),
    ]
    if not more:
        shapes.append(jax.ShapeDtypeStruct((extra.shape[0], model), f32))
    return pl.pallas_call(
        functools.partial(expert_out_kernel, size, rows, units, model, start, tiles, more),
        out_shape=shapes,
        in_specs=[hbm, hbm, hbm] + [vmem] * (2 if more else 1),
        out_specs=[vmem, hbm] + ([] if more else [vmem]),
        scratch_shapes=[
            pltpu.VMEM(lhs.shape, bf16),
            pltpu.VMEM((lhs.shape[0], model), bf16),
            pltpu.VMEM((size, 2 * rows, padded), bf16),
            pltpu.VMEM((2, size, half, width), bf16),
            pltpu.VMEM((2, 2, half, width), bf16),
            pltpu.VMEM((2, 2, half, width), bf16),
            pltpu.VMEM((3, 2, size // 2, chunk, width), bf16),
            pltpu.VMEM((size, chunk, width), bf16),
            pltpu.VMEM((chunk, width), bf16),
            pltpu.VMEM((2, units // tiles, model), f32),
            dma((3,)),
            dma((3, 2, size // 2)),
            dma((3, 2, size // 2)),
            dma((size + 1,)),
            dma((size + 1,)),
            dma((2, size)),
            dma((2, size)),
            dma((2,)),
            dma((2,)),
            dma((2,)),
        ],
        compiler_params=pltpu.CompilerParams(
            collective_id=ident, has_side_effects=True, vmem_limit_bytes=vmem_most
        ),
        name="expert_back" if more else "expert_out",
    )(lhs, w, x, *((dg, place) if more else (extra,)))


def turn(x, cosine, sine):
    half = HEAD_DIMENSION // 2
    width = x.shape[-1]
    if width % 128:
        starts = [start for at in range(0, width, 2 * half) for start in (at + half, at)]
        swapped = jnp.concatenate([x[:, start : start + half] for start in starts], axis=1)
    else:
        lane = lax.broadcasted_iota(jnp.int32, x.shape, 1)
        swapped = jnp.where(
            lane % HEAD_DIMENSION < half, pltpu.roll(x, width - half, 1), pltpu.roll(x, half, 1)
        )
    return x * cosine + swapped * sine


def spread(table, width):
    pieces = [table] * (width // 128) + ([table[:, : width % 128]] if width % 128 else [])
    return jnp.concatenate(pieces, axis=1) if len(pieces) > 1 else pieces[0]


def project_kernel(heads, x_ref, w_ref, b_ref, cos_ref, sin_ref, q_ref, k_ref, v_ref):
    width = heads * HEAD_DIMENSION
    y = jnp.dot(x_ref[...], w_ref[...], preferred_element_type=f32) + b_ref[...]
    cosine, sine = cos_ref[...], sin_ref[...]
    pad = 128
    q_ref[...] = turn(y[:, :width], spread(cosine, width), spread(sine, width)).astype(bf16)
    kv = y[:, width : width + pad]
    k_ref[...] = turn(kv, cosine, sine)[:, :HEAD_DIMENSION].astype(bf16)
    v_ref[...] = kv[:, HEAD_DIMENSION:].astype(bf16)


def project(x, w, bias, cosine, sine, heads):
    length, model = x.shape
    rows = min(256, length)
    width = heads * HEAD_DIMENSION
    row = lambda i: (i, 0)
    fixed = lambda i: (0, 0)
    return pl.pallas_call(
        functools.partial(project_kernel, heads),
        grid=(length // rows,),
        out_shape=(
            jax.ShapeDtypeStruct((length, width), bf16),
            jax.ShapeDtypeStruct((length, HEAD_DIMENSION), bf16),
            jax.ShapeDtypeStruct((length, HEAD_DIMENSION), bf16),
        ),
        in_specs=[
            pl.BlockSpec((rows, model), row),
            pl.BlockSpec(w.shape, fixed),
            pl.BlockSpec(bias.shape, fixed),
            pl.BlockSpec((rows, 128), row),
            pl.BlockSpec((rows, 128), row),
        ],
        out_specs=(
            pl.BlockSpec((rows, width), row),
            pl.BlockSpec((rows, HEAD_DIMENSION), row),
            pl.BlockSpec((rows, HEAD_DIMENSION), row),
        ),
        compiler_params=pltpu.CompilerParams(vmem_limit_bytes=vmem_bytes),
        name="project_rows",
    )(x, w, bias, cosine, sine)


def each_reach(block, rows, length, run):
    classes = min(4, length // rows)
    per = length // rows // classes
    for level in range(classes):
        pl.when(block // per == level)(functools.partial(run, (level + 1) * per * rows))


def attend_kernel(heads, length, sink_ref, q_ref, k_ref, v_ref, w_ref, o_ref, low_ref, lse_ref, p_ref):
    rows = q_ref.shape[0]
    block = pl.program_id(0)
    scale = 1.0 / math.sqrt(HEAD_DIMENSION)

    def run(reach):
        keys, values = k_ref[:reach], v_ref[:reach]
        row = block * rows + lax.broadcasted_iota(jnp.int32, (rows, reach), 0)
        allowed = lax.broadcasted_iota(jnp.int32, (rows, reach), 1) <= row
        outs, totals = [], []
        for head in range(heads):
            query = q_ref[:, head * HEAD_DIMENSION : (head + 1) * HEAD_DIMENSION]
            scores = jnp.where(allowed, across(query, keys) * scale, masked_score)
            sink = sink_ref[0, head]
            top = jnp.maximum(jnp.max(scores, axis=1, keepdims=True), sink)
            weights = jnp.exp(scores - top)
            total = jnp.sum(weights, axis=1, keepdims=True) + jnp.exp(sink - top)
            mixed = jnp.dot(weights.astype(bf16), values, preferred_element_type=f32)
            outs.append(mixed / total)
            totals.append(top + jnp.log(total))
        joined = jnp.concatenate(outs, axis=1)
        o_ref[...] = joined
        joined_low = joined.astype(bf16)
        low_ref[...] = joined_low
        p_ref[...] = across(joined_low, w_ref[...]).astype(bf16)
        lse_ref[...] = jnp.concatenate(totals, axis=1)

    each_reach(block, rows, length, run)


def attend(sinks, q, k, v, w):
    length, width = q.shape
    model = w.shape[0]
    heads = width // HEAD_DIMENSION
    rows = min(256, length)
    row = lambda i: (i, 0)
    fixed = lambda i: (0, 0)
    return pl.pallas_call(
        functools.partial(attend_kernel, heads, length),
        grid=(length // rows,),
        out_shape=(
            jax.ShapeDtypeStruct((length, width), f32),
            jax.ShapeDtypeStruct((length, width), bf16),
            jax.ShapeDtypeStruct((length, heads), f32),
            jax.ShapeDtypeStruct((length, model), bf16),
        ),
        in_specs=[
            pl.BlockSpec(memory_space=pltpu.SMEM),
            pl.BlockSpec((rows, width), row),
            pl.BlockSpec(k.shape, fixed),
            pl.BlockSpec(v.shape, fixed),
            pl.BlockSpec(w.shape, fixed),
        ],
        out_specs=(
            pl.BlockSpec((rows, width), row),
            pl.BlockSpec((rows, width), row),
            pl.BlockSpec((rows, heads), row),
            pl.BlockSpec((rows, model), row),
        ),
        compiler_params=pltpu.CompilerParams(vmem_limit_bytes=vmem_bytes),
        name="attend_rows",
    )(sinks, q, k, v, w)


def spread_kernel(x_ref, w_ref, o_ref):
    o_ref[...] = across(x_ref[...], w_ref[...]).astype(o_ref.dtype)


def spread_rows(x, w):
    count, width = x.shape
    rows = min(256, count)
    return pl.pallas_call(
        spread_kernel,
        grid=(count // rows,),
        out_shape=jax.ShapeDtypeStruct((count, w.shape[0]), bf16),
        in_specs=[
            pl.BlockSpec((rows, width), lambda i: (i, 0)),
            pl.BlockSpec(w.shape, lambda i: (0, 0)),
        ],
        out_specs=pl.BlockSpec((rows, w.shape[0]), lambda i: (i, 0)),
        compiler_params=pltpu.CompilerParams(vmem_limit_bytes=vmem_bytes),
        name="spread_rows",
    )(x, w)


def attend_back_kernel(
    heads, length, sink_ref, q_ref, k_ref, v_ref, o_ref, lse_ref, do_ref, cos_ref, sin_ref,
    kcos_ref, ksin_ref, dq_ref, dkv_ref, dsink_ref, dk_acc, dv_acc, sink_acc,
):
    rows = q_ref.shape[0]
    block = pl.program_id(0)
    scale = 1.0 / math.sqrt(HEAD_DIMENSION)

    @pl.when(block == 0)
    def _():
        dk_acc[...] = jnp.zeros_like(dk_acc)
        dv_acc[...] = jnp.zeros_like(dv_acc)
        sink_acc[...] = jnp.zeros_like(sink_acc)

    def run(reach):
        keys, values = k_ref[:reach], v_ref[:reach]
        row = block * rows + lax.broadcasted_iota(jnp.int32, (rows, reach), 0)
        allowed = lax.broadcasted_iota(jnp.int32, (rows, reach), 1) <= row
        parts, sink_parts = [], []
        key_sum = jnp.zeros((reach, HEAD_DIMENSION), f32)
        value_sum = jnp.zeros((reach, HEAD_DIMENSION), f32)
        for head in range(heads):
            span = slice(head * HEAD_DIMENSION, (head + 1) * HEAD_DIMENSION)
            query, grad = q_ref[:, span], do_ref[:, span]
            lse = lse_ref[:, head : head + 1]
            delta = jnp.sum(grad.astype(f32) * o_ref[:, span], axis=1, keepdims=True)
            scores = jnp.where(allowed, across(query, keys) * scale, masked_score)
            probs = jnp.exp(scores - lse)
            value_sum = value_sum + down(probs.astype(bf16), grad)
            score_grad = (probs * (across(grad, values) - delta)).astype(bf16)
            parts.append(jnp.dot(score_grad, keys, preferred_element_type=f32) * scale)
            key_sum = key_sum + down(score_grad, query)
            share = jnp.exp(sink_ref[0, head] - lse) * delta
            sink_parts.append(jnp.sum(share, axis=0, keepdims=True))
        dq = jnp.concatenate(parts, axis=1)
        wide = dq.shape[1]
        dq_ref[...] = turn(dq, spread(cos_ref[...], wide), -spread(sin_ref[...], wide)).astype(bf16)
        dk_acc[:reach] += key_sum * scale
        dv_acc[:reach] += value_sum
        sink_acc[...] -= jnp.concatenate(sink_parts, axis=1)

    each_reach(block, rows, length, run)

    @pl.when(block == pl.num_programs(0) - 1)
    def _():
        both = jnp.concatenate([dk_acc[...], dv_acc[...]], axis=1)
        turned = turn(both, kcos_ref[...], -ksin_ref[...])
        lane = lax.broadcasted_iota(jnp.int32, both.shape, 1)
        dkv_ref[...] = jnp.where(lane < HEAD_DIMENSION, turned, both).astype(bf16)
        dsink_ref[...] = sink_acc[...]


def attend_back(sinks, q, k, v, o, lse, do, cosine, sine):
    length, width = q.shape
    heads = width // HEAD_DIMENSION
    rows = min(256, length)
    row = lambda i: (i, 0)
    fixed = lambda i: (0, 0)
    return pl.pallas_call(
        functools.partial(attend_back_kernel, heads, length),
        grid=(length // rows,),
        out_shape=(
            jax.ShapeDtypeStruct((length, width), bf16),
            jax.ShapeDtypeStruct((length, 2 * HEAD_DIMENSION), bf16),
            jax.ShapeDtypeStruct((1, heads), f32),
        ),
        in_specs=[
            pl.BlockSpec(memory_space=pltpu.SMEM),
            pl.BlockSpec((rows, width), row),
            pl.BlockSpec(k.shape, fixed),
            pl.BlockSpec(v.shape, fixed),
            pl.BlockSpec((rows, width), row),
            pl.BlockSpec((rows, heads), row),
            pl.BlockSpec((rows, width), row),
            pl.BlockSpec((rows, 128), row),
            pl.BlockSpec((rows, 128), row),
            pl.BlockSpec((length, 128), fixed),
            pl.BlockSpec((length, 128), fixed),
        ],
        out_specs=(
            pl.BlockSpec((rows, width), row),
            pl.BlockSpec((length, 2 * HEAD_DIMENSION), fixed),
            pl.BlockSpec((1, heads), fixed),
        ),
        scratch_shapes=[
            pltpu.VMEM((length, HEAD_DIMENSION), f32),
            pltpu.VMEM((length, HEAD_DIMENSION), f32),
            pltpu.VMEM((1, heads), f32),
        ],
        compiler_params=pltpu.CompilerParams(vmem_limit_bytes=vmem_bytes),
        name="attend_rows_back",
    )(sinks, q, k, v, o, lse, do, cosine, sine, cosine, sine)


def rms_norm(row_block, gain_vec):
    return (
        row_block
        * lax.rsqrt(jnp.mean(row_block * row_block, axis=-1, keepdims=True) + rms_eps)
        * gain_vec
    )


def rotary(length):
    half_size = HEAD_DIMENSION // 2
    frequency = rope_base ** (-2.0 * jnp.arange(half_size, dtype=f32) / HEAD_DIMENSION)
    angles = jnp.arange(length, dtype=f32)[:, None] * frequency[None, :]
    cosine, sine = jnp.cos(angles), jnp.sin(angles)
    return (
        jnp.concatenate([cosine] * 4, axis=1),
        jnp.concatenate([-sine, sine, -sine, sine], axis=1),
    )


def project_grad(left, right):
    return lax.dot_general(left, right, (((0,), (0,)), ((), ())), preferred_element_type=f32)


def on_device(
    tokens,
    gain_attn,
    w_query,
    b_query,
    key_value_weight,
    key_value_bias,
    sinks,
    w_out,
    b_out,
    gain_moe,
    w_router,
    b_router,
    routes,
    w_gate_up,
    b_gate_up,
    w_down,
    b_down,
    cotangent,
):
    tok_rows, model = tokens.shape
    ctx_size, ctx_rank = lax.axis_size("ctx"), lax.axis_index("ctx")
    seq_size, seq_rank = lax.axis_size("seq"), lax.axis_index("seq")
    tp_size, tp_rank = lax.axis_size("tp"), lax.axis_index("tp")
    local_heads = sinks.shape[0]
    kv_width = key_value_weight.shape[2]
    kv_heads = kv_width // HEAD_DIMENSION
    group = local_heads // kv_heads
    heads = local_heads // ctx_size
    width = heads * HEAD_DIMENSION
    experts = w_router.shape[1]
    weight_rows = w_query.shape[0]
    padded_rows = -(-weight_rows // 16) * 16
    length = ctx_size * tok_rows
    blocks = seq_size * ctx_size
    kernels = (
        seq_size == 2 and tp_size == 2 and tok_rows % 64 == 0
        and 3 * blocks * tok_rows * model * 2 <= vmem_bytes
    )

    kv_of = [(index * heads) // group for index in range(ctx_size)]
    kv_mine = (ctx_rank * heads) // group

    kv_split = key_value_weight.reshape(weight_rows, 2, kv_heads, HEAD_DIMENSION)
    send = []
    for index in range(ctx_size):
        cols = slice(index * width, (index + 1) * width)
        send.append(
            jnp.concatenate(
                [
                    w_query[:, cols],
                    kv_split[:, 0, kv_of[index]],
                    kv_split[:, 1, kv_of[index]],
                    w_out[cols].T,
                ],
                axis=1,
            )
        )
    send = jnp.pad(jnp.stack(send), ((0, 0), (0, padded_rows - weight_rows), (0, 0)))

    residual = tokens.astype(f32)
    normed_attn, attn_norm_back = jax.vjp(rms_norm, residual, gain_attn)
    normed_low = normed_attn.astype(bf16)
    if kernels:
        rows_all, weights = enter(normed_low, send, ctx_size, 1)
    else:
        rows_all, weights = plain_enter(normed_low, send)
    weights = weights[:, :weight_rows].reshape(model, 2 * width + 2 * HEAD_DIMENSION)
    proj_width = width + 2 * HEAD_DIMENSION
    w_in, w_back = weights[:, :proj_width], weights[:, proj_width:]

    cosine, sine = rotary(length)
    bias = jnp.concatenate(
        [
            lax.dynamic_slice_in_dim(b_query, ctx_rank * width, width),
            lax.dynamic_slice_in_dim(key_value_bias[0], kv_mine * HEAD_DIMENSION, HEAD_DIMENSION),
            lax.dynamic_slice_in_dim(key_value_bias[1], kv_mine * HEAD_DIMENSION, HEAD_DIMENSION),
        ]
    )[None]
    sinks_mine = lax.dynamic_slice_in_dim(sinks, ctx_rank * heads, heads)[None]
    query, keys, values = project(rows_all, w_in, bias, cosine, sine, heads)
    attended, attended_low, log_total, out_part = attend(sinks_mine, query, keys, values, w_back)
    attn_out = ring_sum(out_part, ctx_size, False, 2) if kernels else plain_sum(out_part, "ctx")
    hidden = residual + attn_out.astype(f32) + b_out

    normed_moe, moe_norm_back = jax.vjp(rms_norm, hidden, gain_moe)
    moe_input = normed_moe.astype(bf16)
    logits = jnp.dot(moe_input, w_router, preferred_element_type=f32) + b_router
    onehot = (routes[..., None] == jnp.arange(experts, dtype=jnp.int32)).astype(f32)
    chosen = jnp.sum(onehot * logits[:, None, :], axis=-1)
    gates = jax.nn.softmax(chosen, axis=-1)
    gate_table = jnp.sum(onehot * gates[..., None], axis=1)
    gate_high = lax.reduce_precision(gate_table, 8, 7)
    gate_low = (gate_table - gate_high).astype(bf16)
    wide = -(-(model + 2 * experts) // 128) * 128
    payload = jnp.concatenate(
        [moe_input, gate_high.astype(bf16), gate_low, jnp.zeros((tok_rows, wide - model - 2 * experts), bf16)],
        axis=1,
    )

    gate_up_rows = jnp.transpose(w_gate_up[0], (1, 2, 0)).reshape(-1, model)
    down_weight = w_down[0]
    units = down_weight.shape[0]
    splits = seq_size * tp_size
    lead = ((seq_rank == 0) & (tp_rank == 0)).astype(f32).reshape(1, 1)
    tail = model // 128 * 128
    at = jnp.arange(wide - tail)[None] + tail - model
    pick = ((at == ctx_rank) | (at == experts + ctx_rank)).astype(bf16)
    pick = jnp.concatenate([pick, jnp.zeros((15, wide - tail), bf16)])
    back_wide = -(-(model + 2 * splits * experts) // 128) * 128
    column = 2 * (ctx_rank * splits + seq_rank * tp_size + tp_rank)
    at = jnp.arange(back_wide - tail)[None] + tail - model
    place = jnp.concatenate([at == column, at == column + 1]).astype(bf16)
    place = jnp.concatenate([place, jnp.zeros((14, back_wide - tail), bf16)])

    def expert(rows, upstream):
        return expert_rows(
            lead, rows, upstream, gate_up_rows, b_gate_up[0].reshape(-1, 1), down_weight, b_down, pick, place
        )

    def weight_grads(rows, upstream, gated_act, proj_grad):
        return (
            jnp.dot(proj_grad, rows[:, :model], preferred_element_type=f32),
            jnp.dot(gated_act, upstream, preferred_element_type=f32),
        )

    if kernels:
        dy_wide = -(-model // 128) * 128
        payload = jnp.concatenate([payload, jnp.pad(cotangent, ((0, 0), (0, dy_wide - model)))], axis=1)
        bias_high = lax.reduce_precision(lead * b_down, 8, 7)
        bias_low = lead * b_down - bias_high
        extra_rows = jnp.concatenate([bias_high, bias_low, bias_high, jnp.zeros((13, model), f32)]).astype(bf16)
        rows_all_units, gated_act, proj_grad, dg_rows, gate_bias = expert_in(
            payload, gate_up_rows, down_weight, b_gate_up[0].reshape(-1, 1), extra_rows, pick,
            model, wide, ctx_size, 3,
        )
        back_rows, gate_up_grad = expert_out(
            proj_grad, gate_up_rows, rows_all_units, 0, 5, ctx_size, 4, dg=dg_rows, place=place
        )
        expert_out_sum, down_grad, down_extra = expert_out(
            gated_act, down_weight, rows_all_units, wide, 3, ctx_size, 5, extra=extra_rows
        )
        down_bias = down_extra[0:1] + down_extra[2:3]
    else:
        pieces = blocks * tok_rows // math.gcd(blocks * tok_rows, 2048)

        def one_piece(total, packed):
            rows, upstream = (
                lax.all_gather(part, ("seq", "ctx"), axis=0, tiled=True) for part in packed
            )
            expert_part, back_part, gated_act, proj_grad, gate_bias, down_bias = expert(rows, upstream)
            more = weight_grads(rows, upstream, gated_act, proj_grad) + (gate_bias, down_bias)
            total = jax.tree.map(jnp.add, total, more)
            return total, (plain_sum(expert_part, ("seq", "ctx")), plain_sum(back_part, ("seq", "ctx")))

        start = tuple(
            jnp.zeros(shape, f32) for shape in ((2 * units, model), (units, model), (2 * units, 1), (1, model))
        )
        cut = lambda v: v.reshape(pieces, tok_rows // pieces, v.shape[1])
        total, (expert_out_sum, back_rows) = lax.scan(one_piece, start, (cut(payload), cut(cotangent)))
        gate_up_grad, down_grad, gate_bias, down_bias = total
        expert_out_sum, back_rows = (part.reshape(tok_rows, -1) for part in (expert_out_sum, back_rows))
    grad_w_gate_up = jnp.transpose(gate_up_grad.reshape(2, units, model), (2, 0, 1))[None]
    grad_b_gate_up = gate_bias.reshape(1, 2, units)
    grad_w_down = down_grad[None]
    grad_b_down = down_bias
    mixed = (hidden + expert_out_sum.astype(f32)).astype(bf16)

    upstream = cotangent.astype(f32)
    gate_grad = back_rows[:, model : model + 2 * splits * experts].astype(f32)
    gate_grad = jnp.sum(gate_grad.reshape(tok_rows, experts, 2 * splits), axis=-1)
    gate_grad = jnp.sum(onehot * gate_grad[:, None], axis=-1)
    chosen_grad = gates * (gate_grad - jnp.sum(gates * gate_grad, axis=1, keepdims=True))
    logit_grad = jnp.sum(onehot * chosen_grad[..., None], axis=1).astype(bf16)
    grad_w_router = project_grad(moe_input, logit_grad)
    grad_b_router = jnp.sum(logit_grad, axis=0, dtype=f32)
    moe_grad = back_rows[:, :model].astype(f32) + across(logit_grad, w_router)
    hidden_norm_grad, grad_gain_moe = moe_norm_back(moe_grad)
    hidden_grad = upstream + hidden_norm_grad
    branch_grad = hidden_grad.astype(bf16)
    grad_b_out = jnp.sum(branch_grad, axis=0, dtype=f32)
    if kernels:
        branch_all = ring_gather(branch_grad, ctx_size, 6)
    else:
        branch_all = lax.all_gather(branch_grad, "ctx", axis=0, tiled=True)

    out_grad = jnp.dot(branch_all, w_back, preferred_element_type=f32).astype(bf16)
    dq, dkv, dsinks = attend_back(
        sinks_mine, query, keys, values, attended, log_total, out_grad, cosine, sine
    )
    both = jnp.concatenate([dq, dkv], axis=1)
    input_rows = spread_rows(both, w_in)
    grad_in = project_grad(rows_all, both)
    grad_out = project_grad(branch_all, attended_low)
    gain_part = jnp.sum(grad_in * w_in.astype(f32), axis=1) / gain_attn
    grads = jnp.concatenate([grad_in, grad_out], axis=1).astype(bf16).reshape(blocks, weight_rows, -1)
    grads = jnp.pad(grads, ((0, 0), (0, padded_rows - weight_rows), (0, 0)))

    sum_q = jnp.sum(dq, axis=0, dtype=f32)
    sum_kv = jnp.sum(dkv, axis=0, dtype=f32).reshape(2, HEAD_DIMENSION)
    at_q = lax.dynamic_update_slice_in_dim(jnp.zeros_like(b_query), sum_q, ctx_rank * width, 0)
    at_kv = lax.dynamic_update_slice_in_dim(
        jnp.zeros_like(key_value_bias), sum_kv, kv_mine * HEAD_DIMENSION, 1
    )
    at_sinks = lax.dynamic_update_slice_in_dim(jnp.zeros_like(sinks), dsinks[0], ctx_rank * heads, 0)
    parts = (gain_part, grad_gain_moe, grad_b_out, grad_w_router, grad_b_router, at_q, at_kv, at_sinks)
    packed, starts = [], []
    for part in parts:
        flat = part.reshape(-1)
        starts.append(sum(piece.shape[0] for piece in packed))
        packed.append(jnp.pad(flat, (0, -flat.shape[0] % 1024)))
    shared = packed[0].shape[0] // 128
    small = jnp.concatenate(packed).reshape(-1, 128)
    if kernels:
        normed_grad, owned, small = leave(input_rows, grads, small, shared, ctx_size, 7)
    else:
        normed_grad, owned, small = plain_leave(input_rows, grads, small, shared)
    small = small.reshape(-1)
    sums = [
        small[start : start + part.size].reshape(part.shape) for start, part in zip(starts, parts)
    ]
    tokens_norm_grad, _ = attn_norm_back(normed_grad.astype(f32))
    grad_tokens = (hidden_grad + tokens_norm_grad).astype(bf16)

    owned = owned[:, :weight_rows].astype(f32)
    grad_w_query = jnp.transpose(owned[:, :, :width], (1, 0, 2)).reshape(weight_rows, -1)
    grad_kv = owned[:, :, width:proj_width].reshape(kv_heads, -1, weight_rows, 2, HEAD_DIMENSION)
    grad_w_key_value = jnp.transpose(jnp.sum(grad_kv, axis=1), (1, 2, 0, 3)).reshape(
        weight_rows, 2, kv_width
    )
    grad_w_out = jnp.transpose(owned[:, :, proj_width:], (0, 2, 1)).reshape(-1, weight_rows)

    return (
        mixed,
        grad_tokens,
        sums[0],
        grad_w_query,
        sums[5],
        grad_w_key_value,
        sums[6],
        sums[7],
        grad_w_out,
        sums[2],
        sums[1],
        sums[3],
        sums[4],
        grad_w_gate_up,
        grad_b_gate_up,
        grad_w_down,
        grad_b_down,
    )


def solution(mesh):
    in_specs = (
        P(("seq", "ctx"), None),
        P(),
        P(("seq", "ctx"), "tp"),
        P("tp"),
        P(("seq", "ctx"), None, "tp"),
        P(None, "tp"),
        P("tp"),
        P("tp", ("seq", "ctx")),
        P(),
        P(),
        P(),
        P(),
        P(("seq", "ctx"), None),
        P("ctx", None, None, ("seq", "tp")),
        P("ctx", None, ("seq", "tp")),
        P("ctx", ("seq", "tp"), None),
        P("ctx", None),
        P(("seq", "ctx"), None),
    )
    out_specs = (
        P(("seq", "ctx"), None),
        P(("seq", "ctx"), None),
        P(),
        P(("seq", "ctx"), "tp"),
        P("tp"),
        P(("seq", "ctx"), None, "tp"),
        P(None, "tp"),
        P("tp"),
        P("tp", ("seq", "ctx")),
        P(),
        P(),
        P(),
        P(),
        P("ctx", None, None, ("seq", "tp")),
        P("ctx", None, ("seq", "tp")),
        P("ctx", ("seq", "tp"), None),
        P("ctx", None),
    )
    return jax.shard_map(
        on_device, mesh=mesh, in_specs=in_specs, out_specs=out_specs, check_vma=False
    )
```

time: 3000 us -> 720 us (0.24)
  blocking collectives: 1460 us -> 0 us
  waiting for transfers between devices: 867 us -> 0 us
  Pallas kernels: 0 us -> 589 us
  local copies, waits for them, and re-layouts: 248 us -> 73.9 us
  matrix products: 192 us -> 20.3 us
  starting transfers between devices: 119 us -> 0 us
  other arithmetic: 79.2 us -> 26.8 us
    unnamed x2 -> x0, blocking collectives: 1050 us -> none
    pallas_call x0 -> x11, Pallas kernels: none -> 589 us  [the longest x2 152 us: expert_out(): pl.pallas_call(functools.partial(expert_out_kernel, size, rows, units, mo...]
    all_gather x5 -> x0, waiting for transfers between devices: 398 us -> none  [the longest x2 125 us: to_experts(): return lax.all_gather(arrived[None], 'seq', axis=0, tiled=True)]
    all_to_all x2 -> x0, blocking collectives: 271 us -> none  [to_experts(): lax.all_to_all(outgoing, 'ctx', split_axis=0, concat_axis=0, tiled=True)]
    reduce_scatter x2 -> x0, waiting for transfers between devices: 257 us -> none  [from_hidden(): lax.psum_scatter(partial_sum.astype(jnp.bfloat16), 'seq', scatter_dimensi...]
    all_to_all x2 -> x0, waiting for transfers between devices: 149 us -> none  [to_sources(): lax.all_to_all(expert_rows, 'ctx', split_axis=0, concat_axis=0, tiled=True)]
    dot_general x19 -> x3, matrix products: 132 us -> 8.95 us  [the longest x1 5.74 us: on_device(): jnp.dot(branch_all, w_back, preferred_element_type=f32).astype(bf16)]
    ppermute x32 -> x0, starting transfers between devices: 102 us -> none  [the longest x16 61 us: passed_along(): return lax.ppermute(x, axis, pairs)]
  transfers between devices with their start and end apart: 47 -> 0, of which waited for: 19 -> 0; matrix products, arithmetic and copies ran while one was open for 45% -> 0% of each run, Pallas kernels for 0% -> 0%
where the time goes in v1:
time: 720 us; the launch traced here: 712 us
  Pallas kernels  589 us (82%)
  local copies, waits for them, and re-layouts  73.9 us (10%)
  other arithmetic  26.8 us (4%)
  matrix products  20.3 us (3%)
    pallas_call x2, Pallas kernels, expert_out(): pl.pallas_call(functools.partial(expert_out_kernel, size, rows, units, mo...  152 us
    pallas_call x1, Pallas kernels, expert_in(): pl.pallas_call(functools.partial(expert_in_kernel, size, units, model, wi...  131 us
    pallas_call x1, Pallas kernels, leave(): pl.pallas_call(functools.partial(leave_kernel, size, shared), out_shape=(...  91.4 us
    pallas_call x1, Pallas kernels, enter(): pl.pallas_call(functools.partial(enter_kernel, size), out_shape=(jax.Shap...  88.6 us
    pallas_call x1, Pallas kernels, ring_sum(): pl.pallas_call(functools.partial(sum_kernel, size, both), out_shape=jax.S...  44.7 us
    unnamed x131, local copies, waits for them, and re-layouts  37.5 us
    pallas_call x1, Pallas kernels, ring_gather(): pl.pallas_call(functools.partial(gather_kernel, size, both), out_shape=sh...  36 us
    pallas_call x1, Pallas kernels, attend_back(): pl.pallas_call(functools.partial(attend_back_kernel, heads, length), grid...  15.7 us

profile of v1, /device:TPU:0, one launch (start us, length us, event | category | flops | bytes accessed | tf_op | source)
XLA Modules:
  0.0 711.8 jit_solution(9949874590275889833)
XLA Ops:
  0.7 1.5 copy.122
  2.2 1.3 dynamic-slice_bitcast_fusion.2.sink_ref
  4.7 1.1 fusion.8.x_ref
  6.9 0.7 slice_bitcast_fusion.2
  7.6 0.7 fusion.51
  8.6 0.9 copy.155
  9.4 0.9 copy.154
  10.3 1.1 fusion.27
  11.4 1.0 fusion.30
  12.4 0.9 copy.157
  13.3 0.9 copy.156
  14.4 0.9 copy.159
  15.3 0.9 copy.158
  16.4 1.5 pad.42.w_ref
  17.8 88.6 %enter_rows_and_weights.1 = (bf16[1024,2880]{1,0:T(8,128)(2,1)}, bf16[16,192,640]{2,1,0:T(8,128)(2,1)}) custom-call(bf16[128,2880]{1,0:T(8,128)(2,1)} %fusion.8.x_ref, bf16[8,192,640]{2,1,0:T(8,128)(2,1)} %pad.42.w_ref), custom_call_target="tpu_custom_call" | custom-call | tf_op jit(solution)/shard_map/enter_rows_and_weights/pallas_call | solution.py:297
  106.4 4.3 slice.172
  110.7 4.6 reshape.267
  115.3 3.3 slice.202.w_ref
  118.7 0.8 dynamic_slice.17
  120.1 2.0 fusion.37
  122.1 1.9 pad_maximum_fusion
  123.9 8.1 %project_rows.1 = (bf16[1024,256]{1,0:T(8,128)(2,1)}, bf16[1024,64]{1,0:T(8,128)(2,1)}, bf16[1024,64]{1,0:T(8,128)(2,1)}) custom-call(bf16[1024,2880]{1,0:T(8,128)(2,1)} %get-tuple-element.42.x_ref, bf16[2880,384]{1,0:T(8,128)(2,1)} %slice.202.w_ref, f32[1,384]{1,0:T(1,128)} %broadcast_in_dim.23.b_ref, f32[1024,128]{1,0:T(8,128)} %get-tuple-element.202.cos_ref.kcos_ref, ...), custom_call_target="tpu_custom_call" | custom-call | tf_op jit(solution)/shard_map/project_rows/pallas_call | solution.py:1251
  132.1 2.6 slice.203.w_ref
  134.6 13.6 %attend_rows.1 = (f32[1024,256]{1,0:T(8,128)}, bf16[1024,256]{1,0:T(8,128)(2,1)}, f32[1024,4]{1,0:T(8,128)}, bf16[1024,2880]{1,0:T(8,128)(2,1)}) custom-call(f32[1,4]{1,0:T(1,128)} %dynamic-slice_bitcast_fusion.2.sink_ref, bf16[1024,256]{1,0:T(8,128)(2,1)} %get-tuple-element.44.q_ref, bf16[1024,64]{1,0:T(8,128)(2,1)} %get-tuple-element.45.k_ref, ...), custom_call_target="tpu_custom_call" | custom-call | tf_op jit(solution)/shard_map/attend_rows/pallas_call | solution.py:1320
  148.2 44.7 %sum_ctx.1 = bf16[128,2880]{1,0:T(8,128)(2,1)} custom-call(bf16[1024,2880]{1,0:T(8,128)(2,1)} %get-tuple-element.47.p_ref), custom_call_target="tpu_custom_call" | custom-call | tf_op jit(solution)/shard_map/sum_ctx/pallas_call | solution.py:485
  193.0 1.6 multiply_reduce_fusion.3
  196.7 1.9 concatenate.79.x_ref
  198.6 1.2 reshape_squeeze.4.bias_ref
  199.9 0.7 maximum_maximum_fusion.extra_ref.refs_3_
  201.3 131.2 %expert_in.1 = (bf16[8,256,5888]{2,1,0:T(8,128)(2,1)}, bf16[736,2048]{1,0:T(8,128)(2,1)}, bf16[1440,2048]{1,0:T(8,128)(2,1)}, bf16[16,2048]{1,0:T(8,128)(2,1)}, f32[1440,1]{1,0:T(8,128)}) custom-call(bf16[128,5888]{1,0:T(8,128)(2,1)} %concatenate.79.x_ref, bf16[1440,2880]{1,0:T(8,128)(2,1)} %bitcast.117, bf16[720,2880]{1,0:T(8,128)(2,1)} %bitcast.119, ...), custom_call_target="tpu_custom_call" | custom-call | tf_op jit(solution)/shard_map/expert_in/pallas_call | solution.py:912
  333.1 81.0 %expert_back.1 = (bf16[128,2944]{1,0:T(8,128)(2,1)}, f32[1440,2880]{1,0:T(8,128)}) custom-call(bf16[1440,2048]{1,0:T(8,128)(2,1)} %get-tuple-element.51.refs_0_, bf16[1440,2880]{1,0:T(8,128)(2,1)} %bitcast.118, bf16[8,256,5888]{2,1,0:T(8,128)(2,1)} %get-tuple-element.49.refs_2_, bf16[16,2048]{1,0:T(8,128)(2,1)} %get-tuple-element.52.refs_3_, ...), custom_call_target="tpu_custom_call" | custom-call | tf_op jit(solution)/shard_map/expert_back/pallas_call | solution.py:1181
  414.1 0.8 slice_convert_fusion.1
  415.2 2.9 multiply_reduce_fusion.1
  418.2 1.5 convert_reduce_fusion
  419.7 36.0 %gather_ctx.1 = bf16[1024,2880]{1,0:T(8,128)(2,1)} custom-call(bf16[128,2880]{1,0:T(8,128)(2,1)} %get-tuple-element.155.refs_0_), custom_call_target="tpu_custom_call" | custom-call | tf_op jit(solution)/shard_map/gather_ctx/pallas_call | solution.py:244
  455.8 5.7 convolution_convert_fusion.1.do_ref
  461.5 15.7 %attend_rows_back.1 = (bf16[1024,256]{1,0:T(8,128)(2,1)}, bf16[1024,128]{1,0:T(8,128)(2,1)}, f32[1,4]{1,0:T(1,128)}) custom-call(f32[1,4]{1,0:T(1,128)} %dynamic-slice_bitcast_fusion.2.sink_ref, bf16[1024,256]{1,0:T(8,128)(2,1)} %get-tuple-element.44.q_ref, bf16[1024,64]{1,0:T(8,128)(2,1)} %get-tuple-element.45.k_ref, ...), custom_call_target="tpu_custom_call" | custom-call | tf_op jit(solution)/shard_map/attend_rows_back/pallas_call | solution.py:1426
  477.2 1.1 constant_dynamic-update-slice_fusion.1
  478.2 1.0 constant_dynamic-update-slice_fusion.x_ref
  479.3 0.9 copy-done.9
  480.1 7.4 %spread_rows.1.p_ref = bf16[1024,2880]{1,0:T(8,128)(2,1)} custom-call(bf16[1024,384]{1,0:T(8,128)(2,1)} %copy-done.9, bf16[2880,384]{1,0:T(8,128)(2,1)} %slice.202.w_ref), custom_call_target="tpu_custom_call" | custom-call | tf_op jit(solution)/shard_map/spread_rows/pallas_call | solution.py:1354
  487.5 2.8 convolution_convert_fusion
  490.4 1.3 concatenate.88
  491.7 8.1 %multiply_reduce_fusion = (f32[2880]{0:T(1024)S(1)}, bf16[2880,384]{1,0:T(8,128)(2,1)}) fusion(bf16[2880,640]{1,0:T(8,128)(2,1)} %reshape.267, bf16[1024,2880]{1,0:T(8,128)(2,1)} %get-tuple-element.42.x_ref, bf16[1024,384]{1,0:T(8,128)(2,1)S(1)} %copy-done.10), kind=kOutput, calls=%fused_computation.3 | convolution fusion | flops 2269345024 | bytes 11119872 | tf_op jit(solution)/shard_map/dot_general | solution.py:1482
  499.7 2.5 concatenate.87
  502.3 3.4 fusion.2.g_ref
  506.1 0.7 reshape.271
  508.6 91.4 %leave_rows_and_weights.1 = (bf16[128,2880]{1,0:T(8,128)(2,1)}, bf16[8,192,640]{2,1,0:T(8,128)(2,1)}, f32[296,128]{1,0:T(8,128)}) custom-call(bf16[1024,2880]{1,0:T(8,128)(2,1)} %spread_rows.1.p_ref, bf16[16,192,640]{2,1,0:T(8,128)(2,1)} %fusion.2.g_ref, f32[296,128]{1,0:T(8,128)} %bitcast.151), custom_call_target="tpu_custom_call" | custom-call | tf_op jit(solution)/shard_map/leave_rows_and_weights/pallas_call | solution.py:573
  599.9 1.5 fusion.10
  601.5 71.2 %expert_out.1 = (bf16[128,2880]{1,0:T(8,128)(2,1)}, f32[720,2880]{1,0:T(8,128)}, f32[16,2880]{1,0:T(8,128)}) custom-call(bf16[736,2048]{1,0:T(8,128)(2,1)} %get-tuple-element.48.refs_0_, bf16[720,2880]{1,0:T(8,128)(2,1)} %bitcast.120, bf16[8,256,5888]{2,1,0:T(8,128)(2,1)} %get-tuple-element.49.refs_2_, bf16[16,2880]{1,0:T(8,128)(2,1)} %maximum_maximum_fusion.extra_ref.refs_3_), custom_call_target="tpu_custom_call" | custom-call | tf_op jit(solution)/shard_map/expert_out/pallas_call | solution.py:1181
  672.7 3.4 fusion.5
  676.1 1.1 copy.145
  677.3 1.1 copy.146
  679.0 1.8 slice_convert_fusion
  681.6 1.7 copy.161
  684.5 0.9 copy.147
  687.1 1.7 copy.162
  688.8 0.8 reshape.281
  689.6 1.1 copy.148
  691.5 0.7 reshape.283
  692.2 1.6 slice_add_fusion
  693.8 13.2 %copy.185 = f32[1,2880,2,720]{1,3,2,0:T(8,128)} copy(f32[1,2880,2,720]{1,3,2,0:T(8,128)} %bitcast.121) | data formatting | bytes 33177600
  707.0 0.9 slice-done.2
  707.9 3.4 copy.186
  (185 shorter events, 14.5 us)
Async XLA Ops:
  0.7 194.8 %copy-start = (bf16[2880,8]{0,1:T(8,128)(2,1)S(1)}, bf16[2880,8]{0,1:T(8,128)(2,1)}, u32[]{:S(2)}) copy-start(bf16[2880,8]{0,1:T(8,128)(2,1)} %param.28) | copy-start | bytes 138244
  0.7 4.0 copy-start.17
  2.2 3.7 copy-start.20
  3.7 0.5 copy-start.39
  3.7 3.2 copy-start.13
  4.2 0.5 copy-start.34
  5.8 1.8 copy-start.14
  115.3 3.3 copy-start.38
  148.2 44.7 %copy-start.18 = (f32[2880]{0:T(1024)S(1)}, f32[2880]{0:T(1024)}, u32[]{:S(2)}) copy-start(f32[2880]{0:T(1024)} %param.26) | copy-start | bytes 34564
  193.0 2.1 copy-start.2
  193.0 2.1 copy-start.23
  194.6 1.2 copy-start.41
  194.6 0.9 copy-start.43
  194.6 0.5 copy-start.31
  195.1 0.7 copy-start.25
  195.1 1.1 copy-start.16
  195.5 1.2 copy-start.4
  195.9 0.8 copy-start.28
  196.6 2.0 copy-start.6
  196.7 1.9 copy-start.30
  196.7 3.1 copy-start.27
  333.1 82.0 %copy-start.29 = (f32[128]{0:T(128)S(1)}, f32[128]{0:T(128)}, u32[]{:S(2)}) copy-start(f32[128]{0:T(128)} %copy-done.28) | copy-start | bytes 1540
  333.1 82.0 %copy-start.32 = (f32[128]{0:T(128)S(1)}, f32[128]{0:T(128)}, u32[]{:S(2)}) copy-start(f32[128]{0:T(128)} %copy-done.31) | copy-start | bytes 1540
  415.2 2.9 copy-start.42
  415.2 3.0 copy-start.3
  415.2 3.0 copy-start.7
  418.1 1.6 copy-start.8
  418.1 1.6 copy-start.36
  461.5 26.0 %slice-start.3 = ((s8[6029312]{0:T(1024)(128)(4,1)}), s8[4194304]{0:T(1024)(128)(4,1)S(1)}, s32[]{:S(2)}) async-start(s8[6029312]{0:T(1024)(128)(4,1)} %bitcast.125), calls=%async_computation.3 | async-start | bytes 8388608
  479.3 0.9 copy-start.9
  480.1 7.4 %slice-start.4 = ((s8[6029312]{0:T(1024)(128)(4,1)}), s8[1835008]{0:T(1024)(128)(4,1)S(1)}, s32[]{:S(2)}) async-start(s8[6029312]{0:T(1024)(128)(4,1)} %bitcast.125), calls=%async_computation.4 | async-start | bytes 3670016
  490.4 1.3 copy-start.10
  502.3 3.4 copy-start.26
  502.3 3.4 copy-start.5
  505.7 1.2 copy-start.11
  506.1 1.3 copy-start.12
  506.1 1.7 copy-start.44
  507.9 0.7 copy-start.21
  599.9 1.5 copy-start.40
  601.4 71.3 %copy-start.19 = (f32[2880]{0:T(1024)S(1)}, f32[2880]{0:T(1024)}, u32[]{:S(2)}) copy-start(f32[2880]{0:T(1024)} %param.26) | copy-start | bytes 34564
  601.4 71.2 %copy-start.24 = (f32[2880]{0:T(1024)S(1)}, f32[2880]{0:T(1024)}, u32[]{:S(2)}) copy-start(f32[2880]{0:T(1024)} %param.27) | copy-start | bytes 34564
  601.4 71.2 %copy-start.33 = (f32[128]{0:T(128)S(1)}, f32[128]{0:T(128)}, u32[]{:S(2)}) copy-start(f32[128]{0:T(128)} %copy-done.31) | copy-start | bytes 1540
  601.4 71.2 %copy-start.35 = (f32[128]{0:T(128)S(1)}, f32[128]{0:T(128)}, u32[]{:S(2)}) copy-start(f32[128]{0:T(128)} %copy-done.34) | copy-start | bytes 1540
  601.5 71.2 %copy-start.37 = (f32[128]{0:T(128)S(1)}, f32[128]{0:T(128)}, u32[]{:S(2)}) copy-start(f32[128]{0:T(128)} %copy-done.36) | copy-start | bytes 1540
  676.1 2.3 copy-start.22
  688.8 2.4 copy-start.15
  689.6 17.4 %slice-start = ((s8[8478720]{0:T(1024)(128)(4,1)}), s8[90112]{0:T(1024)(128)(4,1)S(1)}, s32[]{:S(2)}) async-start(s8[8478720]{0:T(1024)(128)(4,1)} %bitcast.122), calls=%async_computation | async-start | bytes 180224
  693.8 13.2 %slice-start.1 = ((s8[8478720]{0:T(1024)(128)(4,1)}), s8[4194304]{0:T(1024)(128)(4,1)S(1)}, s32[]{:S(2)}) async-start(s8[8478720]{0:T(1024)(128)(4,1)} %bitcast.122), calls=%async_computation.1 | async-start | bytes 8388608
  693.8 14.1 %slice-start.2 = ((s8[8478720]{0:T(1024)(128)(4,1)}), s8[4194304]{0:T(1024)(128)(4,1)S(1)}, s32[]{:S(2)}) async-start(s8[8478720]{0:T(1024)(128)(4,1)} %bitcast.122), calls=%async_computation.2 | async-start | bytes 8388608
  707.9 3.4 copy-start.1

commit v2 on v1

--- a/solution.py
+++ b/solution.py
@@ -3,6 +3,7 @@
 
 import jax
 import jax.numpy as jnp
+import numpy as np
 from jax import lax
 from jax.experimental import pallas as pl
 from jax.experimental.pallas import tpu as pltpu
@@ -255,60 +256,6 @@
     return out if both else out[0]
 
 
-def enter_kernel(size, x_ref, w_ref, o_ref, wo_ref, w_s, w_r, wx_s, wx_r, wl, *sems):
-    a = Around(size)
-    ring = RingGather(a, False, x_ref, o_ref, *sems)
-    order = []
-    for d in range(1, size // 2 + 1):
-        order += [d] if 2 * d == size else [d, size - d]
-    greet(ring.partners() + [a.across] + [a.at(d) for d in order if 1 < d < size - 1])
-    mine = a.seq * size + a.ctx
-    local = pltpu.make_async_copy(w_ref.at[a.ctx], wo_ref.at[mine], wl)
-    local.start()
-    ring.start()
-    crossed = [remote(w_ref.at[a.ctx], wo_ref.at[mine], wx_s.at[0], wx_r.at[0], a.across)]
-    sent = {}
-    for d in order:
-        sent[d] = remote(w_ref.at[a.index(d)], wo_ref.at[mine], w_s.at[d], w_r.at[d], a.at(d))
-    taken = 0
-
-    def take():
-        d = order[len(crossed) - 1]
-        sent[d].wait_recv()
-        block = wo_ref.at[a.seq * size + a.index(-d)]
-        crossed.append(remote(block, block, wx_s.at[d], wx_r.at[d], a.across))
-
-    for k in range(size // 2):
-        ring.step(k)
-        for _ in range(2):
-            if len(crossed) < size:
-                take()
-    ring.finish()
-    for copy in crossed:
-        copy.wait()
-    for copy in sent.values():
-        copy.wait_send()
-    local.wait()
-
-
-def enter(x, w, size, ident):
-    dma = pltpu.SemaphoreType.DMA
-    hbm = pl.BlockSpec(memory_space=pl.ANY)
-    return pl.pallas_call(
-        functools.partial(enter_kernel, size),
-        out_shape=(
-            jax.ShapeDtypeStruct((size * x.shape[0], x.shape[1]), x.dtype),
-            jax.ShapeDtypeStruct((2 * size,) + w.shape[1:], w.dtype),
-        ),
-        in_specs=[hbm, hbm],
-        out_specs=(hbm, hbm),
-        scratch_shapes=[dma((size,)), dma((size,)), dma((size,)), dma((size,)), dma(())]
-        + RingGather.semaphores(size, False),
-        compiler_params=pltpu.CompilerParams(collective_id=ident, has_side_effects=True),
-        name="enter_rows_and_weights",
-    )(x, w)
-
-
 class RingSum:
     def __init__(
         self, around, both, p_ref, o_ref, acc, met, ringbuf, crossbuf, lastbuf,
@@ -496,107 +443,124 @@
 
 
 def leave_kernel(
-    size, shared, p_ref, g_ref, v_ref, o_ref, go_ref, vo_ref,
-    gacc, gmet, vmet, gx_s, gx_r, g_s, g_r, gl, v_s, v_r, *scratch,
+    size, halves, p_ref, g_ref, v_ref, o_ref, go_ref, vo_ref, gmet, vmet, g_s, g_r, gl, v_s, v_r, *scratch
 ):
     a = Around(size)
     ring = RingSum(a, False, p_ref, o_ref, *scratch)
-    order = ring.order
-    greet(ring.partners() + [a.across] + [a.at(d) for d in order if 1 < d < size - 1])
-
+    pair = a.ctx + 1 - 2 * (a.ctx % 2)
+    peers = [(a.seq, lax.rem(a.ctx + 2 * d, size), a.core) for d in range(1, size // 2)]
+    load = pltpu.make_async_copy(g_ref.at[0], go_ref, gl)
+    greet([a.right, a.left, a.sibling, a.across, (a.seq, pair, a.core)] + peers)
     swaps = [remote(v_ref, vmet.at[0], v_s.at[0], v_r.at[0], a.across)]
-
-    def swap(slot, device):
-        return remote(vo_ref, vmet.at[slot], v_s.at[slot], v_r.at[slot], device)
-
-    crossed, here = {}, {}
-    for d in order:
-        index = a.index(d)
-        crossed[d] = remote(
-            g_ref.at[(1 - a.seq) * size + index], gmet.at[d], gx_s.at[d], gx_r.at[d], a.across
-        )
-        here[d] = pltpu.make_async_copy(g_ref.at[a.seq * size + index], gacc.at[d], gl.at[d])
-        here[d].start()
+    crossed = [remote(g_ref.at[1, i], gmet.at[i], g_s.at[i], g_r.at[i], a.across) for i in range(size)]
     ring.start()
-    sent = {}
-
-    def pass_on(d):
-        crossed[d].wait_recv()
-        here[d].wait()
-        ring.add(gacc.at[d], gmet.at[d])
-        if d:
-            sent[d] = remote(gacc.at[d], go_ref.at[a.ctx], g_s.at[d], g_r.at[d], a.at(d))
-        else:
-            go_ref[a.ctx] = gacc[d]
-
-    todo = list(order)
-    pair = a.ctx + 1 - 2 * (a.ctx % 2)
+    load.start()
+    last = 3 + size // 2
+
+    def take(first, upto):
+        for i in range(first, upto):
+            crossed[i].wait_recv()
+            ring.add(go_ref.at[i], gmet.at[i])
+
     for k in range(size // 2):
         ring.step(k)
         if k == 0:
             swaps[0].wait()
-            vo_ref[...] = v_ref[...] + vmet[0]
-            swaps = [swap(1, (a.seq, pair, a.core))]
-        elif k == 2:
+            vmet[1] = v_ref[...] + vmet[0]
+            swaps = [remote(vmet.at[1], vmet.at[2], v_s.at[1], v_r.at[1], (a.seq, pair, a.core))]
+            load.wait()
+        elif k == 1:
             swaps[0].wait()
-            vo_ref[...] += vmet[1]
+            vmet[3] = vmet[1] + vmet[2]
             swaps = [
-                swap(1 + d, (a.seq, lax.rem(a.ctx + 2 * d, size), a.core)) for d in range(1, size // 2)
+                remote(vmet.at[3], vmet.at[3 + d], v_s.at[1 + d], v_r.at[1 + d], peers[d - 1])
+                for d in range(1, size // 2)
             ]
-        for _ in range(2):
-            pass_on(todo.pop(0))
-    ring.finish()
-    while todo:
-        pass_on(todo.pop(0))
+        take(2 * k, 2 * k + 1 if k == size // 2 - 1 else 2 * (k + 1))
     for copy in swaps:
         copy.wait()
+    total = vmet[3]
     for d in range(1, size // 2):
-        vo_ref[...] += vmet[1 + d]
-    head = pl.ds(0, shared)
-    last = 1 + size // 2
-    copy = remote(vo_ref.at[head], vmet.at[last, head], v_s.at[last], v_r.at[last], a.sibling)
+        total = total + vmet[3 + d]
+    vmet[last] = total
+    copy = remote(vmet.at[last], vmet.at[last + 1], v_s.at[size // 2 + 1], v_r.at[size // 2 + 1], a.sibling)
+    ring.finish()
+    take(size - 1, size)
     copy.wait()
-    vo_ref[head] += vmet[last, head]
-    for copy in crossed.values():
+    own, other = vmet[last], vmet[last + 1]
+    vo_ref[...] = jnp.zeros_like(vo_ref)
+    vo_ref[0:1] = own[0:1] + other[0:1]
+    vo_ref[1:2] = own[1:2]
+    core = lax.broadcasted_iota(jnp.int32, (halves, own.shape[1]), 0) * 0 + a.core
+    first, second = own[2 : 2 + halves], other[2 : 2 + halves]
+    vo_ref[2 : 2 + halves] = jnp.where(core == 0, first, second)
+    vo_ref[2 + halves : 2 + 2 * halves] = jnp.where(core == 0, second, first)
+    for copy in crossed:
         copy.wait_send()
-    for copy in sent.values():
-        copy.wait()
-
-
-def leave(p, g, small, shared, size, ident):
-    rows, width = p.shape[0] // size, p.shape[1]
+
+
+def leave(p, g, small, halves, size, ident):
+    rows, model = p.shape[0] // size, p.shape[1]
     dma = pltpu.SemaphoreType.DMA
     hbm = pl.BlockSpec(memory_space=pl.ANY)
     vmem = pl.BlockSpec(memory_space=pltpu.VMEM)
-    block = (size,) + g.shape[1:]
-    steps = 2 + size // 2
+    steps = size // 2 + 2
+    out_rows = -(-(2 + 2 * halves) // 8) * 8
     return pl.pallas_call(
-        functools.partial(leave_kernel, size, shared),
+        functools.partial(leave_kernel, size, halves),
         out_shape=(
-            jax.ShapeDtypeStruct((rows, width), p.dtype),
-            jax.ShapeDtypeStruct(block, g.dtype),
-            jax.ShapeDtypeStruct(small.shape, small.dtype),
+            jax.ShapeDtypeStruct((rows, model), p.dtype),
+            jax.ShapeDtypeStruct(g.shape[1:], g.dtype),
+            jax.ShapeDtypeStruct((out_rows, small.shape[1]), small.dtype),
         ),
         in_specs=[hbm, hbm, vmem],
         out_specs=(vmem, vmem, vmem),
         scratch_shapes=[
-            pltpu.VMEM(block, g.dtype),
-            pltpu.VMEM(block, g.dtype),
-            pltpu.VMEM((steps,) + small.shape, small.dtype),
+            pltpu.VMEM(g.shape[1:], g.dtype),
+            pltpu.VMEM((size // 2 + 5,) + small.shape, small.dtype),
             dma((size,)),
             dma((size,)),
-            dma((size,)),
-            dma((size,)),
-            dma((size,)),
+            dma(()),
             dma((steps,)),
             dma((steps,)),
         ]
-        + RingSum.scratch(size, False, rows, width, p.dtype),
+        + RingSum.scratch(size, False, rows, model, p.dtype),
         compiler_params=pltpu.CompilerParams(
             collective_id=ident, has_side_effects=True, vmem_limit_bytes=vmem_bytes
         ),
-        name="leave_rows_and_weights",
+        name="leave_rows",
     )(p, g, small)
+
+
+def settle_kernel(width, kv_of, spans, g_ref, v_ref, q_ref, kv_ref, wo_ref, *small_refs):
+    proj = width + 2 * HEAD_DIMENSION
+    weight_rows = q_ref.shape[0]
+    by_head = {}
+    for index, head_at in enumerate(kv_of):
+        block = g_ref[index, :weight_rows].astype(f32)
+        span = slice(index * width, (index + 1) * width)
+        q_ref[:, span] = block[:, :width]
+        wo_ref[:, span] = block[:, proj:]
+        piece = block[:, width:proj]
+        by_head[head_at] = by_head[head_at] + piece if head_at in by_head else piece
+    for head_at, piece in by_head.items():
+        kv_ref[:, head_at * 2 * HEAD_DIMENSION : (head_at + 1) * 2 * HEAD_DIMENSION] = piece
+    for ref, (row, start) in zip(small_refs, spans):
+        ref[...] = v_ref[row : row + ref.shape[0], start : start + ref.shape[1]]
+
+
+def settle_gradients(g, v, width, weight_rows, kv_of, spans, shapes):
+    kv_wide = (max(kv_of) + 1) * 2 * HEAD_DIMENSION
+    large = [(weight_rows, len(kv_of) * width), (weight_rows, kv_wide), (weight_rows, len(kv_of) * width)]
+    vmem = pl.BlockSpec(memory_space=pltpu.VMEM)
+    return pl.pallas_call(
+        functools.partial(settle_kernel, width, kv_of, spans),
+        out_shape=[jax.ShapeDtypeStruct(shape, f32) for shape in large + shapes],
+        in_specs=[vmem] * 2,
+        out_specs=[vmem] * (3 + len(shapes)),
+        compiler_params=pltpu.CompilerParams(vmem_limit_bytes=vmem_bytes),
+        name="settle_gradients",
+    )(g, v)
 
 
 def plain_enter(x, w):
@@ -610,10 +574,10 @@
     return lax.psum(part, "tp")
 
 
-def plain_leave(p, g, small, shared):
+def plain_leave(p, g, small):
     kept = lax.psum_scatter(g, "seq", scatter_dimension=0, tiled=True)
     owned = lax.all_to_all(kept, "ctx", split_axis=0, concat_axis=0, tiled=True)
-    small = jnp.concatenate([lax.psum(small[:shared], "tp"), small[shared:]])
+    small = jnp.concatenate([lax.psum(small[:1], "tp"), small[1:]])
     return plain_sum(p, "ctx"), owned, lax.psum(small, ("seq", "ctx"))
 
 
@@ -735,101 +699,396 @@
     return {j: slot for slot, j in enumerate(unit_order(size))}
 
 
-def expert_in_kernel(
-    size, units, model, wide,
-    x_ref, wt_ref, wd_ref, bias_ref, extra_ref, pick_ref,
-    x_all, act_all, dgu_all, dg_ref, gbias_ref,
-    xbuf, wt, wd, act_buf, dgu_buf,
-    load_s, ring_s, ring_r, cross_s, cross_r, core_s, core_r, keep_s,
+class UnitGather:
+    def __init__(self, around, x_ref, buf, sems, first):
+        self.a, self.x, self.buf = around, x_ref, buf
+        self.own_s, self.ring_s, self.ring_r, self.cross_s, self.cross_r, self.core_s, self.core_r = sems
+        self.rows = x_ref.shape[0]
+        self.half = self.rows // 2
+        self.starts, self.counts = (0, first), (first, self.half - first)
+        size = around.size
+        far, near = size // 2, size - 1 - size // 2
+        self.items = [(1, 0, far, near), (0, 0, near, far), (0, 1, far, near)]
+        self.slot_of = unit_slots(size)
+        self.sent, self.ring, self.crossed, self.shared = [], {}, {}, {}
+
+    @staticmethod
+    def semaphores(size):
+        dma = pltpu.SemaphoreType.DMA
+        return [
+            dma((2,)),
+            dma((3, 2, size // 2)),
+            dma((3, 2, size // 2)),
+            dma((size + 1,)),
+            dma((size + 1,)),
+            dma((size, 2, 2)),
+            dma((size, 2, 2)),
+        ]
+
+    def spot(self, j, other, core, piece):
+        start = other * self.rows + core * self.half + self.starts[piece]
+        return self.buf.at[self.slot_of[j], pl.ds(start, self.counts[piece])]
+
+    def hop(self, item, way, k, src):
+        a = self.a
+        piece, other, _, _ = self.items[item]
+        j = a.size - (k + 1) if way == 0 else k + 1
+        copy = remote(
+            src, self.spot(j, other, 0, piece), self.ring_s.at[item, way, k], self.ring_r.at[item, way, k],
+            a.right if way == 0 else a.left,
+        )
+        self.ring[item, way, k] = copy
+        self.sent.append(copy)
+
+    def cross(self, j, piece, src):
+        at = self.slot_of[j] if piece else self.a.size
+        copy = remote(src, self.spot(j, 1, 0, piece), self.cross_s.at[at], self.cross_r.at[at], self.a.across)
+        self.crossed[j, piece] = copy
+        self.sent.append(copy)
+
+    def share(self, j, other, piece):
+        at = (self.slot_of[j], other, piece)
+        copy = remote(
+            self.spot(j, other, 0, piece), self.spot(j, other, 1, piece), self.core_s.at[at],
+            self.core_r.at[at], self.a.sibling,
+        )
+        self.shared[j, other, piece] = copy
+        self.sent.append(copy)
+
+    def start(self):
+        a, half = self.a, self.half
+
+        def own(core, start, count):
+            return self.x.at[pl.ds(pl.multiple_of(core * half + start, 16), count)]
+
+        pieces = [own(a.core, start, count) for start, count in zip(self.starts, self.counts)]
+        self.cross(0, 0, pieces[0])
+        for item in range(2):
+            for way in range(2):
+                self.hop(item, way, 0, pieces[self.items[item][0]])
+        self.cross(0, 1, pieces[1])
+        self.mine = [
+            pltpu.make_async_copy(
+                own(a.core if here == 0 else 1 - a.core, 0, half),
+                self.buf.at[self.slot_of[0], pl.ds(here * half, half)],
+                self.own_s.at[here],
+            )
+            for here in range(2)
+        ]
+        for copy in self.mine:
+            copy.start()
+
+    def first(self):
+        self.crossed[0, 0].wait_recv()
+        for way in range(2):
+            self.hop(2, way, 0, self.spot(0, 1, 0, 0))
+        self.share(0, 1, 0)
+        self.crossed[0, 1].wait_recv()
+        self.share(0, 1, 1)
+
+    def step(self, k):
+        size = self.a.size
+        for item, (piece, other, right, left) in enumerate(self.items):
+            for way, hops in ((0, right), (1, left)):
+                if k >= hops:
+                    continue
+                self.ring[item, way, k].wait_recv()
+                j = size - (k + 1) if way == 0 else k + 1
+                if k + 1 < hops:
+                    self.hop(item, way, k + 1, self.spot(j, other, 0, piece))
+                if item == 0:
+                    self.cross(j, 1, self.spot(j, 0, 0, 1))
+                self.share(j, other, piece)
+
+    def after(self, k):
+        if k < 0:
+            return [0]
+        return [k + 1] if 2 * (k + 1) == self.a.size else [k + 1, self.a.size - (k + 1)]
+
+    def collect(self, js):
+        for j in js:
+            if j == 0:
+                for copy in self.mine:
+                    copy.wait()
+            else:
+                self.crossed[j, 1].wait_recv()
+                self.share(j, 1, 1)
+        for j in js:
+            for key in [(j, 0, 0), (j, 0, 1), (j, 1, 0), (j, 1, 1)]:
+                if key in self.shared:
+                    self.shared[key].wait_recv()
+
+    def finish(self):
+        for copy in self.sent:
+            copy.wait_send()
+
+
+class UnitSum:
+    def __init__(self, around, rows, lhs, w, ends, o_ref, scratch, first):
+        (
+            self.acc, self.own, self.out, self.ringbuf, self.crossbuf, self.lastbuf,
+            self.ring_s, self.ring_r, self.cross_s, self.cross_r, self.core_s, self.core_r,
+            self.out_s, self.out_r,
+        ) = scratch
+        self.a, self.rows, self.lhs, self.w, self.ends, self.o = around, rows, lhs, w, ends, o_ref
+        self.half = rows // 2
+        self.starts, self.counts = (0, first), (first, self.half - first)
+        size = around.size
+        far, near = size // 2, size - 1 - size // 2
+        self.items = [(0, 1, far, near), (0, 0, near, far), (1, 0, far, near)]
+        self.slot_of = unit_slots(size)
+        self.ring, self.sent, self.joined, self.made = {}, [], set(), 0
+
+    @staticmethod
+    def scratch(size, rows, width, first):
+        half = rows // 2
+        dma = pltpu.SemaphoreType.DMA
+        return [
+            pltpu.VMEM((2, size, half, width), bf16),
+            pltpu.VMEM((2, 2, half, width), bf16),
+            pltpu.VMEM((2, 2, half, width), bf16),
+            pltpu.VMEM((2, size // 2, half + first, width), bf16),
+            pltpu.VMEM((size, half - first, width), bf16),
+            pltpu.VMEM((first, width), bf16),
+            dma((3, 2, size // 2)),
+            dma((3, 2, size // 2)),
+            dma((size + 1,)),
+            dma((size + 1,)),
+            dma((2, size)),
+            dma((2, size)),
+            dma((2,)),
+            dma((2,)),
+        ]
+
+    def arrived(self, item, way, d):
+        first, second = self.counts
+        start, count = ((0, first), (first, first), (2 * first, second))[item]
+        return self.ringbuf.at[way, d, pl.ds(start, count)]
+
+    def handed(self, slot, other):
+        return pltpu.make_async_remote_copy(
+            src_ref=self.out.at[slot % 2, other],
+            dst_ref=self.acc.at[other, slot],
+            send_sem=self.core_s.at[other, slot],
+            recv_sem=self.core_r.at[other, slot],
+            device_id=self.a.sibling,
+            device_id_type=pl.DeviceIdType.MESH,
+        )
+
+    def over(self, slot):
+        return pltpu.make_async_remote_copy(
+            src_ref=self.acc.at[1, slot, pl.ds(self.starts[1], self.counts[1])],
+            dst_ref=self.crossbuf.at[slot],
+            send_sem=self.cross_s.at[slot],
+            recv_sem=self.cross_r.at[slot],
+            device_id=self.a.across,
+            device_id_type=pl.DeviceIdType.MESH,
+        )
+
+    def add(self, into, more):
+        into[...] = (into[...].astype(f32) + more[...].astype(f32)).astype(bf16)
+
+    def settle(self, slot):
+        for other in range(2):
+            self.handed(slot, other).wait_recv()
+            self.add(self.acc.at[other, slot], self.own.at[slot % 2, other])
+        self.over(slot).start()
+
+    def produce(self, slot, carry):
+        @pl.when(slot >= 2)
+        def _():
+            for other in range(2):
+                self.handed(slot - 2, other).wait_send()
+
+        rows, half = self.rows, self.half
+        model = self.w.shape[1]
+        columns = pl.ds(pl.multiple_of(slot * 2 * rows, 2 * rows), 2 * rows)
+        y = down(self.lhs[:, columns], self.w[...])
+        spots = [(other, place, into) for other in range(2) for place, into in ((0, self.own), (half, self.out))]
+        for other, place, into in spots:
+            start = other * rows + place
+            into[slot % 2, other, :, :model] = y[start : start + half].astype(bf16)
+        if self.ends is not None:
+            dg_ref, place_ref = self.ends
+            ends = down(dg_ref[:, columns], place_ref[...])[:, model % 128 :].astype(bf16)
+            for other, place, into in spots:
+                start = other * rows + place
+                into[slot % 2, other, :, model:] = ends[start : start + half]
+        for other in range(2):
+            self.handed(slot, other).start()
+
+        @pl.when(slot >= 1)
+        def _():
+            self.settle(slot - 1)
+
+        return carry
+
+    def make(self, upto):
+        upto = min(upto, self.a.size)
+        if upto > self.made:
+            lax.fori_loop(self.made, upto, self.produce, 0)
+            self.made = upto
+
+    def part(self, other, j, piece):
+        return self.acc.at[other, self.slot_of[j], pl.ds(self.starts[piece], self.counts[piece])]
+
+    def join(self, j):
+        if j not in self.joined:
+            self.joined.add(j)
+            self.over(self.slot_of[j]).wait_recv()
+            self.add(self.part(0, j, 1), self.crossbuf.at[self.slot_of[j]])
+
+    def begin(self):
+        self.make(2)
+        self.leave(0, 0)
+        self.make(3)
+        self.leave(1, 0)
+        self.leave(0, 1)
+        self.make(4)
+        self.leave(2, 0)
+        self.leave(1, 1)
+        self.leave(2, 1)
+
+    def leave(self, slot, piece):
+        for item, (part, other, right, left) in enumerate(self.items):
+            for way, d in ((0, right), (1, left)):
+                j = d if way == 0 else self.a.size - d
+                if part == piece and self.slot_of[j] == slot:
+                    if piece == 1:
+                        self.join(j)
+                    self.send(item, way, d, self.part(other, j, piece))
+
+    def send(self, item, way, d, block):
+        copy = remote(
+            block, self.arrived(item, way, d - 1), self.ring_s.at[item, way, d - 1],
+            self.ring_r.at[item, way, d - 1], self.a.right if way == 0 else self.a.left,
+        )
+        self.ring[item, way, d - 1] = copy
+        self.sent.append(copy)
+
+    def step(self, k):
+        a = self.a
+        for item, (piece, other, right, left) in enumerate(self.items):
+            for way, hops in ((0, right), (1, left)):
+                d = hops - k
+                if d < 1:
+                    continue
+                j = d if way == 0 else a.size - d
+                if piece == 1:
+                    self.join(j)
+                block = self.part(other, j, piece)
+                self.ring[item, way, d].wait_recv()
+                self.add(block, self.arrived(item, way, d))
+                self.send(item, way, d, block)
+
+    def finish(self):
+        a, size = self.a, self.a.size
+        last = []
+        for item, (piece, other, _, _) in enumerate(self.items):
+            if piece == 1:
+                self.join(0)
+            block = self.part(other, 0, piece)
+            for way in range(2):
+                self.ring[item, way, 0].wait_recv()
+                self.add(block, self.arrived(item, way, 0))
+            if other:
+                final = remote(block, self.lastbuf, self.cross_s.at[size], self.cross_r.at[size], a.across)
+                self.sent.append(final)
+            else:
+                last.append((piece, block))
+        outs = []
+        for piece, block in sorted(last, key=lambda entry: -entry[0]):
+            if piece == 0:
+                final.wait_recv()
+                self.add(block, self.lastbuf)
+            start = pl.multiple_of(a.core * self.half + self.starts[piece], 16)
+            where = self.o.at[pl.ds(start, self.counts[piece])]
+            where[...] = block[...]
+            outs.append(remote(where, where, self.out_s.at[piece], self.out_r.at[piece], a.sibling))
+        for copy in outs:
+            copy.wait()
+        for copy in self.sent:
+            copy.wait_send()
+        for slot in range(size):
+            self.over(slot).wait_send()
+        for slot in range(size - 2, size):
+            for other in range(2):
+                self.handed(slot, other).wait_send()
+
+
+def expert_kernel_all(
+    size, units, model, experts,
+    x_ref, dy_all, wt_ref, wd_ref, bias_ref, bd_ref,
+    x_all, act_all, dgu_all, extra_all, o_ref, gbias_ref,
+    xbuf, dybuf, wt, wd, act_buf, dgu_buf, dg_ref, pick_ref, place_ref, load_s, dy_s, keep_s, *scratch,
 ):
     a = Around(size)
+    tail = model // 128 * 128
+    few = len(UnitGather.semaphores(size))
+    gather = UnitGather(a, x_ref, xbuf, scratch[:few], x_ref.shape[0] // 8)
+    total = UnitSum(
+        a, x_ref.shape[0], dgu_buf, wt, (dg_ref, place_ref), o_ref, scratch[few:], x_ref.shape[0] // 4
+    )
+    lane = lax.broadcasted_iota(jnp.int32, pick_ref.shape, 1) + tail - model
+    line = lax.broadcasted_iota(jnp.int32, pick_ref.shape, 0)
+    wanted = (lane == a.ctx) | (lane == experts + a.ctx)
+    pick_ref[...] = jnp.where((line == 0) & wanted, 1.0, 0.0).astype(bf16)
+    lane = lax.broadcasted_iota(jnp.int32, place_ref.shape, 1) + tail - model
+    line = lax.broadcasted_iota(jnp.int32, place_ref.shape, 0)
+    column = 2 * (4 * a.ctx + 2 * a.seq + a.core)
+    place_ref[...] = jnp.where((line < 2) & (lane == column + line), 1.0, 0.0).astype(bf16)
     rows = x_ref.shape[0]
-    half, chunk = rows // 2, rows // 4
-    far, near = size // 2, size - 1 - size // 2
-    items = [(1, 0, far, near), (0, 0, near, far), (0, 1, far, near)]
-    slot_of = unit_slots(size)
-    tail = model // 128 * 128
+    wide = x_ref.shape[1]
+    slot_of = gather.slot_of
 
     loads = [
         pltpu.make_async_copy(wt_ref, wt, load_s.at[0]),
         pltpu.make_async_copy(wd_ref, wd.at[pl.ds(0, units)], load_s.at[1]),
     ]
+    greet([a.right, a.left, a.sibling, a.across])
+    gather.start()
+
+    def fetch(js):
+        for j in js:
+            slot = slot_of[j]
+            copy = pltpu.make_async_copy(dy_all.at[slot], dybuf.at[slot % 2], dy_s.at[slot])
+            copy.start()
+            fetched[j] = copy
+
+    fetched = {}
     for copy in loads:
         copy.start()
-    wd[units:] = extra_ref[...]
+    fetch(gather.after(-1))
+    lead = jnp.where((a.seq == 0) & (a.core == 0), 1.0, 0.0)
+    bias = bd_ref[...] * lead
+    bias_high = bias.astype(bf16)
+    bias_low = (bias - bias_high.astype(f32)).astype(bf16)
+    wd[units:] = jnp.concatenate([bias_high, bias_low, bias_high] + [jnp.zeros_like(bias_high)] * 13, axis=0)
+    keep_extra = pltpu.make_async_copy(wd.at[pl.ds(units, 16)], extra_all, load_s.at[2])
+    keep_extra.start()
     gbias_ref[...] = jnp.zeros_like(gbias_ref)
-    greet([a.right, a.left, a.sibling, a.across])
-
-    def spot(j, other, core, piece):
-        return xbuf.at[slot_of[j], pl.ds(other * rows + core * half + piece * chunk, chunk)]
-
-    sent, ring, crossed, shared = [], {}, {}, {}
-
-    def hop(item, way, k, src):
-        piece, other, _, _ = items[item]
-        j = size - (k + 1) if way == 0 else k + 1
-        copy = remote(
-            src, spot(j, other, 0, piece), ring_s.at[item, way, k], ring_r.at[item, way, k],
-            a.right if way == 0 else a.left,
-        )
-        ring[item, way, k] = copy
-        sent.append(copy)
-
-    def cross(j, piece, src):
-        at = slot_of[j] if piece else size
-        copy = remote(src, spot(j, 1, 0, piece), cross_s.at[at], cross_r.at[at], a.across)
-        crossed[j, piece] = copy
-        sent.append(copy)
-
-    def share(j, other, piece):
-        at = (slot_of[j], other, piece)
-        copy = remote(
-            spot(j, other, 0, piece), spot(j, other, 1, piece), core_s.at[at], core_r.at[at], a.sibling
-        )
-        shared[j, other, piece] = copy
-        sent.append(copy)
-
-    def own(core, piece, count):
-        return x_ref.at[rows_at(core * half + piece * chunk, count)]
-
-    mine = [
-        pltpu.make_async_copy(
-            own(a.core if here == 0 else 1 - a.core, 0, half),
-            xbuf.at[slot_of[0], pl.ds(here * half, half)],
-            load_s.at[2 + here],
-        )
-        for here in range(2)
-    ]
-    for copy in mine:
-        copy.start()
-    cross(0, 0, own(a.core, 0, chunk))
-    for item in range(2):
-        for way in range(2):
-            hop(item, way, 0, own(a.core, items[item][0], chunk))
-    cross(0, 1, own(a.core, 1, chunk))
 
     def unit(slot, carry):
         x = xbuf[slot, :, :model]
-        dy = xbuf[slot, :, wide : wide + model]
+        dy = dybuf[lax.rem(slot, 2), :, :model]
         ends = xbuf[slot, :, tail:wide]
         columns = pl.ds(pl.multiple_of(slot * 2 * rows, 2 * rows), 2 * rows)
         gate_row = across(pick_ref[...], ends)[:1]
-        gate = clamp_limit * jnp.tanh((across(wt[:units], x) + bias_ref[:units]) / clamp_limit)
-        up = clamp_limit * jnp.tanh((across(wt[units:], x) + bias_ref[units:]) / clamp_limit)
-        squash = jax.nn.sigmoid(glu_alpha * gate)
-        swish = gate * squash
-        act = (up + 1.0) * swish
+        gate_tanh = jnp.tanh((across(wt[:units], x) + bias_ref[:units]) * (1.0 / clamp_limit))
+        up_tanh = jnp.tanh((across(wt[units:], x) + bias_ref[units:]) * (1.0 / clamp_limit))
+        squash = 0.5 + 0.5 * jnp.tanh((0.5 * glu_alpha * clamp_limit) * gate_tanh)
+        swish = clamp_limit * gate_tanh * squash
+        up = clamp_limit * up_tanh + 1.0
+        act = up * swish
         act_grad = across(wd[...], dy)
         bias_dot = act_grad[units : units + 1] + act_grad[units + 1 : units + 2]
         act_grad = act_grad[:units]
         gate_grad = jnp.sum(act * act_grad, axis=0, keepdims=True) + bias_dot
         gate_grad = jnp.where(gate_row > 0, gate_grad, 0.0)
         act_grad = act_grad * gate_row
-        slope = 1.0 - (gate / clamp_limit) * (gate / clamp_limit)
-        dgate = (
-            act_grad * (up + 1.0) * (squash + glu_alpha * swish * (1.0 - squash)) * slope
-        ).astype(bf16)
-        dup = (act_grad * swish * (1.0 - (up / clamp_limit) * (up / clamp_limit))).astype(bf16)
+        slope = (squash + glu_alpha * swish * (1.0 - squash)) * (1.0 - gate_tanh * gate_tanh)
+        dgate = (act_grad * up * slope).astype(bf16)
+        dup = (act_grad * swish * (1.0 - up_tanh * up_tanh)).astype(bf16)
         dgu_buf[:units, columns] = dgate
         dgu_buf[units:, columns] = dup
         gbias_ref[:units] += jnp.sum(dgate.astype(f32), axis=1, keepdims=True)
@@ -846,16 +1105,9 @@
     kept = []
 
     def compute(js):
+        gather.collect(js)
         for j in js:
-            if j == 0:
-                for copy in mine:
-                    copy.wait()
-            else:
-                crossed[j, 1].wait_recv()
-                share(j, 1, 1)
-            for key in [(j, 0, 0), (j, 0, 1), (j, 1, 0), (j, 1, 1)]:
-                if key in shared:
-                    shared[key].wait_recv()
+            fetched[j].wait()
         slots = [slot_of[j] for j in js]
         lax.fori_loop(slots[0], slots[-1] + 1, unit, 0)
         for slot in slots:
@@ -871,345 +1123,113 @@
                 copy.start()
                 kept.append(copy)
 
-    crossed[0, 0].wait_recv()
-    for way in range(2):
-        hop(2, way, 0, spot(0, 1, 0, 0))
-    share(0, 1, 0)
-    crossed[0, 1].wait_recv()
-    share(0, 1, 1)
+    gather.first()
     for copy in loads:
         copy.wait()
-    ready = [0]
     for k in range(size // 2):
-        compute(ready)
-        for item, (piece, other, right, left) in enumerate(items):
-            for way, hops in ((0, right), (1, left)):
-                if k >= hops:
-                    continue
-                ring[item, way, k].wait_recv()
-                j = size - (k + 1) if way == 0 else k + 1
-                if k + 1 < hops:
-                    hop(item, way, k + 1, spot(j, other, 0, piece))
-                if item == 0:
-                    cross(j, 1, spot(j, 0, 0, 1))
-                share(j, other, piece)
-        ready = [k + 1] if 2 * (k + 1) == size else [k + 1, size - (k + 1)]
-    compute(ready)
-    for copy in sent:
-        copy.wait_send()
+        gather.step(k)
+        compute(gather.after(k - 1))
+        fetch(gather.after(k))
+    compute(gather.after(size // 2 - 1))
+    total.begin()
+    gather.finish()
+    total.make(6)
+    for k in range(1, size // 2):
+        if k == size // 2 - 1:
+            total.settle(size - 1)
+        total.step(k)
+        total.make(6 + 2 * k)
+    total.finish()
     for copy in kept:
         copy.wait()
-
-
-def expert_in(x, wt, wd, bias, extra, pick, model, wide, size, ident):
-    rows, width = x.shape
-    units = wd.shape[0]
-    deep = units + extra.shape[0]
+    keep_extra.wait()
+
+
+def expert_all(x, dy, wt, wd, bias, bd, experts, width, size, ident):
+    rows, wide = x.shape
+    units, model = wd.shape
+    deep = units + 16
     count = 2 * size * rows
+    tail = model // 128 * 128
     dma = pltpu.SemaphoreType.DMA
     hbm = pl.BlockSpec(memory_space=pl.ANY)
     vmem = pl.BlockSpec(memory_space=pltpu.VMEM)
     return pl.pallas_call(
-        functools.partial(expert_in_kernel, size, units, model, wide),
+        functools.partial(expert_kernel_all, size, units, model, experts),
         out_shape=(
-            jax.ShapeDtypeStruct((size, 2 * rows, width), bf16),
+            jax.ShapeDtypeStruct((size, 2 * rows, wide), bf16),
             jax.ShapeDtypeStruct((deep, count), bf16),
             jax.ShapeDtypeStruct((2 * units, count), bf16),
-            jax.ShapeDtypeStruct((16, count), bf16),
+            jax.ShapeDtypeStruct((16, model), bf16),
+            jax.ShapeDtypeStruct((rows, width), bf16),
             jax.ShapeDtypeStruct((2 * units, 1), f32),
         ),
-        in_specs=[hbm, hbm, hbm, vmem, vmem, vmem],
-        out_specs=(hbm, hbm, hbm, vmem, vmem),
+        in_specs=[hbm, hbm, hbm, hbm, vmem, vmem],
+        out_specs=(hbm, hbm, hbm, hbm, vmem, vmem),
         scratch_shapes=[
-            pltpu.VMEM((size, 2 * rows, width), bf16),
+            pltpu.VMEM((size, 2 * rows, wide), bf16),
+            pltpu.VMEM((2,) + dy.shape[1:], bf16),
             pltpu.VMEM((2 * units, model), bf16),
             pltpu.VMEM((deep, model), bf16),
             pltpu.VMEM((deep, count), bf16),
             pltpu.VMEM((2 * units, count), bf16),
-            dma((4,)),
-            dma((3, 2, size // 2)),
-            dma((3, 2, size // 2)),
-            dma((size + 1,)),
-            dma((size + 1,)),
-            dma((size, 2, 2)),
-            dma((size, 2, 2)),
+            pltpu.VMEM((16, count), bf16),
+            pltpu.VMEM((16, wide - tail), bf16),
+            pltpu.VMEM((16, width - tail), bf16),
+            dma((3,)),
+            dma((size,)),
             dma((3, size)),
-        ],
+        ]
+        + UnitGather.semaphores(size)
+        + UnitSum.scratch(size, rows, width, rows // 4),
         compiler_params=pltpu.CompilerParams(
             collective_id=ident, has_side_effects=True, vmem_limit_bytes=vmem_most
         ),
-        name="expert_in",
-    )(x, wt, wd, bias, extra, pick)
-
-
-def expert_out_kernel(
-    size, rows, units, model, start, tiles, more, *refs,
-):
-    if more:
-        lhs_ref, w_ref, x_ref, dg_ref, place_ref, o_ref, grad_ref, *refs = refs
-    else:
-        lhs_ref, w_ref, x_ref, extra_ref, o_ref, grad_ref, grad_extra, *refs = refs
-    (
-        lhs, w, x, acc, own, out, ringbuf, crossbuf, lastbuf, tile,
-        load_s, ring_s, ring_r, cross_s, cross_r, core_s, core_r, out_s, out_r, tile_s,
-    ) = refs
-    a = Around(size)
-    half, chunk = rows // 2, rows // 4
-    far, near = size // 2, size - 1 - size // 2
-    items = [(0, 1, far, near), (0, 0, near, far), (1, 0, far, near)]
-    slot_of = unit_slots(size)
-    tail = model // 128 * 128
-    step_rows = units // tiles
-
-    loads = [
-        pltpu.make_async_copy(w_ref, w.at[pl.ds(0, units)], load_s.at[0]),
-        pltpu.make_async_copy(lhs_ref, lhs, load_s.at[1]),
-        pltpu.make_async_copy(
-            x_ref.at[:, :, pl.ds(start, x.shape[2])], x, load_s.at[2]
+        name="expert_all",
+    )(x, dy, wt, wd, bias, bd)
+
+
+def weights_kernel(model, first_ref, second_ref, x_ref, dy_ref, one_ref, two_ref, extra_ref):
+    units = two_ref.shape[0]
+    one_ref[...] = jnp.dot(first_ref[...], x_ref[...], preferred_element_type=f32)
+    both = jnp.dot(second_ref[...], dy_ref[...], preferred_element_type=f32)
+    two_ref[...] = both[:units]
+    extra_ref[...] = both[units : units + 1] + both[units + 2 : units + 3]
+
+
+def weight_gradients(first, second, x, dy, model, units):
+    count = x.shape[0]
+    cols = 384
+    col = lambda i: (0, i)
+    fixed = lambda i: (0, 0)
+    once = pl.Buffered(1)
+    return pl.pallas_call(
+        functools.partial(weights_kernel, model),
+        grid=(-(-model // cols),),
+        out_shape=(
+            jax.ShapeDtypeStruct((first.shape[0], model), f32),
+            jax.ShapeDtypeStruct((units, model), f32),
+            jax.ShapeDtypeStruct((1, model), f32),
         ),
-    ]
-    for copy in loads:
-        copy.start()
-    if not more:
-        w[units:] = extra_ref[...]
-    greet([a.right, a.left, a.sibling, a.across])
-    for copy in loads[:2]:
-        copy.wait()
-
-    def handed(slot, other):
-        return pltpu.make_async_remote_copy(
-            src_ref=out.at[slot % 2, other],
-            dst_ref=acc.at[other, slot],
-            send_sem=core_s.at[other, slot],
-            recv_sem=core_r.at[other, slot],
-            device_id=a.sibling,
-            device_id_type=pl.DeviceIdType.MESH,
-        )
-
-    def over(slot):
-        return pltpu.make_async_remote_copy(
-            src_ref=acc.at[1, slot, pl.ds(chunk, chunk)],
-            dst_ref=crossbuf.at[slot],
-            send_sem=cross_s.at[slot],
-            recv_sem=cross_r.at[slot],
-            device_id=a.across,
-            device_id_type=pl.DeviceIdType.MESH,
-        )
-
-    def add(into, other):
-        into[...] = (into[...].astype(f32) + other[...].astype(f32)).astype(bf16)
-
-    def settle(slot):
-        for other in range(2):
-            handed(slot, other).wait_recv()
-            add(acc.at[other, slot], own.at[slot % 2, other])
-        over(slot).start()
-
-    def produce(slot, carry):
-        @pl.when(slot >= 2)
-        def _():
-            for other in range(2):
-                handed(slot - 2, other).wait_send()
-
-        columns = pl.ds(pl.multiple_of(slot * 2 * rows, 2 * rows), 2 * rows)
-        y = down(lhs[:, columns], w[...])
-        for other in range(2):
-            for place, into in ((0, own), (half, out)):
-                part = y[other * rows + place : other * rows + place + half]
-                into[slot % 2, other, :, :model] = part.astype(bf16)
-        if more:
-            ends = down(dg_ref[:, columns], place_ref[...])[:, model - tail :].astype(bf16)
-            for other in range(2):
-                for place, into in ((0, own), (half, out)):
-                    part = ends[other * rows + place : other * rows + place + half]
-                    into[slot % 2, other, :, model:] = part
-        for other in range(2):
-            handed(slot, other).start()
-
-        @pl.when(slot >= 1)
-        def _():
-            settle(slot - 1)
-
-        return carry
-
-    def tile_copy(i):
-        return pltpu.make_async_copy(
-            tile.at[i % 2], grad_ref.at[pl.ds(pl.multiple_of(i * step_rows, 16), step_rows)], tile_s.at[i % 2]
-        )
-
-    def weight_grad(i, carry):
-        @pl.when(i >= 2)
-        def _():
-            tile_copy(i - 2).wait()
-
-        left = lhs[pl.ds(pl.multiple_of(i * step_rows, 16), step_rows)]
-        total = None
-        for at in range(size):
-            piece = jnp.dot(
-                left[:, at * 2 * rows : (at + 1) * 2 * rows], x[at, :, :model], preferred_element_type=f32
-            )
-            total = piece if total is None else total + piece
-        tile[i % 2] = total
-        tile_copy(i).start()
-        return carry
-
-    ring, sent = {}, []
-
-    def part(other, j, piece):
-        return acc.at[other, slot_of[j], pl.ds(piece * chunk, chunk)]
-
-    joined = set()
-
-    def join(j):
-        if j not in joined:
-            joined.add(j)
-            over(slot_of[j]).wait_recv()
-            add(part(0, j, 1), crossbuf.at[slot_of[j]])
-
-    def step(k):
-        for item, (piece, other, right, left) in enumerate(items):
-            for way, hops in ((0, right), (1, left)):
-                d = hops - k
-                if d < 1:
-                    continue
-                j = d if way == 0 else size - d
-                if piece == 1:
-                    join(j)
-                block = part(other, j, piece)
-                if k > 0:
-                    ring[item, way, d].wait_recv()
-                    add(block, ringbuf.at[item, way, d])
-                copy = remote(
-                    block, ringbuf.at[item, way, d - 1], ring_s.at[item, way, d - 1],
-                    ring_r.at[item, way, d - 1], a.right if way == 0 else a.left,
-                )
-                ring[item, way, d - 1] = copy
-                sent.append(copy)
-
-    made, graded = [0], [0]
-
-    def make(upto):
-        lax.fori_loop(made[0], upto, produce, 0)
-        made[0] = upto
-
-    def grade(count):
-        upto = min(tiles, graded[0] + count)
-        if upto > graded[0]:
-            lax.fori_loop(graded[0], upto, weight_grad, 0)
-            graded[0] = upto
-
-    steps = size // 2
-    per = -(-tiles // steps)
-    make(4)
-    step(0)
-    make(min(6, size))
-    loads[2].wait()
-    for k in range(1, steps):
-        upto = min(size, 4 + 2 * (k + 1))
-        if k > 1 and made[0] < upto:
-            make(upto)
-        if k == steps - 1:
-            settle(size - 1)
-        if k == 1 and steps > 2:
-            grade(per)
-            step(k)
-            make(min(size, 8))
-            continue
-        grade(per)
-        step(k)
-    grade(tiles)
-
-    last = []
-    for item, (piece, other, _, _) in enumerate(items):
-        if piece == 1:
-            join(0)
-        block = part(other, 0, piece)
-        for way in range(2):
-            ring[item, way, 0].wait_recv()
-            add(block, ringbuf.at[item, way, 0])
-        if other:
-            final = remote(block, lastbuf, cross_s.at[size], cross_r.at[size], a.across)
-            sent.append(final)
-        else:
-            last.append((piece, block))
-    outs = []
-    for piece, block in sorted(last, key=lambda entry: -entry[0]):
-        if piece == 0:
-            final.wait_recv()
-            add(block, lastbuf)
-        where = o_ref.at[rows_at(a.core * half + piece * chunk, chunk)]
-        where[...] = block[...]
-        outs.append(remote(where, where, out_s.at[piece], out_r.at[piece], a.sibling))
-    if not more:
-        left = lhs[pl.ds(units, lhs.shape[0] - units)]
-        total = None
-        for at in range(size):
-            piece = jnp.dot(
-                left[:, at * 2 * rows : (at + 1) * 2 * rows], x[at, :, :model], preferred_element_type=f32
-            )
-            total = piece if total is None else total + piece
-        grad_extra[...] = total
-    for copy in outs:
-        copy.wait()
-    for copy in sent:
-        copy.wait_send()
-    for slot in range(size):
-        over(slot).wait_send()
-    for slot in range(size - 2, size):
-        for other in range(2):
-            handed(slot, other).wait_send()
-    for i in range(max(0, tiles - 2), tiles):
-        tile_copy(i).wait()
-
-
-def expert_out(lhs, w, x, start, tiles, size, ident, dg=None, place=None, extra=None):
-    units, model = w.shape
-    rows = x.shape[1] // 2
-    half, chunk = rows // 2, rows // 4
-    more = dg is not None
-    padded = -(-model // 128) * 128
-    width = model // 128 * 128 + place.shape[1] if more else model
-    dma = pltpu.SemaphoreType.DMA
-    hbm = pl.BlockSpec(memory_space=pl.ANY)
-    vmem = pl.BlockSpec(memory_space=pltpu.VMEM)
-    shapes = [
-        jax.ShapeDtypeStruct((rows, width), bf16),
-        jax.ShapeDtypeStruct((units, model), f32),
-    ]
-    if not more:
-        shapes.append(jax.ShapeDtypeStruct((extra.shape[0], model), f32))
-    return pl.pallas_call(
-        functools.partial(expert_out_kernel, size, rows, units, model, start, tiles, more),
-        out_shape=shapes,
-        in_specs=[hbm, hbm, hbm] + [vmem] * (2 if more else 1),
-        out_specs=[vmem, hbm] + ([] if more else [vmem]),
-        scratch_shapes=[
-            pltpu.VMEM(lhs.shape, bf16),
-            pltpu.VMEM((lhs.shape[0], model), bf16),
-            pltpu.VMEM((size, 2 * rows, padded), bf16),
-            pltpu.VMEM((2, size, half, width), bf16),
-            pltpu.VMEM((2, 2, half, width), bf16),
-            pltpu.VMEM((2, 2, half, width), bf16),
-            pltpu.VMEM((3, 2, size // 2, chunk, width), bf16),
-            pltpu.VMEM((size, chunk, width), bf16),
-            pltpu.VMEM((chunk, width), bf16),
-            pltpu.VMEM((2, units // tiles, model), f32),
-            dma((3,)),
-            dma((3, 2, size // 2)),
-            dma((3, 2, size // 2)),
-            dma((size + 1,)),
-            dma((size + 1,)),
-            dma((2, size)),
-            dma((2, size)),
-            dma((2,)),
-            dma((2,)),
-            dma((2,)),
+        in_specs=[
+            pl.BlockSpec(first.shape, fixed, pipeline_mode=once),
+            pl.BlockSpec(second.shape, fixed, pipeline_mode=once),
+            pl.BlockSpec((count, cols), col),
+            pl.BlockSpec((count, cols), col),
         ],
-        compiler_params=pltpu.CompilerParams(
-            collective_id=ident, has_side_effects=True, vmem_limit_bytes=vmem_most
+        out_specs=(
+            pl.BlockSpec((first.shape[0], cols), col),
+            pl.BlockSpec((units, cols), col),
+            pl.BlockSpec((1, cols), col),
         ),
-        name="expert_back" if more else "expert_out",
-    )(lhs, w, x, *((dg, place) if more else (extra,)))
+        compiler_params=pltpu.CompilerParams(vmem_limit_bytes=vmem_bytes),
+        cost_estimate=pl.CostEstimate(
+            flops=2 * count * (first.shape[0] + second.shape[0]) * model,
+            bytes_accessed=4 * (first.shape[0] + second.shape[0]) * model + 4 * count * model,
+            transcendentals=0,
+        ),
+        name="weight_gradients",
+    )(first, second, x, dy)
 
 
 def turn(x, cosine, sine):
@@ -1280,32 +1300,37 @@
         pl.when(block // per == level)(functools.partial(run, (level + 1) * per * rows))
 
 
+def attend_block(block, reach, heads, sink_ref, q, k_ref, v_ref):
+    rows = q.shape[0]
+    scale = 1.0 / math.sqrt(HEAD_DIMENSION)
+    keys, values = k_ref[:reach], v_ref[:reach]
+    row = block * rows + lax.broadcasted_iota(jnp.int32, (rows, reach), 0)
+    allowed = lax.broadcasted_iota(jnp.int32, (rows, reach), 1) <= row
+    outs, totals = [], []
+    for head in range(heads):
+        query = q[:, head * HEAD_DIMENSION : (head + 1) * HEAD_DIMENSION]
+        scores = jnp.where(allowed, across(query, keys) * scale, masked_score)
+        sink = sink_ref[0, head]
+        top = jnp.maximum(jnp.max(scores, axis=1, keepdims=True), sink)
+        weights = jnp.exp(scores - top)
+        total = jnp.sum(weights, axis=1, keepdims=True) + jnp.exp(sink - top)
+        mixed = jnp.dot(weights.astype(bf16), values, preferred_element_type=f32)
+        outs.append(mixed / total)
+        totals.append(top + jnp.log(total))
+    return jnp.concatenate(outs, axis=1), jnp.concatenate(totals, axis=1)
+
+
 def attend_kernel(heads, length, sink_ref, q_ref, k_ref, v_ref, w_ref, o_ref, low_ref, lse_ref, p_ref):
     rows = q_ref.shape[0]
     block = pl.program_id(0)
-    scale = 1.0 / math.sqrt(HEAD_DIMENSION)
 
     def run(reach):
-        keys, values = k_ref[:reach], v_ref[:reach]
-        row = block * rows + lax.broadcasted_iota(jnp.int32, (rows, reach), 0)
-        allowed = lax.broadcasted_iota(jnp.int32, (rows, reach), 1) <= row
-        outs, totals = [], []
-        for head in range(heads):
-            query = q_ref[:, head * HEAD_DIMENSION : (head + 1) * HEAD_DIMENSION]
-            scores = jnp.where(allowed, across(query, keys) * scale, masked_score)
-            sink = sink_ref[0, head]
-            top = jnp.maximum(jnp.max(scores, axis=1, keepdims=True), sink)
-            weights = jnp.exp(scores - top)
-            total = jnp.sum(weights, axis=1, keepdims=True) + jnp.exp(sink - top)
-            mixed = jnp.dot(weights.astype(bf16), values, preferred_element_type=f32)
-            outs.append(mixed / total)
-            totals.append(top + jnp.log(total))
-        joined = jnp.concatenate(outs, axis=1)
+        joined, totals = attend_block(block, reach, heads, sink_ref, q_ref[...], k_ref, v_ref)
         o_ref[...] = joined
         joined_low = joined.astype(bf16)
         low_ref[...] = joined_low
         p_ref[...] = across(joined_low, w_ref[...]).astype(bf16)
-        lse_ref[...] = jnp.concatenate(totals, axis=1)
+        lse_ref[...] = totals
 
     each_reach(block, rows, length, run)
 
@@ -1365,13 +1390,47 @@
     )(x, w)
 
 
+def attend_back_block(block, reach, heads, sink_ref, q, k_ref, v_ref, o, lses, do, dk_acc, dv_acc, sink_acc):
+    rows = q.shape[0]
+    scale = 1.0 / math.sqrt(HEAD_DIMENSION)
+    keys, values = k_ref[:reach], v_ref[:reach]
+    row = block * rows + lax.broadcasted_iota(jnp.int32, (rows, reach), 0)
+    allowed = lax.broadcasted_iota(jnp.int32, (rows, reach), 1) <= row
+    parts, sink_parts = [], []
+    key_sum = jnp.zeros((reach, HEAD_DIMENSION), f32)
+    value_sum = jnp.zeros((reach, HEAD_DIMENSION), f32)
+    for head in range(heads):
+        span = slice(head * HEAD_DIMENSION, (head + 1) * HEAD_DIMENSION)
+        query, grad = q[:, span], do[:, span]
+        lse = lses[:, head : head + 1]
+        delta = jnp.sum(grad.astype(f32) * o[:, span], axis=1, keepdims=True)
+        scores = jnp.where(allowed, across(query, keys) * scale, masked_score)
+        probs = jnp.exp(scores - lse)
+        value_sum = value_sum + down(probs.astype(bf16), grad)
+        score_grad = (probs * (across(grad, values) - delta)).astype(bf16)
+        parts.append(jnp.dot(score_grad, keys, preferred_element_type=f32) * scale)
+        key_sum = key_sum + down(score_grad, query)
+        share = jnp.exp(sink_ref[0, head] - lse) * delta
+        sink_parts.append(jnp.sum(share, axis=0, keepdims=True))
+    dk_acc[:reach] += key_sum * scale
+    dv_acc[:reach] += value_sum
+    sink_acc[...] -= jnp.concatenate(sink_parts, axis=1)
+    return jnp.concatenate(parts, axis=1)
+
+
+def turned_back(dk, dv, cosine, sine):
+    both = jnp.concatenate([dk, dv], axis=1)
+    turned = turn(both, cosine, -sine)
+    lane = lax.broadcasted_iota(jnp.int32, both.shape, 1)
+    return jnp.where(lane < HEAD_DIMENSION, turned, both)
+
+
 def attend_back_kernel(
     heads, length, sink_ref, q_ref, k_ref, v_ref, o_ref, lse_ref, do_ref, cos_ref, sin_ref,
     kcos_ref, ksin_ref, dq_ref, dkv_ref, dsink_ref, dk_acc, dv_acc, sink_acc,
 ):
     rows = q_ref.shape[0]
     block = pl.program_id(0)
-    scale = 1.0 / math.sqrt(HEAD_DIMENSION)
 
     @pl.when(block == 0)
     def _():
@@ -1380,40 +1439,18 @@
         sink_acc[...] = jnp.zeros_like(sink_acc)
 
     def run(reach):
-        keys, values = k_ref[:reach], v_ref[:reach]
-        row = block * rows + lax.broadcasted_iota(jnp.int32, (rows, reach), 0)
-        allowed = lax.broadcasted_iota(jnp.int32, (rows, reach), 1) <= row
-        parts, sink_parts = [], []
-        key_sum = jnp.zeros((reach, HEAD_DIMENSION), f32)
-        value_sum = jnp.zeros((reach, HEAD_DIMENSION), f32)
-        for head in range(heads):
-            span = slice(head * HEAD_DIMENSION, (head + 1) * HEAD_DIMENSION)
-            query, grad = q_ref[:, span], do_ref[:, span]
-            lse = lse_ref[:, head : head + 1]
-            delta = jnp.sum(grad.astype(f32) * o_ref[:, span], axis=1, keepdims=True)
-            scores = jnp.where(allowed, across(query, keys) * scale, masked_score)
-            probs = jnp.exp(scores - lse)
-            value_sum = value_sum + down(probs.astype(bf16), grad)
-            score_grad = (probs * (across(grad, values) - delta)).astype(bf16)
-            parts.append(jnp.dot(score_grad, keys, preferred_element_type=f32) * scale)
-            key_sum = key_sum + down(score_grad, query)
-            share = jnp.exp(sink_ref[0, head] - lse) * delta
-            sink_parts.append(jnp.sum(share, axis=0, keepdims=True))
-        dq = jnp.concatenate(parts, axis=1)
+        dq = attend_back_block(
+            block, reach, heads, sink_ref, q_ref[...], k_ref, v_ref, o_ref[...], lse_ref[...], do_ref[...],
+            dk_acc, dv_acc, sink_acc,
+        )
         wide = dq.shape[1]
         dq_ref[...] = turn(dq, spread(cos_ref[...], wide), -spread(sin_ref[...], wide)).astype(bf16)
-        dk_acc[:reach] += key_sum * scale
-        dv_acc[:reach] += value_sum
-        sink_acc[...] -= jnp.concatenate(sink_parts, axis=1)
 
     each_reach(block, rows, length, run)
 
     @pl.when(block == pl.num_programs(0) - 1)
     def _():
-        both = jnp.concatenate([dk_acc[...], dv_acc[...]], axis=1)
-        turned = turn(both, kcos_ref[...], -ksin_ref[...])
-        lane = lax.broadcasted_iota(jnp.int32, both.shape, 1)
-        dkv_ref[...] = jnp.where(lane < HEAD_DIMENSION, turned, both).astype(bf16)
+        dkv_ref[...] = turned_back(dk_acc[...], dv_acc[...], kcos_ref[...], ksin_ref[...]).astype(bf16)
         dsink_ref[...] = sink_acc[...]
 
 
@@ -1459,6 +1496,328 @@
     )(sinks, q, k, v, o, lse, do, cosine, sine, cosine, sine)
 
 
+def front_kernel(
+    size, heads, kv_of,
+    sink_ref, x_ref, wq_ref, kvw_ref, wt_ref, dy_ref, bias_ref, cos_ref, sin_ref,
+    q_ref, k_ref, v_ref, o_ref, low_ref, lse_ref, rows_all, w_all, dy_all, out_ref,
+    rows, send, blocks, w, part, dybuf, w_s, w_r, wx_s, wx_r, load_s, keep_s, *scratch,
+):
+    a = Around(size)
+    one, two = len(RingGather.semaphores(size, False)), len(UnitGather.semaphores(size))
+    ring = RingGather(a, False, x_ref, rows, *scratch[:one])
+    gather = UnitGather(a, dy_ref, dybuf, scratch[one : one + two], dy_ref.shape[0] // 8)
+    total = RingSum(a, False, part, out_ref, *scratch[one + two :])
+    length, model = rows.shape
+    weight_rows = wq_ref.shape[0]
+    width = heads * HEAD_DIMENSION
+    proj = width + 2 * HEAD_DIMENSION
+    count = 256
+    steps = length // count
+    order = []
+    for d in range(1, size // 2 + 1):
+        order += [d] if 2 * d == size else [d, size - d]
+    greet(ring.partners() + [a.across] + [a.at(d) for d in order if 1 < d < size - 1])
+    ring.start()
+
+    whole = weight_rows // 16 * 16
+    send[:, whole:] = jnp.zeros((size, send.shape[1] - whole, send.shape[2]), bf16)
+    for index in range(size):
+        span = slice(index * width, (index + 1) * width)
+        at = kv_of[index] * 2 * HEAD_DIMENSION
+        send[index, :weight_rows, :width] = wq_ref[:, span]
+        send[index, :weight_rows, width:proj] = kvw_ref[:, at : at + 2 * HEAD_DIMENSION]
+        send[index, :weight_rows, proj:] = wt_ref[:, span]
+    mine = a.seq * size + a.ctx
+    spans = (pl.ds(0, proj), pl.ds(proj, width))
+    sent, crossed = {}, {}
+
+    def start_part(h):
+        src = send.at[a.ctx, :, spans[h]]
+        crossed[h, 0] = remote(src, blocks.at[mine, :, spans[h]], wx_s.at[h, 0], wx_r.at[h, 0], a.across)
+        for d in order:
+            src = send.at[a.index(d), :, spans[h]]
+            sent[h, d] = remote(src, blocks.at[mine, :, spans[h]], w_s.at[h, d], w_r.at[h, d], a.at(d))
+
+    def pass_part(h, times):
+        for d in order:
+            if (h, d) not in crossed and times > 0:
+                sent[h, d].wait_recv()
+                block = blocks.at[a.seq * size + a.index(-d), :, spans[h]]
+                crossed[h, d] = remote(block, block, wx_s.at[h, d], wx_r.at[h, d], a.across)
+                times -= 1
+
+    def put_part(h):
+        pass_part(h, size)
+        for d in [0] + order:
+            crossed[h, d].wait_recv()
+        columns = slice(0, proj) if h == 0 else slice(proj, proj + width)
+        for i in range(2 * size):
+            w[i * weight_rows : (i + 1) * weight_rows, columns] = blocks[i, :weight_rows, columns]
+
+    start_part(0)
+    blocks[mine] = send[a.ctx]
+    for k in range(size // 2):
+        ring.step(k)
+        pass_part(0, 2)
+    start_part(1)
+    ring.finish()
+    gather.start()
+    keep_rows = pltpu.make_async_copy(rows, rows_all, load_s.at[0])
+    keep_rows.start()
+    put_part(0)
+
+    def project_step(i, carry):
+        span = pl.ds(pl.multiple_of(i * count, count), count)
+        y = jnp.dot(rows[span], w[:, :proj], preferred_element_type=f32) + bias_ref[...]
+        cosine, sine = cos_ref[span], sin_ref[span]
+        q_ref[span] = turn(y[:, :width], spread(cosine, width), spread(sine, width)).astype(bf16)
+        kv = y[:, width:]
+        k_ref[span] = turn(kv, cosine, sine)[:, :HEAD_DIMENSION].astype(bf16)
+        v_ref[span] = kv[:, HEAD_DIMENSION:].astype(bf16)
+        return carry
+
+    lax.fori_loop(0, steps // 2, project_step, 0)
+    gather.first()
+    pass_part(1, 2)
+    lax.fori_loop(steps // 2, steps, project_step, 0)
+    pass_part(1, 2)
+    gather.step(0)
+    for i in range(steps):
+        span = slice(i * count, (i + 1) * count)
+        joined, totals = attend_block(i, (i + 1) * count, heads, sink_ref, q_ref[span], k_ref, v_ref)
+        o_ref[span] = joined
+        low_ref[span] = joined.astype(bf16)
+        lse_ref[span] = totals
+        pass_part(1, 2)
+        if i == steps // 2:
+            gather.step(1)
+    put_part(1)
+    keep_w = pltpu.make_async_copy(w, w_all, load_s.at[1])
+    keep_w.start()
+
+    def out_step(i, carry):
+        span = pl.ds(pl.multiple_of(i * count, count), count)
+        part[span] = across(low_ref[span], w[:, proj:]).astype(bf16)
+        return carry
+
+    lax.fori_loop(0, steps, out_step, 0)
+    total.start()
+    total.step(0)
+    for k in range(1, size // 2):
+        if k + 1 < size // 2:
+            gather.step(k + 1)
+        total.step(k)
+    total.finish()
+    kept = []
+    for k in range(-1, size // 2):
+        js = gather.after(k)
+        gather.collect(js)
+        for j in js:
+            slot = gather.slot_of[j]
+            copy = pltpu.make_async_copy(dybuf.at[slot], dy_all.at[slot], keep_s.at[slot])
+            copy.start()
+            kept.append(copy)
+    gather.finish()
+    for copy in kept + [keep_rows, keep_w]:
+        copy.wait()
+    for copy in list(sent.values()) + list(crossed.values()):
+        copy.wait_send()
+
+
+def front(sinks, x, wq, kvw, wt, dy, bias, cosine, sine, heads, kv_of, padded, size, ident):
+    own, model = x.shape
+    length = size * own
+    width = heads * HEAD_DIMENSION
+    block = (padded, 2 * width + 2 * HEAD_DIMENSION)
+    dma = pltpu.SemaphoreType.DMA
+    hbm = pl.BlockSpec(memory_space=pl.ANY)
+    vmem = pl.BlockSpec(memory_space=pltpu.VMEM)
+    return pl.pallas_call(
+        functools.partial(front_kernel, size, heads, kv_of),
+        out_shape=(
+            jax.ShapeDtypeStruct((length, width), bf16),
+            jax.ShapeDtypeStruct((length, HEAD_DIMENSION), bf16),
+            jax.ShapeDtypeStruct((length, HEAD_DIMENSION), bf16),
+            jax.ShapeDtypeStruct((length, width), f32),
+            jax.ShapeDtypeStruct((length, width), bf16),
+            jax.ShapeDtypeStruct((length, heads), f32),
+            jax.ShapeDtypeStruct((length, model), bf16),
+            jax.ShapeDtypeStruct((model, block[1]), bf16),
+            jax.ShapeDtypeStruct((size, 2 * own, dy.shape[1]), bf16),
+            jax.ShapeDtypeStruct((own, model), bf16),
+        ),
+        in_specs=[pl.BlockSpec(memory_space=pltpu.SMEM), hbm, vmem, vmem, vmem, hbm, vmem, vmem, vmem],
+        out_specs=(vmem,) * 6 + (hbm, hbm, hbm, vmem),
+        scratch_shapes=[
+            pltpu.VMEM((length, model), bf16),
+            pltpu.VMEM((size,) + block, bf16),
+            pltpu.VMEM((2 * size,) + block, bf16),
+            pltpu.VMEM((model, block[1]), bf16),
+            pltpu.VMEM((length, model), bf16),
+            pltpu.VMEM((size, 2 * own, dy.shape[1]), bf16),
+            dma((2, size)),
+            dma((2, size)),
+            dma((2, size)),
+            dma((2, size)),
+            dma((2,)),
+            dma((size,)),
+        ]
+        + RingGather.semaphores(size, False)
+        + UnitGather.semaphores(size)
+        + RingSum.scratch(size, False, own, model, bf16),
+        compiler_params=pltpu.CompilerParams(
+            collective_id=ident, has_side_effects=True, vmem_limit_bytes=vmem_most
+        ),
+        name="attend_front",
+    )(sinks, x, wq, kvw, wt, dy, bias, cosine, sine)
+
+
+def rear_kernel(
+    size, heads, own_rows, weight_rows,
+    sink_ref, act_ref, wd_ref, extra_ref, da_ref, rows_ref, w_ref, q_ref, k_ref, v_ref, o_ref, low_ref, lse_ref,
+    cos_ref, sin_ref,
+    out_ref, back_ref, g_ref, gain_ref, bias_ref, dsink_ref,
+    act, wd, da, w, do, both, dk_acc, dv_acc, back, load_s, keep_s, *scratch,
+):
+    a = Around(size)
+    few = len(RingGather.semaphores(size, False))
+    gather = RingGather(a, False, da_ref, da, *scratch[:few])
+    total = UnitSum(a, own_rows, act, wd, None, out_ref, scratch[few:], own_rows // 8)
+    units = wd_ref.shape[0]
+    length, model = da.shape
+    width = heads * HEAD_DIMENSION
+    proj = width + 2 * HEAD_DIMENSION
+    count = 256
+    steps = length // count
+    blocks = 2 * size
+    loads = [
+        pltpu.make_async_copy(wd_ref, wd.at[pl.ds(0, units)], load_s.at[0]),
+        pltpu.make_async_copy(act_ref, act, load_s.at[1]),
+        pltpu.make_async_copy(w_ref, w, load_s.at[2]),
+    ]
+    greet([a.right, a.left, a.sibling, a.across])
+    gather.start()
+    for copy in loads:
+        copy.start()
+    wd[units:] = extra_ref[...]
+    dk_acc[...] = jnp.zeros_like(dk_acc)
+    dv_acc[...] = jnp.zeros_like(dv_acc)
+    dsink_ref[...] = jnp.zeros_like(dsink_ref)
+    low_rows = weight_rows // 16 * 16
+    g_ref[:, :, low_rows:] = jnp.zeros((2, size, g_ref.shape[2] - low_rows, g_ref.shape[3]), bf16)
+
+    def grad_step(i, carry):
+        span = pl.ds(pl.multiple_of(i * count, count), count)
+        do[span] = jnp.dot(da[span], w[:, proj:], preferred_element_type=f32).astype(bf16)
+        return carry
+
+    def attend_step(i):
+        span = slice(i * count, (i + 1) * count)
+        dq = attend_back_block(
+            i, (i + 1) * count, heads, sink_ref, q_ref[span], k_ref, v_ref, o_ref[span], lse_ref[span], do[span],
+            dk_acc, dv_acc, dsink_ref,
+        )
+        dq = turn(dq, spread(cos_ref[span], width), -spread(sin_ref[span], width))
+        both[span, :width] = dq.astype(bf16)
+
+    def back_copy(i):
+        span = pl.ds(pl.multiple_of(i * count, count), count)
+        return pltpu.make_async_copy(back.at[i % 2], back_ref.at[span], keep_s.at[i % 2])
+
+    def back_step(i, carry):
+        @pl.when(i >= 2)
+        def _():
+            back_copy(i - 2).wait()
+
+        span = pl.ds(pl.multiple_of(i * count, count), count)
+        back[i % 2] = across(both[span], w[:, :proj]).astype(bf16)
+        back_copy(i).start()
+        return carry
+
+    for copy in loads[:2]:
+        copy.wait()
+    for k in range(size // 2):
+        total.make(2 * (k + 1))
+        gather.step(k)
+    gather.finish()
+    total.settle(size - 1)
+    total.begin()
+    loads[2].wait()
+    lax.fori_loop(0, steps, grad_step, 0)
+    grad_out = down(da[...], low_ref[...]).astype(bf16)
+    again = pltpu.make_async_copy(rows_ref, da, load_s.at[3])
+    again.start()
+    for i in range(blocks):
+        g_ref[lax.rem(i // size + a.seq, 2), i % size, :weight_rows, proj:] = grad_out[i * weight_rows : (i + 1) * weight_rows]
+    todo = list(range(steps))
+    attend_step(todo.pop())
+    for k in range(1, size // 2):
+        total.step(k)
+        for _ in range(2 if k == 1 else 1):
+            if todo:
+                attend_step(todo.pop())
+                if not todo:
+                    turned = turned_back(dk_acc[...], dv_acc[...], cos_ref[...], sin_ref[...])
+                    both[:, width:] = turned.astype(bf16)
+                    lax.fori_loop(0, steps, back_step, 0)
+    bias_ref[...] = jnp.sum(both[...].astype(f32), axis=0, keepdims=True)
+    again.wait()
+    grad_in = down(da[...], both[...])
+    product = grad_in * w[:, :proj].astype(f32)
+    high = product.astype(bf16)
+    low = (product - high.astype(f32)).astype(bf16)
+    ones = jnp.ones((16, proj), bf16)
+    gain_ref[...] = (across(ones, high) + across(ones, low))[:1]
+    grad_in = grad_in.astype(bf16)
+    for i in range(blocks):
+        g_ref[lax.rem(i // size + a.seq, 2), i % size, :weight_rows, :proj] = grad_in[i * weight_rows : (i + 1) * weight_rows]
+    total.finish()
+    for i in range(max(0, steps - 2), steps):
+        back_copy(i).wait()
+
+
+def rear(sinks, act, wd, extra, da, rows, w, q, k, v, o, low, lse, cosine, sine, weight_rows, padded, size, ident):
+    length, width = q.shape
+    heads = width // HEAD_DIMENSION
+    own_rows, model = da.shape
+    proj = width + 2 * HEAD_DIMENSION
+    dma = pltpu.SemaphoreType.DMA
+    hbm = pl.BlockSpec(memory_space=pl.ANY)
+    vmem = pl.BlockSpec(memory_space=pltpu.VMEM)
+    return pl.pallas_call(
+        functools.partial(rear_kernel, size, heads, own_rows, weight_rows),
+        out_shape=(
+            jax.ShapeDtypeStruct((own_rows, model), bf16),
+            jax.ShapeDtypeStruct((length, model), bf16),
+            jax.ShapeDtypeStruct((2, size, padded, w.shape[1]), bf16),
+            jax.ShapeDtypeStruct((1, model), f32),
+            jax.ShapeDtypeStruct((1, proj), f32),
+            jax.ShapeDtypeStruct((1, heads), f32),
+        ),
+        in_specs=[pl.BlockSpec(memory_space=pltpu.SMEM), hbm, hbm, vmem, hbm, hbm, hbm] + [vmem] * 8,
+        out_specs=(vmem, hbm, vmem, vmem, vmem, vmem),
+        scratch_shapes=[
+            pltpu.VMEM(act.shape, bf16),
+            pltpu.VMEM((act.shape[0], model), bf16),
+            pltpu.VMEM((length, model), bf16),
+            pltpu.VMEM(w.shape, bf16),
+            pltpu.VMEM((length, width), bf16),
+            pltpu.VMEM((length, proj), bf16),
+            pltpu.VMEM((length, HEAD_DIMENSION), f32),
+            pltpu.VMEM((length, HEAD_DIMENSION), f32),
+            pltpu.VMEM((2, 256, model), bf16),
+            dma((4,)),
+            dma((2,)),
+        ]
+        + RingGather.semaphores(size, False)
+        + UnitSum.scratch(size, own_rows, model, own_rows // 8),
+        compiler_params=pltpu.CompilerParams(
+            collective_id=ident, has_side_effects=True, vmem_limit_bytes=vmem_most
+        ),
+        name="attend_rear",
+    )(sinks, act, wd, extra, da, rows, w, q, k, v, o, low, lse, cosine, sine)
+
+
 def rms_norm(row_block, gain_vec):
     return (
         row_block
@@ -1469,12 +1828,12 @@
 
 def rotary(length):
     half_size = HEAD_DIMENSION // 2
-    frequency = rope_base ** (-2.0 * jnp.arange(half_size, dtype=f32) / HEAD_DIMENSION)
-    angles = jnp.arange(length, dtype=f32)[:, None] * frequency[None, :]
-    cosine, sine = jnp.cos(angles), jnp.sin(angles)
+    frequency = rope_base ** (-2.0 * np.arange(half_size) / HEAD_DIMENSION)
+    angles = np.arange(length)[:, None] * frequency[None, :]
+    cosine, sine = np.cos(angles).astype(np.float32), np.sin(angles).astype(np.float32)
     return (
-        jnp.concatenate([cosine] * 4, axis=1),
-        jnp.concatenate([-sine, sine, -sine, sine], axis=1),
+        jnp.asarray(np.concatenate([cosine] * 4, axis=1)),
+        jnp.asarray(np.concatenate([-sine, sine, -sine, sine], axis=1)),
     )
 
 
@@ -1525,33 +1884,31 @@
     kv_of = [(index * heads) // group for index in range(ctx_size)]
     kv_mine = (ctx_rank * heads) // group
 
-    kv_split = key_value_weight.reshape(weight_rows, 2, kv_heads, HEAD_DIMENSION)
-    send = []
-    for index in range(ctx_size):
-        cols = slice(index * width, (index + 1) * width)
-        send.append(
-            jnp.concatenate(
-                [
-                    w_query[:, cols],
-                    kv_split[:, 0, kv_of[index]],
-                    kv_split[:, 1, kv_of[index]],
-                    w_out[cols].T,
-                ],
-                axis=1,
-            )
-        )
-    send = jnp.pad(jnp.stack(send), ((0, 0), (0, padded_rows - weight_rows), (0, 0)))
-
     residual = tokens.astype(f32)
     normed_attn, attn_norm_back = jax.vjp(rms_norm, residual, gain_attn)
     normed_low = normed_attn.astype(bf16)
     if kernels:
-        rows_all, weights = enter(normed_low, send, ctx_size, 1)
+        kv_cols = key_value_weight.reshape(weight_rows, 2, kv_heads, HEAD_DIMENSION)
+        kv_cols = jnp.transpose(kv_cols, (0, 2, 1, 3)).reshape(weight_rows, -1)
     else:
+        kv_split = key_value_weight.reshape(weight_rows, 2, kv_heads, HEAD_DIMENSION)
+        send = []
+        for index in range(ctx_size):
+            cols = slice(index * width, (index + 1) * width)
+            send.append(
+                jnp.concatenate(
+                    [
+                        w_query[:, cols],
+                        kv_split[:, 0, kv_of[index]],
+                        kv_split[:, 1, kv_of[index]],
+                        w_out[cols].T,
+                    ],
+                    axis=1,
+                )
+            )
+        send = jnp.pad(jnp.stack(send), ((0, 0), (0, padded_rows - weight_rows), (0, 0)))
         rows_all, weights = plain_enter(normed_low, send)
-    weights = weights[:, :weight_rows].reshape(model, 2 * width + 2 * HEAD_DIMENSION)
     proj_width = width + 2 * HEAD_DIMENSION
-    w_in, w_back = weights[:, :proj_width], weights[:, proj_width:]
 
     cosine, sine = rotary(length)
     bias = jnp.concatenate(
@@ -1562,9 +1919,19 @@
         ]
     )[None]
     sinks_mine = lax.dynamic_slice_in_dim(sinks, ctx_rank * heads, heads)[None]
-    query, keys, values = project(rows_all, w_in, bias, cosine, sine, heads)
-    attended, attended_low, log_total, out_part = attend(sinks_mine, query, keys, values, w_back)
-    attn_out = ring_sum(out_part, ctx_size, False, 2) if kernels else plain_sum(out_part, "ctx")
+    if kernels:
+        dy_wide = -(-model // 128) * 128
+        upstream_low = jnp.pad(cotangent, ((0, 0), (0, dy_wide - model)))
+        query, keys, values, attended, attended_low, log_total, rows_all, weights, dy_all, attn_out = front(
+            sinks_mine, normed_low, w_query, kv_cols, jnp.transpose(w_out), upstream_low, bias, cosine, sine, heads,
+            kv_of, padded_rows, ctx_size, 2,
+        )
+    else:
+        weights = weights[:, :weight_rows].reshape(model, 2 * width + 2 * HEAD_DIMENSION)
+        w_in, w_back = weights[:, :proj_width], weights[:, proj_width:]
+        query, keys, values = project(rows_all, w_in, bias, cosine, sine, heads)
+        attended, attended_low, log_total, out_part = attend(sinks_mine, query, keys, values, w_back)
+        attn_out = plain_sum(out_part, "ctx")
     hidden = residual + attn_out.astype(f32) + b_out
 
     normed_moe, moe_norm_back = jax.vjp(rms_norm, hidden, gain_moe)
@@ -1609,22 +1976,14 @@
         )
 
     if kernels:
-        dy_wide = -(-model // 128) * 128
-        payload = jnp.concatenate([payload, jnp.pad(cotangent, ((0, 0), (0, dy_wide - model)))], axis=1)
-        bias_high = lax.reduce_precision(lead * b_down, 8, 7)
-        bias_low = lead * b_down - bias_high
-        extra_rows = jnp.concatenate([bias_high, bias_low, bias_high, jnp.zeros((13, model), f32)]).astype(bf16)
-        rows_all_units, gated_act, proj_grad, dg_rows, gate_bias = expert_in(
-            payload, gate_up_rows, down_weight, b_gate_up[0].reshape(-1, 1), extra_rows, pick,
-            model, wide, ctx_size, 3,
+        moe_all, gated_act, proj_grad, extra_rows, back_rows, gate_bias = expert_all(
+            payload, dy_all, gate_up_rows, down_weight, b_gate_up[0].reshape(-1, 1), b_down, experts, back_wide,
+            ctx_size, 3,
         )
-        back_rows, gate_up_grad = expert_out(
-            proj_grad, gate_up_rows, rows_all_units, 0, 5, ctx_size, 4, dg=dg_rows, place=place
+        count = blocks * tok_rows
+        gate_up_grad, down_grad, down_bias = weight_gradients(
+            proj_grad, gated_act, moe_all.reshape(count, -1), dy_all.reshape(count, -1), model, units
         )
-        expert_out_sum, down_grad, down_extra = expert_out(
-            gated_act, down_weight, rows_all_units, wide, 3, ctx_size, 5, extra=extra_rows
-        )
-        down_bias = down_extra[0:1] + down_extra[2:3]
     else:
         pieces = blocks * tok_rows // math.gcd(blocks * tok_rows, 2048)
 
@@ -1648,15 +2007,13 @@
     grad_b_gate_up = gate_bias.reshape(1, 2, units)
     grad_w_down = down_grad[None]
     grad_b_down = down_bias
-    mixed = (hidden + expert_out_sum.astype(f32)).astype(bf16)
-
     upstream = cotangent.astype(f32)
     gate_grad = back_rows[:, model : model + 2 * splits * experts].astype(f32)
     gate_grad = jnp.sum(gate_grad.reshape(tok_rows, experts, 2 * splits), axis=-1)
     gate_grad = jnp.sum(onehot * gate_grad[:, None], axis=-1)
     chosen_grad = gates * (gate_grad - jnp.sum(gates * gate_grad, axis=1, keepdims=True))
     logit_grad = jnp.sum(onehot * chosen_grad[..., None], axis=1).astype(bf16)
-    grad_w_router = project_grad(moe_input, logit_grad)
+    grad_w_router = project_grad(logit_grad, moe_input)
     grad_b_router = jnp.sum(logit_grad, axis=0, dtype=f32)
     moe_grad = back_rows[:, :model].astype(f32) + across(logit_grad, w_router)
     hidden_norm_grad, grad_gain_moe = moe_norm_back(moe_grad)
@@ -1664,70 +2021,88 @@
     branch_grad = hidden_grad.astype(bf16)
     grad_b_out = jnp.sum(branch_grad, axis=0, dtype=f32)
     if kernels:
-        branch_all = ring_gather(branch_grad, ctx_size, 6)
+        expert_out_sum, input_rows, grads, gain_part, bias_part, dsinks = rear(
+            sinks_mine, gated_act, down_weight, extra_rows, branch_grad, rows_all, weights, query, keys, values,
+            attended, attended_low, log_total, cosine, sine, weight_rows, padded_rows, ctx_size, 5,
+        )
+        gain_part = gain_part[0] / gain_attn
+        sum_q, sum_kv = bias_part[0, :width], bias_part[0, width:].reshape(2, HEAD_DIMENSION)
     else:
         branch_all = lax.all_gather(branch_grad, "ctx", axis=0, tiled=True)
-
-    out_grad = jnp.dot(branch_all, w_back, preferred_element_type=f32).astype(bf16)
-    dq, dkv, dsinks = attend_back(
-        sinks_mine, query, keys, values, attended, log_total, out_grad, cosine, sine
-    )
-    both = jnp.concatenate([dq, dkv], axis=1)
-    input_rows = spread_rows(both, w_in)
-    grad_in = project_grad(rows_all, both)
-    grad_out = project_grad(branch_all, attended_low)
-    gain_part = jnp.sum(grad_in * w_in.astype(f32), axis=1) / gain_attn
-    grads = jnp.concatenate([grad_in, grad_out], axis=1).astype(bf16).reshape(blocks, weight_rows, -1)
-    grads = jnp.pad(grads, ((0, 0), (0, padded_rows - weight_rows), (0, 0)))
-
-    sum_q = jnp.sum(dq, axis=0, dtype=f32)
-    sum_kv = jnp.sum(dkv, axis=0, dtype=f32).reshape(2, HEAD_DIMENSION)
+        out_grad = jnp.dot(branch_all, w_back, preferred_element_type=f32).astype(bf16)
+        dq, dkv, dsinks = attend_back(
+            sinks_mine, query, keys, values, attended, log_total, out_grad, cosine, sine
+        )
+        both = jnp.concatenate([dq, dkv], axis=1)
+        input_rows = spread_rows(both, w_in)
+        grad_in = project_grad(rows_all, both)
+        grad_out = project_grad(branch_all, attended_low)
+        gain_part = jnp.sum(grad_in * w_in.astype(f32), axis=1) / gain_attn
+        grads = jnp.concatenate([grad_in, grad_out], axis=1).astype(bf16).reshape(blocks, weight_rows, -1)
+        grads = jnp.pad(grads, ((0, 0), (0, padded_rows - weight_rows), (0, 0)))
+        sum_q = jnp.sum(dq, axis=0, dtype=f32)
+        sum_kv = jnp.sum(dkv, axis=0, dtype=f32).reshape(2, HEAD_DIMENSION)
+    mixed = (hidden + expert_out_sum.astype(f32)).astype(bf16)
+
     at_q = lax.dynamic_update_slice_in_dim(jnp.zeros_like(b_query), sum_q, ctx_rank * width, 0)
     at_kv = lax.dynamic_update_slice_in_dim(
         jnp.zeros_like(key_value_bias), sum_kv, kv_mine * HEAD_DIMENSION, 1
     )
     at_sinks = lax.dynamic_update_slice_in_dim(jnp.zeros_like(sinks), dsinks[0], ctx_rank * heads, 0)
-    parts = (gain_part, grad_gain_moe, grad_b_out, grad_w_router, grad_b_router, at_q, at_kv, at_sinks)
-    packed, starts = [], []
-    for part in parts:
-        flat = part.reshape(-1)
-        starts.append(sum(piece.shape[0] for piece in packed))
-        packed.append(jnp.pad(flat, (0, -flat.shape[0] % 1024)))
-    shared = packed[0].shape[0] // 128
-    small = jnp.concatenate(packed).reshape(-1, 128)
+    aligned = lambda n: -(-n // 128) * 128
+    late, starts, at = [], [], 0
+    for part in (at_q, at_kv.reshape(-1), at_sinks, grad_b_router):
+        starts.append(at)
+        late.append(jnp.pad(part, (0, aligned(part.shape[0]) - part.shape[0])))
+        at += aligned(part.shape[0])
+    late = jnp.pad(jnp.concatenate(late), (0, model - at))
+    alike = jnp.concatenate([grad_gain_moe[None], grad_b_out[None], grad_w_router], axis=0)
+    halves = alike.shape[0] // 2
     if kernels:
-        normed_grad, owned, small = leave(input_rows, grads, small, shared, ctx_size, 7)
+        part = lax.dynamic_slice_in_dim(alike, tp_rank * halves, halves)
+        small = jnp.concatenate([gain_part[None], late[None], part], axis=0)
+        small = jnp.pad(small, ((0, -small.shape[0] % 8), (0, 0)))
+        normed_grad, kept, small = leave(input_rows, grads, small, halves, ctx_size, 7)
+        owned = lax.all_to_all(kept, "ctx", split_axis=0, concat_axis=0, tiled=True)
+        spans = [(0, 0)] + [(1, start) for start in starts] + [(2, 0), (3, 0), (4, 0)]
+        shapes = [(1, model)] + [(1, v.size) for v in (at_q, at_kv, at_sinks, grad_b_router)]
+        shapes += [(1, model), (1, model), (experts, model)]
+        grad_w_query, grad_kv, grad_wt, *sums = settle_gradients(
+            owned, small, width, weight_rows, kv_of, spans, shapes
+        )
+        grad_w_out = jnp.transpose(grad_wt)
+        grad_kv = grad_kv.reshape(weight_rows, kv_heads, 2, HEAD_DIMENSION)
+        grad_w_key_value = jnp.transpose(grad_kv, (0, 2, 1, 3)).reshape(weight_rows, 2, kv_width)
     else:
-        normed_grad, owned, small = plain_leave(input_rows, grads, small, shared)
-    small = small.reshape(-1)
-    sums = [
-        small[start : start + part.size].reshape(part.shape) for start, part in zip(starts, parts)
-    ]
+        small = jnp.concatenate([gain_part[None], late[None], alike], axis=0)
+        normed_grad, owned, small = plain_leave(input_rows, grads, small)
+        owned = owned[:, :weight_rows].astype(f32)
+        grad_w_query = jnp.transpose(owned[:, :, :width], (1, 0, 2)).reshape(weight_rows, -1)
+        grad_kv = owned[:, :, width:proj_width].reshape(kv_heads, -1, weight_rows, 2, HEAD_DIMENSION)
+        grad_w_key_value = jnp.transpose(jnp.sum(grad_kv, axis=1), (1, 2, 0, 3)).reshape(
+            weight_rows, 2, kv_width
+        )
+        grad_w_out = jnp.transpose(owned[:, :, proj_width:], (0, 2, 1)).reshape(-1, weight_rows)
+        sums = [small[0]]
+        sums += [small[1, at : at + v.size] for at, v in zip(starts, (at_q, at_kv, at_sinks, grad_b_router))]
+        sums += [small[2], small[3], small[4:]]
     tokens_norm_grad, _ = attn_norm_back(normed_grad.astype(f32))
     grad_tokens = (hidden_grad + tokens_norm_grad).astype(bf16)
-
-    owned = owned[:, :weight_rows].astype(f32)
-    grad_w_query = jnp.transpose(owned[:, :, :width], (1, 0, 2)).reshape(weight_rows, -1)
-    grad_kv = owned[:, :, width:proj_width].reshape(kv_heads, -1, weight_rows, 2, HEAD_DIMENSION)
-    grad_w_key_value = jnp.transpose(jnp.sum(grad_kv, axis=1), (1, 2, 0, 3)).reshape(
-        weight_rows, 2, kv_width
-    )
-    grad_w_out = jnp.transpose(owned[:, :, proj_width:], (0, 2, 1)).reshape(-1, weight_rows)
 
     return (
         mixed,
         grad_tokens,
-        sums[0],
+        sums[0].reshape(gain_attn.shape),
         grad_w_query,
-        sums[5],
+        sums[1].reshape(b_query.shape),
         grad_w_key_value,
-        sums[6],
-        sums[7],
+        sums[2].reshape(key_value_bias.shape),
+        sums[3].reshape(sinks.shape),
         grad_w_out,
-        sums[2],
-        sums[1],
-        sums[3],
-        sums[4],
+        sums[6].reshape(b_out.shape),
+        sums[5].reshape(gain_moe.shape),
+        jnp.transpose(sums[7]),
+        sums[4].reshape(b_router.shape),
         grad_w_gate_up,
         grad_b_gate_up,
         grad_w_down,

time: 720 us -> 533 us (0.74)
  Pallas kernels: 589 us -> 485 us
  local copies, waits for them, and re-layouts: 73.9 us -> 21.2 us
  matrix products: 20.3 us -> 2.85 us
  other arithmetic: 26.8 us -> 15.3 us
    pallas_call x11 -> x6, Pallas kernels: 589 us -> 485 us  [the longest x1 165 us: front(): pl.pallas_call(functools.partial(front_kernel, size, heads, kv_of), out_s...]
    unnamed x131 -> x73, local copies, waits for them, and re-layouts: 37.5 us -> 9.15 us
    slice x11 -> x2, local copies, waits for them, and re-layouts: 13.8 us -> 1.37 us  [the longest x1 0.7 us: on_device(): bias_part[0, width:].reshape(2, HEAD_DIMENSION)]
    dot_general x3 -> x1, matrix products: 11.3 us -> 0.2 us  [project_grad(): lax.dot_general(left, right, (((0,), (0,)), ((), ())), preferred_element_...]
  transfers between devices with their start and end apart: 0 -> 1, of which waited for: 0 -> 0; matrix products, arithmetic and copies ran while one was open for 0% -> 2% of each run, Pallas kernels for 0% -> 8%
where the time goes in v2:
time: 533 us; the launch traced here: 530 us
  Pallas kernels  485 us (91%)
  local copies, waits for them, and re-layouts  21.2 us (4%)
  other arithmetic  15.3 us (3%)
    pallas_call x1, Pallas kernels, front(): pl.pallas_call(functools.partial(front_kernel, size, heads, kv_of), out_s...  165 us
    pallas_call x1, Pallas kernels, expert_all(): pl.pallas_call(functools.partial(expert_kernel_all, size, units, model, e...  135 us
    pallas_call x1, Pallas kernels, rear(): pl.pallas_call(functools.partial(rear_kernel, size, heads, own_rows, weig...  83.9 us
    pallas_call x1, Pallas kernels, leave(): pl.pallas_call(functools.partial(leave_kernel, size, halves), out_shape=(...  52.5 us
    pallas_call x1, Pallas kernels, weight_gradients(): pl.pallas_call(functools.partial(weights_kernel, model), grid=(-(-model /...  44.5 us
  transfers between devices with their start and end apart: 1, of which 0 were waited for; matrix products, arithmetic and copies ran while one was open for 2% of the time, Pallas kernels for 8%

profile of v2, /device:TPU:0, one launch (start us, length us, event | category | flops | bytes accessed | tf_op | source)
XLA Modules:
  0.0 529.7 jit_solution(13311718864498019997)
XLA Ops:
  0.7 0.0 copy-start
  0.7 1.5 copy.96
  2.3 0.2 fusion.3
  2.5 0.0 copy-start.32
  2.5 0.0 copy-start.16
  2.6 0.2 copy.97
  2.8 0.8 copy.100.kvw_ref
  3.6 0.3 copy.99
  4.0 0.8 dynamic_slice.20
  4.8 0.1 fusion.13
  4.8 0.1 pad_maximum_fusion
  4.9 0.6 broadcast_in_dim.27.bias_ref
  5.5 0.6 dynamic-slice_bitcast_fusion.sink_ref
  6.1 1.1 fusion.5.x_ref
  7.2 0.9 pad.20.dy_ref
  8.1 165.3 %attend_front.1 = (bf16[1024,256]{1,0:T(8,128)(2,1)}, bf16[1024,64]{1,0:T(8,128)(2,1)}, bf16[1024,64]{1,0:T(8,128)(2,1)}, f32[1024,256]{1,0:T(8,128)}, bf16[1024...) custom-call(f32[1,4]{1,0:T(1,128)} %dynamic-slice_bitcast_fusion.sin, ...), custom_call_target="tpu_custom_call" | custom-call | tf_op jit(solution)/shard_map/attend_front/pallas_call | solution.py:1635
  173.5 1.6 multiply_reduce_fusion.2
  175.1 0.3 multiply_convert_fusion
  175.4 0.3 copy-done.31
  175.7 0.3 convolution_add_fusion.1
  176.1 0.1 copy.101
  176.2 0.1 copy.103
  176.3 0.1 copy.102
  176.5 1.2 reshape_squeeze.8.bias_ref
  177.7 1.0 concatenate.16.x_ref
  178.7 135.1 %expert_all.1 = (bf16[8,256,2944]{2,1,0:T(8,128)(2,1)}, bf16[736,2048]{1,0:T(8,128)(2,1)}, bf16[1440,2048]{1,0:T(8,128)(2,1)}, bf16[16,2880]{1,0:T(8,128)(2,1)},...) custom-call(bf16[128,2944]{1,0:T(8,128)(2,1)} %concatenate.16.x_ref, bf16[8,256,2944]{2,1,0:T(8,128)(2,1)} %get-tuple-element.57.dy_all, ...), custom_call_target="tpu_custom_call" | custom-call | tf_op jit(solution)/shard_map/expert_all/pallas_call | solution.py:1157
  313.9 0.8 slice_convert_fusion
  314.7 0.1 copy.106
  314.9 2.3 multiply_reduce_fusion
  317.3 0.2 fusion.24
  317.5 0.1 convert_reduce_fusion.1
  317.7 1.5 convert_reduce_fusion
  319.2 83.9 %attend_rear.1 = (bf16[128,2880]{1,0:T(8,128)(2,1)}, bf16[1024,2880]{1,0:T(8,128)(2,1)}, bf16[2,8,192,640]{3,2,1,0:T(8,128)(2,1)}, f32[1,2880]{1,0:T(1,128)}, f32[1,384]{1,0:T(1,128)}, /*index=5*/f32[1,4]{1,0:T(1,128)}) custom-call(f32[1,4]{1,0:T(1,128)} %dynamic-slice_bitcast_fusion.sink_ref, bf16[736,2048]{1,0:T(8,128)(2,1)} %get-tuple-element.58.act_ref.second_ref, ...), custom_call_target="tpu_custom_call" | custom-call | tf_op jit(solution)/shard_map/attend_rear/pallas_call | solution.py:1787
  403.2 0.7 slice_reduce_fusion
  403.9 0.7 slice.22
  404.6 0.1 reshape_squeeze.7
  404.6 0.1 dynamic_update_slice.10
  404.8 0.8 bitcast_dynamic-update-slice_fusion
  405.6 0.2 dynamic_update_slice.9
  405.8 0.7 reduce
  406.6 0.1 fusion.9
  406.7 0.7 select_maximum_fusion.v_ref
  407.4 52.5 %leave_rows.1 = (bf16[128,2880]{1,0:T(8,128)(2,1)}, bf16[8,192,640]{2,1,0:T(8,128)(2,1)}, f32[16,2880]{1,0:T(8,128)}) custom-call(bf16[1024,2880]{1,0:T(8,128)(2,1)} %get-tuple-element.70.p_ref, bf16[2,8,192,640]{3,2,1,0:T(8,128)(2,1)} %get-tuple-element.71.g_ref, f32[8,2880]{1,0:T(8,128)} %select_maximum_fusion.v_ref), custom_call_target="tpu_custom_call" | custom-call | tf_op jit(solution)/shard_map/leave_rows/pallas_call | solution.py:509
  459.8 4.0 all-to-all-start
  463.9 0.3 fusion.7
  464.2 0.3 copy-done.30
  464.5 0.5 copy-done.6
  465.0 0.2 copy-done.9
  465.2 3.9 fusion.2
  469.1 2.4 copy.110
  471.5 1.1 copy.111
  472.6 0.3 reduce.6
  472.9 0.7 reshape.238
  473.6 44.5 %weight_gradients.1 = (f32[1440,2880]{1,0:T(8,128)}, f32[720,2880]{1,0:T(8,128)}, f32[1,2880]{1,0:T(1,128)}) custom-call(bf16[1440,2048]{1,0:T(8,128)(2,1)} %get-tuple-element.89.first_ref, bf16[736,2048]{1,0:T(8,128)(2,1)} %get-tuple-element.58.act_ref.second_ref, bf16[2048,2944]{1,0:T(8,128)(2,1)} %bitcast.59, bf16[2048,2944]{1,0:T(8,128)(2,1)} %bitcast.49), custom_call_target="tpu_custom_call" | custom-call | flops 25669140480 | bytes 48660480 | tf_op jit(solution)/shard_map/weight_gradients/pallas_call | solution.py:1206
  518.0 1.3 copy-done.10
  519.3 3.5 settle_gradients.1
  522.8 1.4 reduce.2
  524.2 1.2 copy.108
  525.4 0.9 copy.112
  526.3 0.5 broadcast.202
  526.9 0.7 reduce.12
  527.5 0.6 reshape.230
  528.1 0.6 reduce.4
  528.8 0.6 reduce.5
  (90 shorter events, 0.5 us)
Async XLA Ops:
  0.7 174.8 %copy-start = (bf16[2880,8]{0,1:T(8,128)(2,1)S(1)}, bf16[2880,8]{0,1:T(8,128)(2,1)}, u32[]{:S(2)}) copy-start(bf16[2880,8]{0,1:T(8,128)(2,1)} %param.30) | copy-start | bytes 138244
  0.7 1.9 copy-start.18
  0.7 2.9 copy-start.15
  2.5 2.3 copy-start.29
  2.5 1.4 copy-start.27
  2.5 3.0 copy-start.32
  2.5 3.5 copy-start.16
  3.9 4.2 copy-start.4
  8.1 165.4 %copy-start.17 = (f32[2880]{0:T(1024)S(1)}, f32[2880]{0:T(1024)}, u32[]{:S(2)}) copy-start(f32[2880]{0:T(1024)} %param.28) | copy-start | bytes 34564
  173.4 1.6 copy-start.7
  173.4 1.6 copy-start.19
  175.0 0.7 copy-start.31
  175.1 0.9 copy-start.21
  175.1 1.4 copy-start.24
  175.7 3.0 copy-start.2
  314.9 2.4 copy-start.3
  314.9 2.7 copy-start.5
  314.9 2.7 copy-start.8
  317.3 1.9 copy-start.11
  317.6 1.6 copy-start.25
  459.8 4.1 copy-start.12
  459.8 58.2 %all-to-all-start = ((bf16[8,192,640]{2,1,0:T(8,128)(2,1)}), bf16[8,192,640]{2,1,0:T(8,128)(2,1)S(1)}, u32[]{:S(2)}, u32[]{:S(2)}) async-start(bf16[8,192,640]{2,1,0:T(8,128)(2,1)} %get-tuple-element.76), calls=%async_computation | async-start | bytes 3932160 | tf_op jit(solution)/shard_map/all_to_all | solution.py:2066
  463.8 0.7 copy-start.30
  463.9 1.1 copy-start.6
  463.9 1.3 copy-start.9
  463.9 1.3 copy-start.20
  463.9 1.3 copy-start.26
  469.1 2.4 copy-start.13
  469.1 3.5 copy-start.14
  518.0 1.3 copy-start.10
  519.3 10.1 %copy-start.1 = (bf16[2880,8]{0,1:T(8,128)(2,1)S(1)}, bf16[2880,8]{0,1:T(8,128)(2,1)}, u32[]{:S(2)}) copy-start(bf16[2880,8]{0,1:T(8,128)(2,1)} %param.30) | copy-start | bytes 138244
  522.8 4.1 copy-start.28
  522.8 5.3 %copy-start.23 = (f32[1,2880]{1,0:T(1,128)S(1)}, f32[1,2880]{1,0:T(1,128)}, u32[]{:S(2)}) copy-start(f32[1,2880]{1,0:T(1,128)} %get-tuple-element.85) | copy-start | bytes 34564
  522.8 6.0 %copy-start.22 = (f32[1,2880]{1,0:T(1,128)S(1)}, f32[1,2880]{1,0:T(1,128)}, u32[]{:S(2)}) copy-start(f32[1,2880]{1,0:T(1,128)} %get-tuple-element.86) | copy-start | bytes 34564

commit v3 on v2

--- a/solution.py
+++ b/solution.py
@@ -1119,9 +1119,7 @@
                     (dgu_buf.at[:, columns], dgu_all.at[:, columns]),
                 )
             ):
-                copy = pltpu.make_async_copy(src, dst, keep_s.at[at, slot])
-                copy.start()
-                kept.append(copy)
+                kept.append(pltpu.make_async_copy(src, dst, keep_s.at[at, slot]))
 
     gather.first()
     for copy in loads:
@@ -1132,6 +1130,8 @@
         fetch(gather.after(k))
     compute(gather.after(size // 2 - 1))
     total.begin()
+    for copy in kept:
+        copy.start()
     gather.finish()
     total.make(6)
     for k in range(1, size // 2):
@@ -1739,9 +1739,10 @@
     for k in range(size // 2):
         total.make(2 * (k + 1))
         gather.step(k)
+        if k == size // 2 - 2:
+            total.begin()
     gather.finish()
     total.settle(size - 1)
-    total.begin()
     loads[2].wait()
     lax.fori_loop(0, steps, grad_step, 0)
     grad_out = down(da[...], low_ref[...]).astype(bf16)

time: 533 us -> 532 us (level)
  no operation moved by 1% of the time
where the time goes in v3:
time: 532 us; the launch traced here: 528 us
  Pallas kernels  484 us (91%)
  local copies, waits for them, and re-layouts  21.2 us (4%)
  other arithmetic  15.3 us (3%)
    pallas_call x1, Pallas kernels, front(): pl.pallas_call(functools.partial(front_kernel, size, heads, kv_of), out_s...  165 us
    pallas_call x1, Pallas kernels, expert_all(): pl.pallas_call(functools.partial(expert_kernel_all, size, units, model, e...  135 us
    pallas_call x1, Pallas kernels, rear(): pl.pallas_call(functools.partial(rear_kernel, size, heads, own_rows, weig...  82.4 us
    pallas_call x1, Pallas kernels, leave(): pl.pallas_call(functools.partial(leave_kernel, size, halves), out_shape=(...  53 us
    pallas_call x1, Pallas kernels, weight_gradients(): pl.pallas_call(functools.partial(weights_kernel, model), grid=(-(-model /...  44.5 us
  transfers between devices with their start and end apart: 1, of which 0 were waited for; matrix products, arithmetic and copies ran while one was open for 2% of the time, Pallas kernels for 8%

profile of v3, /device:TPU:0, one launch (start us, length us, event | category | flops | bytes accessed | tf_op | source)
XLA Modules:
  0.0 528.5 jit_solution(5432050189577893315)
XLA Ops:
  0.7 0.0 copy-start
  0.7 1.5 copy.96
  2.3 0.2 fusion.3
  2.5 0.0 copy-start.27
  2.6 0.2 copy.97
  2.8 0.8 copy.100.kvw_ref
  3.6 0.3 copy.99
  4.0 0.8 dynamic_slice.20
  4.8 0.1 fusion.13
  4.8 0.1 pad_maximum_fusion
  4.9 0.6 broadcast_in_dim.27.bias_ref
  5.5 0.6 dynamic-slice_bitcast_fusion.sink_ref
  6.1 1.1 fusion.5.x_ref
  7.2 0.9 pad.20.dy_ref
  8.1 165.3 %attend_front.1 = (bf16[1024,256]{1,0:T(8,128)(2,1)}, bf16[1024,64]{1,0:T(8,128)(2,1)}, bf16[1024,64]{1,0:T(8,128)(2,1)}, f32[1024,256]{1,0:T(8,128)}, bf16[1024...) custom-call(f32[1,4]{1,0:T(1,128)} %dynamic-slice_bitcast_fusion.sin, ...), custom_call_target="tpu_custom_call" | custom-call | tf_op jit(solution)/shard_map/attend_front/pallas_call | solution.py:1635
  173.5 1.6 multiply_reduce_fusion.2
  175.1 0.0 copy-start.24
  175.1 0.3 multiply_convert_fusion
  175.4 0.3 copy-done.31
  175.7 0.3 convolution_add_fusion.1
  176.1 0.1 copy.101
  176.2 0.1 copy.103
  176.3 0.1 copy.102
  176.5 1.2 reshape_squeeze.8.bias_ref
  177.7 1.0 concatenate.16.x_ref
  178.7 135.0 %expert_all.1 = (bf16[8,256,2944]{2,1,0:T(8,128)(2,1)}, bf16[736,2048]{1,0:T(8,128)(2,1)}, bf16[1440,2048]{1,0:T(8,128)(2,1)}, bf16[16,2880]{1,0:T(8,128)(2,1)},...) custom-call(bf16[128,2944]{1,0:T(8,128)(2,1)} %concatenate.16.x_ref, bf16[8,256,2944]{2,1,0:T(8,128)(2,1)} %get-tuple-element.57.dy_all, ...), custom_call_target="tpu_custom_call" | custom-call | tf_op jit(solution)/shard_map/expert_all/pallas_call | solution.py:1157
  313.7 0.8 slice_convert_fusion
  314.6 0.1 copy.106
  314.8 2.3 multiply_reduce_fusion
  317.1 0.2 fusion.24
  317.4 0.1 convert_reduce_fusion.1
  317.5 1.5 convert_reduce_fusion
  319.1 82.4 %attend_rear.1 = (bf16[128,2880]{1,0:T(8,128)(2,1)}, bf16[1024,2880]{1,0:T(8,128)(2,1)}, bf16[2,8,192,640]{3,2,1,0:T(8,128)(2,1)}, f32[1,2880]{1,0:T(1,128)}, f32[1,384]{1,0:T(1,128)}, /*index=5*/f32[1,4]{1,0:T(1,128)}) custom-call(f32[1,4]{1,0:T(1,128)} %dynamic-slice_bitcast_fusion.sink_ref, bf16[736,2048]{1,0:T(8,128)(2,1)} %get-tuple-element.58.act_ref.second_ref, ...), custom_call_target="tpu_custom_call" | custom-call | tf_op jit(solution)/shard_map/attend_rear/pallas_call | solution.py:1788
  401.5 0.7 slice_reduce_fusion
  402.2 0.7 slice.22
  402.9 0.1 reshape_squeeze.7
  403.0 0.1 dynamic_update_slice.10
  403.1 0.8 bitcast_dynamic-update-slice_fusion
  403.9 0.2 dynamic_update_slice.9
  404.2 0.7 reduce
  405.0 0.1 fusion.9
  405.0 0.7 select_maximum_fusion.v_ref
  405.7 53.0 %leave_rows.1 = (bf16[128,2880]{1,0:T(8,128)(2,1)}, bf16[8,192,640]{2,1,0:T(8,128)(2,1)}, f32[16,2880]{1,0:T(8,128)}) custom-call(bf16[1024,2880]{1,0:T(8,128)(2,1)} %get-tuple-element.70.p_ref, bf16[2,8,192,640]{3,2,1,0:T(8,128)(2,1)} %get-tuple-element.71.g_ref, f32[8,2880]{1,0:T(8,128)} %select_maximum_fusion.v_ref), custom_call_target="tpu_custom_call" | custom-call | tf_op jit(solution)/shard_map/leave_rows/pallas_call | solution.py:509
  458.7 4.0 all-to-all-start
  462.8 0.3 fusion.7
  463.1 0.3 copy-done.30
  463.4 0.5 copy-done.6
  463.8 0.2 copy-done.9
  464.1 3.9 fusion.2
  467.9 2.4 copy.110
  470.3 1.1 copy.111
  471.5 0.3 reduce.6
  471.7 0.7 reshape.238
  472.4 44.5 %weight_gradients.1 = (f32[1440,2880]{1,0:T(8,128)}, f32[720,2880]{1,0:T(8,128)}, f32[1,2880]{1,0:T(1,128)}) custom-call(bf16[1440,2048]{1,0:T(8,128)(2,1)} %get-tuple-element.89.first_ref, bf16[736,2048]{1,0:T(8,128)(2,1)} %get-tuple-element.58.act_ref.second_ref, bf16[2048,2944]{1,0:T(8,128)(2,1)} %bitcast.59, bf16[2048,2944]{1,0:T(8,128)(2,1)} %bitcast.49), custom_call_target="tpu_custom_call" | custom-call | flops 25669140480 | bytes 48660480 | tf_op jit(solution)/shard_map/weight_gradients/pallas_call | solution.py:1206
  516.9 1.3 copy-done.10
  518.2 3.5 settle_gradients.1
  521.6 1.4 reduce.2
  523.0 1.2 copy.108
  524.2 0.9 copy.112
  525.2 0.5 broadcast.202
  525.7 0.7 reduce.12
  526.4 0.6 reshape.230
  527.0 0.6 reduce.4
  527.6 0.6 reduce.5
  (90 shorter events, 0.5 us)
Async XLA Ops:
  0.7 174.8 %copy-start = (bf16[2880,8]{0,1:T(8,128)(2,1)S(1)}, bf16[2880,8]{0,1:T(8,128)(2,1)}, u32[]{:S(2)}) copy-start(bf16[2880,8]{0,1:T(8,128)(2,1)} %param.30) | copy-start | bytes 138244
  0.7 1.9 copy-start.18
  0.7 2.9 copy-start.15
  2.5 2.3 copy-start.29
  2.5 1.4 copy-start.27
  2.5 3.0 copy-start.32
  2.5 3.5 copy-start.16
  3.9 4.2 copy-start.4
  8.1 165.4 %copy-start.17 = (f32[2880]{0:T(1024)S(1)}, f32[2880]{0:T(1024)}, u32[]{:S(2)}) copy-start(f32[2880]{0:T(1024)} %param.28) | copy-start | bytes 34564
  173.4 1.6 copy-start.7
  173.4 1.6 copy-start.19
  175.0 0.7 copy-start.31
  175.1 0.9 copy-start.21
  175.1 1.4 copy-start.24
  175.7 3.0 copy-start.2
  314.7 2.4 copy-start.3
  314.8 2.7 copy-start.5
  314.8 2.7 copy-start.8
  317.1 1.9 copy-start.11
  317.5 1.6 copy-start.25
  458.7 4.1 copy-start.12
  458.7 58.2 %all-to-all-start = ((bf16[8,192,640]{2,1,0:T(8,128)(2,1)}), bf16[8,192,640]{2,1,0:T(8,128)(2,1)S(1)}, u32[]{:S(2)}, u32[]{:S(2)}) async-start(bf16[8,192,640]{2,1,0:T(8,128)(2,1)} %get-tuple-element.76), calls=%async_computation | async-start | bytes 3932160 | tf_op jit(solution)/shard_map/all_to_all | solution.py:2067
  462.7 0.7 copy-start.30
  462.7 1.1 copy-start.6
  462.7 1.3 copy-start.9
  462.7 1.3 copy-start.20
  462.7 1.3 copy-start.26
  467.9 2.4 copy-start.13
  467.9 3.5 copy-start.14
  516.9 1.3 copy-start.10
  518.2 10.1 %copy-start.1 = (bf16[2880,8]{0,1:T(8,128)(2,1)S(1)}, bf16[2880,8]{0,1:T(8,128)(2,1)}, u32[]{:S(2)}) copy-start(bf16[2880,8]{0,1:T(8,128)(2,1)} %param.30) | copy-start | bytes 138244
  521.6 4.1 copy-start.28
  521.6 5.3 %copy-start.23 = (f32[1,2880]{1,0:T(1,128)S(1)}, f32[1,2880]{1,0:T(1,128)}, u32[]{:S(2)}) copy-start(f32[1,2880]{1,0:T(1,128)} %get-tuple-element.85) | copy-start | bytes 34564
  521.6 6.0 %copy-start.22 = (f32[1,2880]{1,0:T(1,128)S(1)}, f32[1,2880]{1,0:T(1,128)}, u32[]{:S(2)}) copy-start(f32[1,2880]{1,0:T(1,128)} %get-tuple-element.86) | copy-start | bytes 34564
